TPU v7x, 32 devices: a whole 2x2x4 slice. The times are simulated.
32 devices in a mesh: fsdp: 16 (over z, y, core), dp: 2 (over x).
Axes of the slice: x: 2, y: 2, z: 4, core: 2. Of those that a mesh axis runs over, the one named last changes fastest.
Arguments:
- tokens: bfloat16 [12288, 768], P(('fsdp', 'dp')), may hold values from -6 to 6
- memory: bfloat16 [24576, 768], P(('fsdp', 'dp')), may hold values from -6 to 6
- out_grad: bfloat16 [12288, 768], P(('fsdp', 'dp')), may hold values from -6 to 6
- target_len: int32 [32, 6], P(('fsdp', 'dp')), may hold values from 1 to 128, 384 in all within a row
- source_len: int32 [32, 6], P(('fsdp', 'dp')), may hold values from 1 to 512, 768 in all within a row
- task_ids: int32 [32, 6], P(('fsdp', 'dp')), may hold values from 0 to 7
- norm_gains: bfloat16 [3, 768], P(None, 'fsdp'), may hold values from 0.25 to 1.75
- self_qkv: bfloat16 [768, 2304], P('fsdp'), may hold values from -0.21875 to 0.21875
- self_out: bfloat16 [768, 768], P('fsdp'), may hold values from -0.625 to 0.625
- cross_query: bfloat16 [768, 768], P('fsdp'), may hold values from -0.21875 to 0.21875
- cross_keyval: bfloat16 [768, 1536], P('fsdp'), may hold values from -0.21875 to 0.21875
- cross_out: bfloat16 [768, 768], P('fsdp'), may hold values from -0.875 to 0.875
- feed_in: bfloat16 [768, 3072], P('fsdp'), may hold values from -0.21875 to 0.21875
- feed_out: bfloat16 [3072, 768], P('fsdp'), may hold values from -0.109375 to 0.109375
- task_table: bfloat16 [8, 64], P(None, 'fsdp'), may hold values from -5 to 5
- hyper_in: bfloat16 [64, 128], P(None, 'fsdp'), may hold values from -0.75 to 0.75
- maker_down: bfloat16 [128, 55296], P(None, 'fsdp'), may hold values from -0.03125 to 0.03125
- maker_up: bfloat16 [128, 55296], P(None, 'fsdp'), may hold values from -0.15625 to 0.15625
- maker_norm: bfloat16 [128, 2304], P(None, 'fsdp'), may hold values from -0.1875 to 0.1875
Outputs:
- block_out: bfloat16 [12288, 768], P(('fsdp', 'dp'))
- grad_tokens: float32 [12288, 768], P(('fsdp', 'dp'))
- grad_memory: float32 [24576, 768], P(('fsdp', 'dp'))
- grad_norm_gains: float32 [3, 768], P(None, 'fsdp')
- grad_self_qkv: float32 [768, 2304], P('fsdp')
- grad_self_out: float32 [768, 768], P('fsdp')
- grad_cross_query: float32 [768, 768], P('fsdp')
- grad_cross_keyval: float32 [768, 1536], P('fsdp')
- grad_cross_out: float32 [768, 768], P('fsdp')
- grad_feed_in: float32 [768, 3072], P('fsdp')
- grad_feed_out: float32 [3072, 768], P('fsdp')
- grad_task_table: float32 [8, 64], P(None, 'fsdp')
- grad_hyper_in: float32 [64, 128], P(None, 'fsdp')
- grad_maker_down: float32 [128, 55296], P(None, 'fsdp')
- grad_maker_up: float32 [128, 55296], P(None, 'fsdp')
- grad_maker_norm: float32 [128, 2304], P(None, 'fsdp')
Inputs may be any that keep to these rules, and one draw needn't show every extreme that they name: `target_len`: row g lists the target lengths of the 6 sequences of group g; they sum to 384, and some entry of every row is 128. `source_len`: row g lists the memory lengths of the 6 sequences of group g; they sum to 768, and some entry of every row is 512.
All inputs are finite; a program needn't handle non-finite values.
Results may differ from a plain program's by a relative error of at most 0.035.
Values may be sent and summed in bfloat16 or wider, within the bound.
No kernel may reach another device: no remote copies, remote signals or barrier semaphores. Data moves between devices by JAX's collectives and lax.ppermute only.
A program may use at most 320 MiB of HBM per device.

v0:
```python
import jax
import jax.numpy as jnp
from jax import lax
from jax.sharding import PartitionSpec as P

HEADS = 12


norm_epsilon = 1e-06
masked_score = -1000000000.0
highest = lax.Precision.HIGHEST


def rms_scale(values, gain):
    return (
        values * lax.rsqrt(jnp.mean(values * values, axis=-1, keepdims=True) + norm_epsilon) * gain
    )


def matmul(left, right):
    return jnp.dot(left, right, preferred_element_type=jnp.float32)


def inner_rows(left, right):
    return lax.dot_general(
        left, right, (((0,), (0,)), ((), ())), preferred_element_type=jnp.float32
    )


def inner_cols(left, right):
    return lax.dot_general(
        left, right, (((1,), (1,)), ((), ())), preferred_element_type=jnp.float32
    )


def exact_dot(left, right):
    return jnp.dot(left, right, precision=highest, preferred_element_type=jnp.float32)


def exact_rows(left, right):
    return lax.dot_general(
        left, right, (((0,), (0,)), ((), ())), precision=highest, preferred_element_type=jnp.float32
    )


def exact_cols(left, right):
    return lax.dot_general(
        left, right, (((1,), (1,)), ((), ())), precision=highest, preferred_element_type=jnp.float32
    )


def segment_rows(lengths, count):
    ends = jnp.cumsum(lengths)
    places = jnp.arange(count, dtype=jnp.int32)
    return jnp.sum((places[:, None] >= ends[None, :]).astype(jnp.int32), axis=1)


def split_heads(values):
    return values.reshape(values.shape[0], HEADS, values.shape[1] // HEADS)


def head_scores(query_heads, key_heads, allowed):
    depth = query_heads.shape[2]
    scores = jnp.einsum(
        "qhd,khd->hqk", query_heads, key_heads, preferred_element_type=jnp.float32
    ) * depth ** (-0.5)
    return jnp.where(allowed[None], scores, masked_score)


def attend_forward(queries, keys, values, allowed):
    scores = head_scores(split_heads(queries), split_heads(keys), allowed)
    top = jnp.max(scores, axis=-1, keepdims=True)
    weights = jnp.exp(scores - top)
    total = jnp.sum(weights, axis=-1, keepdims=True)
    probs = (weights / total).astype(jnp.bfloat16)
    mixed = jnp.einsum(
        "hqk,khd->qhd", probs, split_heads(values), preferred_element_type=jnp.float32
    )
    return (mixed.reshape(queries.shape).astype(jnp.bfloat16), top + jnp.log(total))


def attend_backward(queries, keys, values, allowed, logsum, grad_mixed):
    query_heads = split_heads(queries)
    key_heads = split_heads(keys)
    depth = query_heads.shape[2]
    probs = jnp.exp(head_scores(query_heads, key_heads, allowed) - logsum)
    grad_heads = split_heads(grad_mixed)
    grad_values = jnp.einsum(
        "hqk,qhd->khd", probs.astype(jnp.bfloat16), grad_heads, preferred_element_type=jnp.float32
    )
    grad_probs = jnp.einsum(
        "qhd,khd->hqk", grad_heads, split_heads(values), preferred_element_type=jnp.float32
    )
    grad_scores = probs * (grad_probs - jnp.sum(grad_probs * probs, axis=-1, keepdims=True))
    grad_scores = grad_scores.astype(jnp.bfloat16)
    grad_queries = jnp.einsum(
        "hqk,khd->qhd", grad_scores, key_heads, preferred_element_type=jnp.float32
    ) * depth ** (-0.5)
    grad_keys = jnp.einsum(
        "hqk,qhd->khd", grad_scores, query_heads, preferred_element_type=jnp.float32
    ) * depth ** (-0.5)
    return (
        grad_queries.reshape(queries.shape),
        grad_keys.reshape(keys.shape),
        grad_values.reshape(values.shape),
    )


def adapter_parts(made_down, made_up, made_norm, index, width):
    tasks = made_down.shape[0]
    span = made_down.shape[1] // 3
    bottleneck = span // width
    down = made_down[:, index * span : (index + 1) * span].reshape(tasks, width, bottleneck)
    down = jnp.transpose(down, (1, 0, 2)).reshape(width, tasks * bottleneck)
    up = made_up[:, index * span : (index + 1) * span].reshape(tasks * bottleneck, width)
    return (down, up, made_norm[:, index * width : (index + 1) * width])


def adapter_forward(branch, parts, onehot, widemask):
    down, up, gains = parts
    row_gain = exact_dot(onehot, gains)
    normed = rms_scale(branch, row_gain).astype(jnp.bfloat16)
    squeezed = matmul(normed, down) * widemask
    lifted = jax.nn.gelu(squeezed).astype(jnp.bfloat16)
    return (branch + matmul(lifted, up), (normed, squeezed, lifted, row_gain))


def adapter_backward(branch, parts, onehot, widemask, kept, grad_out):
    down, up = (parts[0], parts[1])
    normed, squeezed, lifted, row_gain = kept
    tasks = onehot.shape[1]
    width = down.shape[0]
    grad_lift = grad_out.astype(jnp.bfloat16)
    grad_up = inner_rows(lifted, grad_lift)
    _, gelu_pull = jax.vjp(jax.nn.gelu, squeezed)
    grad_squeezed = gelu_pull(inner_cols(grad_lift, up))[0].astype(jnp.bfloat16) * widemask.astype(
        jnp.bfloat16
    )
    grad_down = inner_rows(normed, grad_squeezed)
    _, norm_pull = jax.vjp(rms_scale, branch, row_gain)
    grad_branch, grad_row_gain = norm_pull(inner_cols(grad_squeezed, down))
    down_rows = jnp.transpose(grad_down.reshape(width, tasks, -1), (1, 0, 2)).reshape(tasks, -1)
    return (
        grad_out + grad_branch,
        (down_rows, grad_up.reshape(tasks, -1), exact_dot(onehot.T, grad_row_gain)),
    )


def per_device(
    tokens,
    memory,
    out_grad,
    target_len,
    source_len,
    task_ids,
    norm_gains,
    self_qkv,
    self_out,
    cross_query,
    cross_keyval,
    cross_out,
    feed_in,
    feed_out,
    task_table,
    hyper_in,
    maker_down,
    maker_up,
    maker_norm,
):
    (
        whole_gains,
        whole_qkv,
        whole_self_out,
        whole_query,
        whole_keyval,
        whole_cross_out,
        whole_feed_in,
        whole_feed_out,
        whole_table,
        whole_hyper,
        whole_down_maker,
        whole_up_maker,
        whole_norm_maker,
    ) = (
        lax.all_gather(norm_gains, "fsdp", axis=1, tiled=True),
        lax.all_gather(self_qkv, "fsdp", axis=0, tiled=True),
        lax.all_gather(self_out, "fsdp", axis=0, tiled=True),
        lax.all_gather(cross_query, "fsdp", axis=0, tiled=True),
        lax.all_gather(cross_keyval, "fsdp", axis=0, tiled=True),
        lax.all_gather(cross_out, "fsdp", axis=0, tiled=True),
        lax.all_gather(feed_in, "fsdp", axis=0, tiled=True),
        lax.all_gather(feed_out, "fsdp", axis=0, tiled=True),
        lax.all_gather(task_table, "fsdp", axis=1, tiled=True),
        lax.all_gather(hyper_in, "fsdp", axis=1, tiled=True),
        lax.all_gather(maker_down, "fsdp", axis=1, tiled=True),
        lax.all_gather(maker_up, "fsdp", axis=1, tiled=True),
        lax.all_gather(maker_norm, "fsdp", axis=1, tiled=True),
    )
    width = tokens.shape[1]
    tasks = task_table.shape[0]
    pre_hidden = matmul(whole_table, whole_hyper)
    hidden = jax.nn.silu(pre_hidden).astype(jnp.bfloat16)
    made_down = matmul(hidden, whole_down_maker).astype(jnp.bfloat16)
    made_up = matmul(hidden, whole_up_maker).astype(jnp.bfloat16)
    made_cond = matmul(hidden, whole_norm_maker).astype(jnp.bfloat16)
    made_norm = 1.0 + made_cond.astype(jnp.float32)
    tok_seg = segment_rows(target_len[0], tokens.shape[0])
    mem_seg = segment_rows(source_len[0], memory.shape[0])
    sequences = jnp.arange(target_len.shape[1], dtype=jnp.int32)
    row_task = jnp.sum(
        jnp.where(tok_seg[:, None] == sequences[None, :], task_ids[0][None, :], 0), axis=1
    )
    onehot = (row_task[:, None] == jnp.arange(tasks, dtype=jnp.int32)[None, :]).astype(jnp.float32)
    widemask = jnp.repeat(onehot, made_down.shape[1] // (3 * width), axis=1)
    places = jnp.arange(tokens.shape[0], dtype=jnp.int32)
    self_allowed = (tok_seg[:, None] == tok_seg[None, :]) & (places[:, None] >= places[None, :])
    cross_allowed = tok_seg[:, None] == mem_seg[None, :]
    parts_one = adapter_parts(made_down, made_up, made_norm, 0, width)
    parts_two = adapter_parts(made_down, made_up, made_norm, 1, width)
    parts_three = adapter_parts(made_down, made_up, made_norm, 2, width)
    gains = whole_gains.astype(jnp.float32)
    inputs = tokens.astype(jnp.float32)
    normed1 = rms_scale(inputs, gains[0]).astype(jnp.bfloat16)
    projected = matmul(normed1, whole_qkv).astype(jnp.bfloat16)
    queries1 = projected[:, :width]
    keys1 = projected[:, width : 2 * width]
    values1 = projected[:, 2 * width :]
    mixed1, logsum1 = attend_forward(queries1, keys1, values1, self_allowed)
    branch1 = matmul(mixed1, whole_self_out)
    adapted1, kept1 = adapter_forward(branch1, parts_one, onehot, widemask)
    stream1 = inputs + adapted1
    normed2 = rms_scale(stream1, gains[1]).astype(jnp.bfloat16)
    queries2 = matmul(normed2, whole_query).astype(jnp.bfloat16)
    memory_kv = matmul(memory, whole_keyval).astype(jnp.bfloat16)
    keys2 = memory_kv[:, :width]
    values2 = memory_kv[:, width:]
    mixed2, logsum2 = attend_forward(queries2, keys2, values2, cross_allowed)
    branch2 = matmul(mixed2, whole_cross_out)
    adapted2, kept2 = adapter_forward(branch2, parts_two, onehot, widemask)
    stream2 = stream1 + adapted2
    normed3 = rms_scale(stream2, gains[2]).astype(jnp.bfloat16)
    pre_feed = matmul(normed3, whole_feed_in)
    active = jax.nn.gelu(pre_feed).astype(jnp.bfloat16)
    branch3 = matmul(active, whole_feed_out)
    adapted3, kept3 = adapter_forward(branch3, parts_three, onehot, widemask)
    result = stream2 + adapted3
    grad_stream = out_grad.astype(jnp.float32)
    grad_branch, made_three = adapter_backward(
        branch3, parts_three, onehot, widemask, kept3, grad_stream
    )
    grad_branch = grad_branch.astype(jnp.bfloat16)
    grad_feed_out = inner_rows(active, grad_branch)
    _, gelu_pull = jax.vjp(jax.nn.gelu, pre_feed)
    grad_pre = gelu_pull(inner_cols(grad_branch, whole_feed_out))[0].astype(jnp.bfloat16)
    grad_feed_in = inner_rows(normed3, grad_pre)
    _, norm_pull = jax.vjp(rms_scale, stream2, gains[2])
    grad_from_norm, grad_gain_three = norm_pull(inner_cols(grad_pre, whole_feed_in))
    grad_stream = grad_stream + grad_from_norm
    grad_branch, made_two = adapter_backward(
        branch2, parts_two, onehot, widemask, kept2, grad_stream
    )
    grad_branch = grad_branch.astype(jnp.bfloat16)
    grad_cross_out = inner_rows(mixed2, grad_branch)
    grad_mixed = inner_cols(grad_branch, whole_cross_out).astype(jnp.bfloat16)
    grad_q2, grad_k2, grad_v2 = attend_backward(
        queries2, keys2, values2, cross_allowed, logsum2, grad_mixed
    )
    grad_q2 = grad_q2.astype(jnp.bfloat16)
    grad_kv = jnp.concatenate([grad_k2, grad_v2], axis=1).astype(jnp.bfloat16)
    grad_query = inner_rows(normed2, grad_q2)
    grad_keyval = inner_rows(memory, grad_kv)
    grad_memory = inner_cols(grad_kv, whole_keyval)
    _, norm_pull = jax.vjp(rms_scale, stream1, gains[1])
    grad_from_norm, grad_gain_two = norm_pull(inner_cols(grad_q2, whole_query))
    grad_stream = grad_stream + grad_from_norm
    grad_branch, made_one = adapter_backward(
        branch1, parts_one, onehot, widemask, kept1, grad_stream
    )
    grad_branch = grad_branch.astype(jnp.bfloat16)
    grad_self_out = inner_rows(mixed1, grad_branch)
    grad_mixed = inner_cols(grad_branch, whole_self_out).astype(jnp.bfloat16)
    grad_q1, grad_k1, grad_v1 = attend_backward(
        queries1, keys1, values1, self_allowed, logsum1, grad_mixed
    )
    grad_projected = jnp.concatenate([grad_q1, grad_k1, grad_v1], axis=1).astype(jnp.bfloat16)
    grad_qkv = inner_rows(normed1, grad_projected)
    _, norm_pull = jax.vjp(rms_scale, inputs, gains[0])
    grad_from_norm, grad_gain_one = norm_pull(inner_cols(grad_projected, whole_qkv))
    grad_tokens = grad_stream + grad_from_norm
    grad_gains = jnp.stack([grad_gain_one, grad_gain_two, grad_gain_three])
    grad_made_down = jnp.concatenate([made_one[0], made_two[0], made_three[0]], axis=1)
    grad_made_up = jnp.concatenate([made_one[1], made_two[1], made_three[1]], axis=1)
    grad_made_norm = jnp.concatenate([made_one[2], made_two[2], made_three[2]], axis=1)
    hidden_wide = hidden.astype(jnp.float32)
    _, silu_pull = jax.vjp(jax.nn.silu, pre_hidden)
    place = lax.axis_index("fsdp")
    table_width = task_table.shape[1]
    hyper_width = hyper_in.shape[1]
    grad_hidden = (
        exact_cols(grad_made_down, whole_down_maker.astype(jnp.float32))
        + exact_cols(grad_made_up, whole_up_maker.astype(jnp.float32))
        + exact_cols(grad_made_norm, whole_norm_maker.astype(jnp.float32))
    )
    grad_pre_hidden = silu_pull(grad_hidden)[0]
    grad_table = exact_cols(grad_pre_hidden, whole_hyper.astype(jnp.float32))
    grad_hyper = exact_rows(whole_table.astype(jnp.float32), grad_pre_hidden)
    (
        share_gains,
        share_qkv,
        share_self_out,
        share_query,
        share_keyval,
        share_cross_out,
        share_feed_in,
        share_feed_out,
        share_down,
        share_up,
        share_norm,
    ) = (
        lax.psum_scatter(grad_gains, ("fsdp", "dp"), scatter_dimension=1, tiled=True),
        lax.psum_scatter(grad_qkv, ("fsdp", "dp"), scatter_dimension=0, tiled=True),
        lax.psum_scatter(grad_self_out, ("fsdp", "dp"), scatter_dimension=0, tiled=True),
        lax.psum_scatter(grad_query, ("fsdp", "dp"), scatter_dimension=0, tiled=True),
        lax.psum_scatter(grad_keyval, ("fsdp", "dp"), scatter_dimension=0, tiled=True),
        lax.psum_scatter(grad_cross_out, ("fsdp", "dp"), scatter_dimension=0, tiled=True),
        lax.psum_scatter(grad_feed_in, ("fsdp", "dp"), scatter_dimension=0, tiled=True),
        lax.psum_scatter(grad_feed_out, ("fsdp", "dp"), scatter_dimension=0, tiled=True),
        lax.psum_scatter(
            exact_rows(hidden_wide, grad_made_down), ("fsdp", "dp"), scatter_dimension=1, tiled=True
        ),
        lax.psum_scatter(
            exact_rows(hidden_wide, grad_made_up), ("fsdp", "dp"), scatter_dimension=1, tiled=True
        ),
        lax.psum_scatter(
            exact_rows(hidden_wide, grad_made_norm), ("fsdp", "dp"), scatter_dimension=1, tiled=True
        ),
    )
    total_table, total_hyper = lax.psum((grad_table, grad_hyper), ("fsdp", "dp"))
    (
        out_gains,
        out_qkv,
        out_self_out,
        out_query,
        out_keyval,
        out_cross_out,
        out_feed_in,
        out_feed_out,
        out_down,
        out_up,
        out_norm,
    ) = (
        lax.all_gather(share_gains.astype(jnp.bfloat16), "dp", axis=1, tiled=True).astype(
            share_gains.dtype
        ),
        lax.all_gather(share_qkv.astype(jnp.bfloat16), "dp", axis=0, tiled=True).astype(
            share_qkv.dtype
        ),
        lax.all_gather(share_self_out.astype(jnp.bfloat16), "dp", axis=0, tiled=True).astype(
            share_self_out.dtype
        ),
        lax.all_gather(share_query.astype(jnp.bfloat16), "dp", axis=0, tiled=True).astype(
            share_query.dtype
        ),
        lax.all_gather(share_keyval.astype(jnp.bfloat16), "dp", axis=0, tiled=True).astype(
            share_keyval.dtype
        ),
        lax.all_gather(share_cross_out.astype(jnp.bfloat16), "dp", axis=0, tiled=True).astype(
            share_cross_out.dtype
        ),
        lax.all_gather(share_feed_in.astype(jnp.bfloat16), "dp", axis=0, tiled=True).astype(
            share_feed_in.dtype
        ),
        lax.all_gather(share_feed_out.astype(jnp.bfloat16), "dp", axis=0, tiled=True).astype(
            share_feed_out.dtype
        ),
        lax.all_gather(share_down.astype(jnp.bfloat16), "dp", axis=1, tiled=True).astype(
            share_down.dtype
        ),
        lax.all_gather(share_up.astype(jnp.bfloat16), "dp", axis=1, tiled=True).astype(
            share_up.dtype
        ),
        lax.all_gather(share_norm.astype(jnp.bfloat16), "dp", axis=1, tiled=True).astype(
            share_norm.dtype
        ),
    )
    out_table = lax.dynamic_slice_in_dim(total_table, place * table_width, table_width, 1)
    out_hyper = lax.dynamic_slice_in_dim(total_hyper, place * hyper_width, hyper_width, 1)
    return (
        result.astype(jnp.bfloat16),
        grad_tokens,
        grad_memory,
        out_gains,
        out_qkv,
        out_self_out,
        out_query,
        out_keyval,
        out_cross_out,
        out_feed_in,
        out_feed_out,
        out_table,
        out_hyper,
        out_down,
        out_up,
        out_norm,
    )


def solution(mesh):
    placed = (
        P(("fsdp", "dp"), None),
        P(("fsdp", "dp"), None),
        P(("fsdp", "dp"), None),
        P(("fsdp", "dp"), None),
        P(("fsdp", "dp"), None),
        P(("fsdp", "dp"), None),
        P(None, "fsdp"),
        P("fsdp", None),
        P("fsdp", None),
        P("fsdp", None),
        P("fsdp", None),
        P("fsdp", None),
        P("fsdp", None),
        P("fsdp", None),
        P(None, "fsdp"),
        P(None, "fsdp"),
        P(None, "fsdp"),
        P(None, "fsdp"),
        P(None, "fsdp"),
    )
    return jax.shard_map(
        per_device,
        mesh=mesh,
        in_specs=placed,
        out_specs=(
            P(("fsdp", "dp"), None),
            P(("fsdp", "dp"), None),
            P(("fsdp", "dp"), None),
            P(None, "fsdp"),
            P("fsdp", None),
            P("fsdp", None),
            P("fsdp", None),
            P("fsdp", None),
            P("fsdp", None),
            P("fsdp", None),
            P("fsdp", None),
            P(None, "fsdp"),
            P(None, "fsdp"),
            P(None, "fsdp"),
            P(None, "fsdp"),
            P(None, "fsdp"),
        ),
        check_vma=False,
    )
```

profile of v0, /device:TPU:0, one launch (start us, length us, event | category | flops | bytes accessed | tf_op | source)
XLA Modules:
  0.0 2107.0 jit_solution(289454955341132360)
XLA Ops:
  15.6 23.1 %all-gather = bf16[16,48,3]{1,2,0:T(4,128)(2,1)S(1)} all-gather(bf16[1,48,3]{1,2,0:T(4,128)(2,1)S(1)} %bitcast.245), channel_id=1, replica_groups=mesh['fsdp'=16,'dp'=2] {'fsdp'}, dimensions={0}, use_global_device_ids=true | all-gather | bytes 4896 | tf_op jit(solution)/shard_map/all_gather | solution.py:185
  39.4 17.4 all-gather.1
  56.9 18.8 all_gather.76
  76.7 20.5 all_gather.77
  119.7 26.8 %all-gather.15.cloned.1.call-done = bf16[768,768]{1,0:T(8,128)(2,1)} async-done(((bf16[48,768]{1,0:T(8,128)(2,1)}), bf16[768,768]{1,0:T(8,128)(2,1)}) %all-gather.15.cloned.1.call-update) | async-done | bytes 1179664 | tf_op jit(solution)/shard_map/all_gather | solution.py:187
  151.0 107.1 %all-gather.19.cloned.1.call-done = bf16[128,55296]{1,0:T(8,128)(2,1)} async-done(((bf16[128,3456]{1,0:T(8,128)(2,1)}), bf16[128,55296]{1,0:T(8,128)(2,1)}) %all-gather.19.cloned.1.call-update) | async-done | bytes 14155792 | tf_op jit(solution)/shard_map/all_gather | solution.py:196
  269.3 99.5 %all-gather.17.cloned.1.call-done = bf16[128,55296]{1,0:T(8,128)(2,1)} async-done(((bf16[128,3456]{1,0:T(8,128)(2,1)}), bf16[128,55296]{1,0:T(8,128)(2,1)}) %all-gather.17.cloned.1.call-update) | async-done | bytes 14155792 | tf_op jit(solution)/shard_map/all_gather | solution.py:195
  368.8 7.0 convolution_convert_fusion.1
  398.2 9.3 all-gather.23.cloned.1.call-done
  427.4 19.7 all-gather.25.cloned.1.call-done
  455.8 45.9 %all-gather.27.cloned.1.call-done = bf16[768,3072]{1,0:T(8,128)(2,1)} async-done(((bf16[48,3072]{1,0:T(8,128)(2,1)}), bf16[768,3072]{1,0:T(8,128)(2,1)}) %all-gather.27.cloned.1.call-update) | async-done | bytes 4718608 | tf_op jit(solution)/shard_map/all_gather | solution.py:191
  508.6 47.3 %all-gather.29.cloned.1.call-done = bf16[3072,768]{1,0:T(8,128)(2,1)} async-done(((bf16[192,768]{1,0:T(8,128)(2,1)}), bf16[3072,768]{1,0:T(8,128)(2,1)}) %all-gather.29.cloned.1.call-update) | async-done | bytes 4718608 | tf_op jit(solution)/shard_map/all_gather | solution.py:192
  585.7 14.4 multiply_reduce_fusion
  600.2 7.1 multiply_convert_fusion
  639.6 7.6 fusion.21
  661.9 7.4 multiply_reduce_fusion.1
  684.2 8.9 fusion.139
  715.4 25.7 %fusion.152 = f32[128,55296]{0,1:T(8,128)} fusion(bf16[8,128]{1,0:T(8,128)(2,1)S(1)} %copy-done.121, f32[8,55296]{1,0:T(8,128)S(1)} %constant_dynamic-update-slice_fusion.3), kind=kOutput, calls=%fused_computation.257 | convolution fusion | flops 679477248 | bytes 30083072 | tf_op jit(solution)/shard_map/dot_general | solution.py:41
  772.4 25.8 %fusion.151 = f32[128,55296]{0,1:T(8,128)} fusion(bf16[8,128]{1,0:T(8,128)(2,1)S(1)} %copy-done.121, f32[8,55296]{1,0:T(8,128)S(1)} %constant_dynamic-update-slice_fusion), kind=kOutput, calls=%fused_computation.256 | convolution fusion | flops 679477248 | bytes 30083072 | tf_op jit(solution)/shard_map/dot_general | solution.py:41
  805.9 14.0 fusion.149
  820.1 11.3 convolution_add_fusion.4
  833.3 40.5 %all-reduce.2 = (bf16[3,768]{1,0:T(4,128)(2,1)}, f32[8,64]{0,1:T(8,128)}, f32[64,128]{1,0:T(8,128)}) all-reduce(f32[3,768]{1,0:T(4,128)} %pad_maximum_fusion.9, f32[8,64]{0,1:T(8,128)} %fusion.150, f32[64,128]{1,0:T(8,128)} %convolution_bitcast_fusion.2), channel_id=2, replica_groups=mesh['fsdp'=16,'dp'=2] {'fsdp','dp'}, use_global_device_ids=true, to_apply=%region_26.27.clone | all-reduce | flops 11008 | bytes 83456
  904.8 17.7 reduce-scatter.20.cloned.1.call-done
  928.7 97.2 %reduce-scatter.18.cloned.1.call-done = f32[24,768]{1,0:T(8,128)} async-done(((f32[768,768]{1,0:T(8,128)}), f32[24,768]{1,0:T(8,128)}) %reduce-scatter.18.cloned.1.call-update) | async-done | bytes 73744 | tf_op jit(solution)/shard_map/reduce_scatter | solution.py:322
  1032.0 106.0 %reduce-scatter.32.cloned.1.call-done = f32[24,1536]{1,0:T(8,128)} async-done(((f32[768,1536]{1,0:T(8,128)}), f32[24,1536]{1,0:T(8,128)}) %reduce-scatter.32.cloned.1.call-update) | async-done | bytes 147472 | tf_op jit(solution)/shard_map/reduce_scatter | solution.py:324
  1144.7 117.1 %reduce-scatter.16.cloned.1.call-done = f32[24,2304]{1,0:T(8,128)} async-done(((f32[768,2304]{1,0:T(8,128)}), f32[24,2304]{1,0:T(8,128)}) %reduce-scatter.16.cloned.1.call-update) | async-done | bytes 221200 | tf_op jit(solution)/shard_map/reduce_scatter | solution.py:321
  1269.0 134.3 %reduce-scatter.26.cloned.1.call-done = f32[96,768]{1,0:T(8,128)} async-done(((f32[3072,768]{1,0:T(8,128)}), f32[96,768]{1,0:T(8,128)}) %reduce-scatter.26.cloned.1.call-update) | async-done | bytes 294928 | tf_op jit(solution)/shard_map/reduce_scatter | solution.py:327
  1411.0 132.5 %reduce-scatter.24.cloned.1.call-done = f32[24,3072]{1,0:T(8,128)} async-done(((f32[768,3072]{1,0:T(8,128)}), f32[24,3072]{1,0:T(8,128)}) %reduce-scatter.24.cloned.1.call-update) | async-done | bytes 294928 | tf_op jit(solution)/shard_map/reduce_scatter | solution.py:326
  1551.2 262.5 %reduce-scatter.30.cloned.1.call-done = f32[128,1728]{0,1:T(8,128)} async-done(((f32[128,55296]{0,1:T(8,128)}), f32[128,1728]{0,1:T(8,128)}) %reduce-scatter.30.cloned.1.call-update) | async-done | bytes 884752 | tf_op jit(solution)/shard_map/reduce_scatter | solution.py:331
  1814.9 12.4 all_gather.94
  1829.2 255.2 %reduce-scatter.28.cloned.1.call-done = f32[128,1728]{0,1:T(8,128)} async-done(((f32[128,55296]{0,1:T(8,128)}), f32[128,1728]{0,1:T(8,128)}) %reduce-scatter.28.cloned.1.call-update) | async-done | bytes 884752 | tf_op jit(solution)/shard_map/reduce_scatter | solution.py:328
  2085.7 12.4 all_gather.93
  (566 shorter events, 338.3 us)
Async XLA Ops:
  7.2 91.8 %copy-start = (bf16[768,768]{1,0:T(8,128)(2,1)S(1)}, bf16[768,768]{1,0:T(8,128)(2,1)}, u32[]{:S(2)}) copy-start(bf16[768,768]{1,0:T(8,128)(2,1)} %param.20) | copy-start | bytes 3538948
  7.2 91.7 %all-gather.21.cloned.1.call-start = ((), (), s32[]{:S(2)}) async-start(), calls=%async_computation.14 | async-start | bytes 2506752 | tf_op jit(solution)/shard_map/all_gather | solution.py:189
  8.0 100.2 %all-gather.13.cloned.1.call-start = ((), (), s32[]{:S(2)}) async-start(), calls=%async_computation.10 | async-start | bytes 3760128 | tf_op jit(solution)/shard_map/all_gather | solution.py:186
  8.7 48.1 %copy-start.149 = (bf16[64,8]{0,1:T(8,128)(2,1)S(1)}, bf16[64,8]{0,1:T(8,128)(2,1)}, u32[]{:S(2)}) copy-start(bf16[64,8]{0,1:T(8,128)(2,1)} %param.34) | copy-start | bytes 3076
  8.8 137.7 %all-gather.15.cloned.1.call-start = ((), (), s32[]{:S(2)}) async-start(), calls=%async_computation.11 | async-start | bytes 1253376 | tf_op jit(solution)/shard_map/all_gather | solution.py:187
  9.5 67.2 %copy-start.130 = (bf16[128,144]{0,1:T(8,128)(2,1)S(1)}, bf16[128,144]{0,1:T(8,128)(2,1)}, u32[]{:S(2)}) copy-start(bf16[128,144]{0,1:T(8,128)(2,1)} %param.37) | copy-start | bytes 110596
  9.5 248.6 %all-gather.19.cloned.1.call-start = ((), (), s32[]{:S(2)}) async-start(), calls=%async_computation.13 | async-start | bytes 15040512 | tf_op jit(solution)/shard_map/all_gather | solution.py:196
  10.1 358.7 %all-gather.17.cloned.1.call-start = ((), (), s32[]{:S(2)}) async-start(), calls=%async_computation.12 | async-start | bytes 15040512 | tf_op jit(solution)/shard_map/all_gather | solution.py:195
  10.7 396.8 %all-gather.23.cloned.1.call-start = ((), (), s32[]{:S(2)}) async-start(), calls=%async_computation.15 | async-start | bytes 1253376 | tf_op jit(solution)/shard_map/all_gather | solution.py:188
  11.2 435.8 %all-gather.25.cloned.1.call-start = ((), (), s32[]{:S(2)}) async-start(), calls=%async_computation.16 | async-start | bytes 1253376 | tf_op jit(solution)/shard_map/all_gather | solution.py:190
  12.0 489.7 %all-gather.27.cloned.1.call-start = ((), (), s32[]{:S(2)}) async-start(), calls=%async_computation.17 | async-start | bytes 5013504 | tf_op jit(solution)/shard_map/all_gather | solution.py:191
  12.7 543.2 %all-gather.29.cloned.1.call-start = ((), (), s32[]{:S(2)}) async-start(), calls=%async_computation.18 | async-start | bytes 5013504 | tf_op jit(solution)/shard_map/all_gather | solution.py:192
  13.5 879.3 %reduce-scatter.34.cloned.1.call-start = ((), (), s32[]{:S(2)}) async-start(), calls=%async_computation.28 | async-start | bytes 1216512
  14.9 87.8 %copy-start.112 = (s32[384]{0:T(512)}, s32[384]{0:T(512)S(1)}, u32[]{:S(2)}) copy-start(s32[384]{0:T(512)S(1)} %select_reduce_fusion) | copy-start | bytes 4612
  15.1 93.1 %copy-start.110 = (f32[384]{0:T(512)}, f32[384]{0:T(512)S(1)}, u32[]{:S(2)}) copy-start(f32[384]{0:T(512)S(1)} %fusion.122) | copy-start | bytes 4612
  39.4 68.8 %copy-start.96 = (f32[768]{0:T(1024)}, f32[768]{0:T(1024)S(1)}, u32[]{:S(2)}) copy-start(f32[768]{0:T(1024)S(1)} %get-tuple-element.104) | copy-start | bytes 9220
  56.9 45.8 %copy-start.108 = (bf16[16,4,8]{2,1,0:T(4,128)(2,1)}, bf16[16,4,8]{2,1,0:T(4,128)(2,1)S(1)}, u32[]{:S(2)}) copy-start(bf16[16,4,8]{2,1,0:T(4,128)(2,1)S(1)} %all-gather.1) | copy-start | bytes 3076
  148.5 109.6 %copy-start.145 = (f32[384]{0:T(512)}, f32[384]{0:T(512)S(1)}, u32[]{:S(2)}) copy-start(f32[384]{0:T(512)S(1)} %get-tuple-element.123) | copy-start | bytes 4612
  148.5 109.6 %copy-start.120 = (bf16[8,128]{1,0:T(8,128)(2,1)S(1)}, bf16[8,128]{1,0:T(8,128)(2,1)}, u32[]{:S(2)}) copy-start(bf16[8,128]{1,0:T(8,128)(2,1)} %copy-done.119) | copy-start | bytes 6148
  148.5 109.5 %copy-start.131 = (f32[384]{0:T(512)}, f32[384]{0:T(512)S(1)}, u32[]{:S(2)}) copy-start(f32[384]{0:T(512)S(1)} %fusion.123) | copy-start | bytes 4612
  151.0 244.0 %copy-start.40 = (bf16[384,768]{1,0:T(8,128)(2,1)}, bf16[384,768]{1,0:T(8,128)(2,1)S(1)}, u32[]{:S(2)}) copy-start(bf16[384,768]{1,0:T(8,128)(2,1)S(1)} %get-tuple-element.125) | copy-start | bytes 1769476
  619.9 278.7 %reduce-scatter.22.cloned.1.call-start = ((), (), s32[]{:S(2)}) async-start(), calls=%async_computation.22 | async-start | bytes 2433024 | tf_op jit(solution)/shard_map/reduce_scatter | solution.py:325
  623.5 299.0 %reduce-scatter.20.cloned.1.call-start = ((), (), s32[]{:S(2)}) async-start(), calls=%async_computation.21 | async-start | bytes 2433024 | tf_op jit(solution)/shard_map/reduce_scatter | solution.py:323
  627.6 398.2 %reduce-scatter.18.cloned.1.call-start = ((), (), s32[]{:S(2)}) async-start(), calls=%async_computation.20 | async-start | bytes 2433024 | tf_op jit(solution)/shard_map/reduce_scatter | solution.py:322
  634.1 504.0 %reduce-scatter.32.cloned.1.call-start = ((), (), s32[]{:S(2)}) async-start(), calls=%async_computation.27 | async-start | bytes 4866048 | tf_op jit(solution)/shard_map/reduce_scatter | solution.py:324
  658.5 603.4 %reduce-scatter.16.cloned.1.call-start = ((), (), s32[]{:S(2)}) async-start(), calls=%async_computation.19 | async-start | bytes 7299072 | tf_op jit(solution)/shard_map/reduce_scatter | solution.py:321
  683.2 720.2 %reduce-scatter.26.cloned.1.call-start = ((), (), s32[]{:S(2)}) async-start(), calls=%async_computation.24 | async-start | bytes 9732096 | tf_op jit(solution)/shard_map/reduce_scatter | solution.py:327
  693.1 850.4 %reduce-scatter.24.cloned.1.call-start = ((), (), s32[]{:S(2)}) async-start(), calls=%async_computation.23 | async-start | bytes 9732096 | tf_op jit(solution)/shard_map/reduce_scatter | solution.py:326
  701.2 1112.5 %reduce-scatter.30.cloned.1.call-start = ((), (), s32[]{:S(2)}) async-start(), calls=%async_computation.26 | async-start | bytes 29196288 | tf_op jit(solution)/shard_map/reduce_scatter | solution.py:331
  741.1 1343.2 %reduce-scatter.28.cloned.1.call-start = ((), (), s32[]{:S(2)}) async-start(), calls=%async_computation.25 | async-start | bytes 29196288 | tf_op jit(solution)/shard_map/reduce_scatter | solution.py:328
  820.1 64.1 %copy-start.139 = (f32[384]{0:T(512)S(1)}, f32[384]{0:T(512)}, u32[]{:S(2)}) copy-start(f32[384]{0:T(512)} %copy-done.138) | copy-start | bytes 4612
  820.1 64.8 %copy-start.6 = (f32[384,768]{1,0:T(8,128)S(1)}, f32[384,768]{1,0:T(8,128)}, u32[]{:S(2)}) copy-start(f32[384,768]{1,0:T(8,128)} %copy-done.5) | copy-start | bytes 3538948
  (160 other events, 726.1 us)
Sparse Core Ops, SparseCore 0:
  10.4 44.9 all-gather.20
  57.7 48.1 all-gather.12
  108.1 38.2 all-gather.14
  148.5 109.5 all-gather.18
  260.1 108.6 all-gather.16
  370.9 36.4 all-gather.22
  409.7 37.3 all-gather.24
  449.3 52.3 all-gather.26
  504.0 51.9 all-gather.28
  620.1 94.7 reduce-scatter.33
  720.1 98.2 reduce-scatter.21
  824.4 98.0 reduce-scatter.19
  927.8 98.0 reduce-scatter.17
  1032.1 105.9 reduce-scatter.31
  1143.6 118.2 reduce-scatter.15
  1268.6 134.6 reduce-scatter.25
  1409.1 134.3 reduce-scatter.23
  1550.9 262.7 reduce-scatter.29
  1821.3 263.0 reduce-scatter.27
where the time goes:
time: 2110 us
  waiting for transfers between devices  1480 us (70%)
  matrix products  263 us (12%)
  blocking collectives  190 us (9%)
  local copies, waits for them, and re-layouts  110 us (5%)
  other arithmetic  42.2 us (2%)
    reduce_scatter x1, waiting for transfers between devices, per_device(): lax.psum_scatter(exact_rows(hidden_wide, grad_made_up), ('fsdp', 'dp'), s...  263 us
    reduce_scatter x1, waiting for transfers between devices, per_device(): lax.psum_scatter(exact_rows(hidden_wide, grad_made_down), ('fsdp', 'dp'),...  255 us
    reduce_scatter x1, waiting for transfers between devices, per_device(): lax.psum_scatter(grad_feed_out, ('fsdp', 'dp'), scatter_dimension=0, tile...  134 us
    reduce_scatter x1, waiting for transfers between devices, per_device(): lax.psum_scatter(grad_feed_in, ('fsdp', 'dp'), scatter_dimension=0, tiled...  133 us
    reduce_scatter x1, waiting for transfers between devices, per_device(): lax.psum_scatter(grad_qkv, ('fsdp', 'dp'), scatter_dimension=0, tiled=True)  117 us
    all_gather x1, waiting for transfers between devices, per_device(): lax.all_gather(maker_up, 'fsdp', axis=1, tiled=True)  107 us
    reduce_scatter x1, waiting for transfers between devices, per_device(): lax.psum_scatter(grad_keyval, ('fsdp', 'dp'), scatter_dimension=0, tiled=...  106 us
    all_gather x1, waiting for transfers between devices, per_device(): lax.all_gather(maker_down, 'fsdp', axis=1, tiled=True)  99.5 us
  transfers between devices with their start and end apart: 19, of which 15 were waited for; matrix products, arithmetic and copies ran while one was open for 16% of the time, Pallas kernels for 0%

commit v1 on v0

v1 whole, which is shorter than its diff:
```python
import functools
import math

import jax
import jax.numpy as jnp
from jax import lax
from jax.experimental import pallas as pl
from jax.experimental.pallas import tpu as pltpu
from jax.sharding import PartitionSpec as P

norm_epsilon = 1e-06
masked_score = -1000000000.0
highest = lax.Precision.HIGHEST


def matmul(left, right):
    return jnp.dot(left, right, preferred_element_type=jnp.float32)


def exact_rows(left, right):
    return lax.dot_general(
        left, right, (((0,), (0,)), ((), ())), precision=highest, preferred_element_type=jnp.float32
    )


def exact_cols(left, right):
    return lax.dot_general(
        left, right, (((1,), (1,)), ((), ())), precision=highest, preferred_element_type=jnp.float32
    )


def segment_rows(lengths, count):
    ends = jnp.cumsum(lengths)
    places = jnp.arange(count, dtype=jnp.int32)
    return jnp.sum((places[:, None] >= ends[None, :]).astype(jnp.int32), axis=1)


def dot(left, right):
    return jnp.dot(left, right, preferred_element_type=jnp.float32)


def dot_nt(left, right):
    return lax.dot_general(
        left, right, (((1,), (1,)), ((), ())), preferred_element_type=jnp.float32
    )


def dot_tn(left, right):
    return lax.dot_general(
        left, right, (((0,), (0,)), ((), ())), preferred_element_type=jnp.float32
    )


def rms_rate(values):
    return lax.rsqrt(jnp.mean(values * values, axis=-1, keepdims=True) + norm_epsilon)


def rms_back(values, rate, gain, grad):
    scaled = grad * gain
    inner = jnp.mean(scaled * values, axis=-1, keepdims=True)
    return rate * (scaled - values * (rate * rate * inner)), grad * values * rate


gelu_slope = math.sqrt(2.0 / math.pi)
gelu_cube = 0.044715


def gelu(values):
    inner = gelu_slope * values * (1.0 + gelu_cube * values * values)
    return 0.5 * values * (1.0 + jnp.tanh(inner))


def gelu_back(values):
    square = values * values
    bent = jnp.tanh(gelu_slope * values * (1.0 + gelu_cube * square))
    slope = gelu_slope * (1.0 + 3.0 * gelu_cube * square)
    return 0.5 * (1.0 + bent) + 0.5 * values * (1.0 - bent * bent) * slope


def halves(dtype):
    lane = lax.broadcasted_iota(jnp.int32, (1, 128), 1)
    first = (lane < 64).astype(jnp.float32)
    return first.astype(dtype), (1.0 - first).astype(dtype)


def lanes(start):
    return pl.ds(pl.multiple_of(start, 128), 128)


def attend_forward(queries, keys, values, starts, cap, probs, mixed):
    factor = math.log2(math.e) / 8.0
    marks = halves(jnp.bfloat16)

    def pair(p, _):
        query = queries[:, lanes(starts[0] + p * 128)].T
        key = keys[:, lanes(starts[1] + p * 128)]
        value = values[:, lanes(starts[2] + p * 128)].T
        parts = []
        for head in (0, 1):
            scores = jnp.minimum(dot(key * marks[head], query) * factor, cap[...])
            weights = jnp.exp2(scores - jnp.max(scores, axis=0, keepdims=True))
            weights = weights * (1.0 / jnp.sum(weights, axis=0, keepdims=True))
            weights = weights.astype(jnp.bfloat16)
            probs[2 * p + head] = weights
            parts.append(dot(value[head * 64 : (head + 1) * 64], weights))
        mixed[:, lanes(p * 128)] = jnp.concatenate(parts, axis=0).T.astype(jnp.bfloat16)
        return 0

    lax.fori_loop(0, mixed.shape[1] // 128, pair, 0)


def attend_backward(queries, keys, values, starts, probs, grad_mixed, grads, places):
    marks = halves(jnp.bfloat16)
    first, second = halves(jnp.float32)

    def pair(p, _):
        query = queries[:, lanes(starts[0] + p * 128)]
        key = keys[:, lanes(starts[1] + p * 128)]
        value = values[:, lanes(starts[2] + p * 128)]
        grad = grad_mixed[:, lanes(p * 128)]
        key_turned = key.T
        grad_turned = grad.T
        grad_query, grad_key, grad_value = [], 0.0, 0.0
        for head, mark in ((0, first), (1, second)):
            weights = probs[2 * p + head]
            grad_value += dot(weights, grad) * mark
            wide = weights.astype(jnp.float32)
            product = wide * dot(value * marks[head], grad_turned)
            product = product - wide * jnp.sum(product, axis=0, keepdims=True)
            product = product.astype(jnp.bfloat16)
            grad_key += dot(product, query) * mark
            grad_query.append(dot(key_turned[head * 64 : (head + 1) * 64], product))
        grad_query = jnp.concatenate(grad_query, axis=0).T * 0.125
        grads[0][:, lanes(places[0] + p * 128)] = grad_query.astype(jnp.bfloat16)
        grads[1][:, lanes(places[1] + p * 128)] = (grad_key * 0.125).astype(jnp.bfloat16)
        grads[2][:, lanes(places[2] + p * 128)] = grad_value.astype(jnp.bfloat16)
        return 0

    lax.fori_loop(0, grad_mixed.shape[1] // 128, pair, 0)


def adapter_forward(branch, tasks, cond, down, up, mask):
    gain = 1.0 + dot(tasks[...], cond[...])
    normed = (branch * rms_rate(branch) * gain).astype(jnp.bfloat16)
    squeezed = dot(normed, down[...]) * mask[...].astype(jnp.float32)
    return branch + dot(gelu(squeezed).astype(jnp.bfloat16), up[...]), squeezed


def adapter_backward(branch, squeezed, tasks, cond, down, up, mask, grad, outs):
    low = grad.astype(jnp.bfloat16)
    outs[1][...] = dot_tn(gelu(squeezed).astype(jnp.bfloat16), low).astype(jnp.bfloat16)
    grad_squeezed = (gelu_back(squeezed) * dot_nt(low, up[...])).astype(jnp.bfloat16) * mask[...]
    gain = 1.0 + dot(tasks[...], cond[...])
    rate = rms_rate(branch)
    normed = (branch * rate * gain).astype(jnp.bfloat16)
    outs[0][...] = dot_tn(normed, grad_squeezed).astype(jnp.bfloat16)
    grad_branch, grad_gain = rms_back(branch, rate, gain, dot_nt(grad_squeezed, down[...]))
    outs[2][...] = dot_tn(tasks[...], grad_gain.astype(jnp.bfloat16))
    return grad + grad_branch


def whole_unit(weight):
    return weight.reshape(-1, weight.shape[-1])


def load_units(packed, first, held, sems):
    copies = []
    for u in range(held.shape[0]):
        copy = pltpu.make_async_copy(packed.at[:, first + u], held.at[u], sems.at[u])
        copy.start()
        copies.append(copy)
    return copies


def emit(place, outs, unit, grad):
    if len(outs) == 1:
        outs[0][0, 0, unit] = grad.astype(jnp.bfloat16)
        return
    rows = outs[0].shape[-2]
    for j in range(8):
        even = grad[2 * j * rows : (2 * j + 1) * rows].astype(jnp.bfloat16)
        odd = grad[(2 * j + 1) * rows : (2 * j + 2) * rows].astype(jnp.bfloat16)
        emit_block(place, outs, unit, j, even, odd)


def emit_block(place, outs, unit, j, even, odd):
    at = ((j & 1) ^ place[1], (j // 2 - place[0]) & 3, unit)
    if len(outs[0].shape) == 6:
        half = outs[0].shape[3]
        at = ((unit // half) ^ place[3],) + at[:2] + (unit % half,)
    outs[0][at] = jnp.where(place[2] == 0, odd, even)
    outs[1][at] = jnp.where(place[2] == 0, even, odd)


def first_kernel(
    tokens, gains, packed, cap, tasks, cond, down, up, mask,
    normed, projected, probs, mixed, branch, squeezed, stream,
    held, sems,
):
    cond, down, up = cond.at[0], down.at[0], up.at[0]
    copies = load_units(packed, 0, held, sems)
    wide = tokens[...].astype(jnp.float32)
    normed[...] = (wide * rms_rate(wide) * gains[0:1]).astype(jnp.bfloat16)
    width = wide.shape[1]
    for u in range(3):
        copies[u].wait()
        projected[:, u * width : (u + 1) * width] = dot(normed[...], whole_unit(held[u])).astype(
            jnp.bfloat16
        )
    attend_forward(projected, projected, projected, (0, width, 2 * width), cap, probs, mixed)
    copies[3].wait()
    branch[...] = dot(mixed[...], whole_unit(held[3]))
    adapted, squeezed[...] = adapter_forward(branch[...], tasks, cond, down, up, mask)
    stream[...] = tokens[...].astype(jnp.float32) + adapted


def second_kernel(
    stream, gains, packed, memory, cap, tasks, cond, down, up, mask,
    normed, query, keyval, probs, mixed, branch, squeezed, result,
    held, sems,
):
    cond, down, up = cond.at[1], down.at[1], up.at[1]
    copies = load_units(packed, 4, held, sems)
    wide = stream[...]
    normed[...] = (wide * rms_rate(wide) * gains[1:2]).astype(jnp.bfloat16)
    width = wide.shape[1]
    copies[0].wait()
    query[...] = dot(normed[...], whole_unit(held[0])).astype(jnp.bfloat16)
    for u in range(2):
        copies[1 + u].wait()
        keyval[:, u * width : (u + 1) * width] = dot(memory[...], whole_unit(held[1 + u])).astype(
            jnp.bfloat16
        )
    attend_forward(query, keyval, keyval, (0, 0, width), cap, probs, mixed)
    copies[3].wait()
    branch[...] = dot(mixed[...], whole_unit(held[3]))
    adapted, squeezed[...] = adapter_forward(branch[...], tasks, cond, down, up, mask)
    result[...] = stream[...] + adapted


def third_kernel(
    place, stream, gains, packed, out_grad, tasks, cond, down, up, mask,
    result, normed, before, grad_branch, grad_down, grad_up, grad_cond, *rest,
):
    cond, down, up = cond.at[2], down.at[2], up.at[2]
    outs, (held_in, held_out, active, total, sems) = rest[:-5], rest[-5:]
    units = active.shape[0]
    copies = load_units(packed, 8, held_in, sems)
    last = pltpu.make_async_copy(packed.at[:, 8 + units :], held_out, sems.at[units])
    last.start()
    wide = stream[...]
    normed[...] = (wide * rms_rate(wide) * gains[2:3]).astype(jnp.bfloat16)
    for copy in copies:
        copy.wait()

    def ahead(u, _):
        value = dot(normed[...], whole_unit(held_in[u]))
        before[u] = value
        active[u] = gelu(value).astype(jnp.bfloat16)
        return 0

    lax.fori_loop(0, units, ahead, 0)
    last.wait()
    total[...] = jnp.zeros_like(total)

    def gather(u, _):
        total[...] += dot(active[u], out_rows(held_out, units, u))
        return 0

    lax.fori_loop(0, units, gather, 0)
    branch = total[...]
    adapted, squeezed = adapter_forward(branch, tasks, cond, down, up, mask)
    result[...] = (stream[...] + adapted).astype(jnp.bfloat16)
    grad_branch[...] = adapter_backward(
        branch, squeezed, tasks, cond, down, up, mask,
        out_grad[...].astype(jnp.float32), (grad_down, grad_up, grad_cond),
    ).astype(jnp.bfloat16)
    half = active.shape[2] // 2

    def out_share(j, _):
        columns = pl.ds(pl.multiple_of((j & 1) * half, half), half)
        grad = dot_tn(active[j // 2, :, columns], grad_branch[...]).astype(jnp.bfloat16)
        if len(outs) == 1:
            outs[0][0, 0, j // 2, columns] = grad
        else:
            rows = outs[0].shape[-2]
            for u in range(4):
                emit_block(
                    place, outs, u, j,
                    grad[u * rows : (u + 1) * rows], grad[(4 + u) * rows : (5 + u) * rows],
                )
        return 0

    lax.fori_loop(0, 2 * units, out_share, 0)


def out_rows(held_out, units, u):
    if held_out.shape[0] == 1:
        return whole_unit(held_out[0, u])
    share = held_out.shape[0] // units
    return whole_unit(held_out[pl.ds(u * share, share)])


def fourth_kernel(
    place, stream, gains, packed, out_grad, normed, before, grad_branch,
    grad_stream, grad_gain, *rest,
):
    outs, (held_in, held_out, total, sems) = rest[:-4], rest[-4:]
    units = before.shape[0]
    copies = load_units(packed, 8, held_in, sems)
    last = pltpu.make_async_copy(packed.at[:, 8 + units :], held_out, sems.at[units])
    last.start()
    for copy in copies:
        copy.wait()
    last.wait()
    total[...] = jnp.zeros_like(total)

    def back(u, _):
        grad = dot_nt(grad_branch[...], out_rows(held_out, units, u)) * gelu_back(before[u])
        grad = grad.astype(jnp.bfloat16)
        emit(place, outs, u, dot_tn(normed[...], grad))
        total[...] += dot_nt(grad, whole_unit(held_in[u]))
        return 0

    lax.fori_loop(0, units, back, 0)
    wide = stream[...]
    grad, gain_rows = rms_back(wide, rms_rate(wide), gains[2:3], total[...])
    grad_stream[...] = out_grad[...].astype(jnp.float32) + grad
    grad_gain[...] = jnp.sum(gain_rows, axis=0, keepdims=True)


def branch_kernel(
    index, unit, grad_result, packed, branch, squeezed, tasks, cond, down, up, mask,
    grad_branch, grad_mixed, grad_down, grad_up, grad_cond,
    held, sems,
):
    cond, down, up = cond.at[index], down.at[index], up.at[index]
    (copy,) = load_units(packed, unit, held, sems)
    grad_branch[...] = adapter_backward(
        branch[...], squeezed[...], tasks, cond, down, up, mask,
        grad_result[...], (grad_down, grad_up, grad_cond),
    ).astype(jnp.bfloat16)
    copy.wait()
    grad_mixed[...] = dot_nt(grad_branch[...], whole_unit(held[0])).astype(jnp.bfloat16)


def cross_kernel(
    place, grad_result, stream, gains, packed, memory, normed, query, keyval, probs, mixed,
    grad_branch, grad_mixed,
    grad_stream, grad_memory, grad_gain, *rest,
):
    outs, (held, grad_query, grad_keyval, sems) = rest[:-4], rest[-4:]
    copies = load_units(packed, 4, held, sems)
    width = stream.shape[1]
    attend_backward(
        query, keyval, keyval, (0, 0, width), probs, grad_mixed,
        (grad_query, grad_keyval, grad_keyval), (0, 0, width),
    )
    emit(place, outs, 3, dot_tn(mixed[...], grad_branch[...]))
    emit(place, outs, 0, dot_tn(normed[...], grad_query[...]))
    for copy in copies:
        copy.wait()
    for u in range(2):
        grad = grad_keyval[:, u * width : (u + 1) * width]
        emit(place, outs, 1 + u, dot_tn(memory[...], grad))
        if u == 0:
            grad_memory[...] = dot_nt(grad, whole_unit(held[1 + u]))
        else:
            grad_memory[...] += dot_nt(grad, whole_unit(held[1 + u]))
    wide = stream[...]
    grad, gain_rows = rms_back(
        wide, rms_rate(wide), gains[1:2], dot_nt(grad_query[...], whole_unit(held[0]))
    )
    grad_stream[...] = grad_result[...] + grad
    grad_gain[...] = jnp.sum(gain_rows, axis=0, keepdims=True)


def self_kernel(
    place, grad_stream, tokens, gains, packed, normed, projected, probs, mixed, grad_branch, grad_mixed,
    grad_tokens, grad_gain, *rest,
):
    outs, (held, grad_projected, total, sems) = rest[:-4], rest[-4:]
    copies = load_units(packed, 0, held, sems)
    width = tokens.shape[1]
    attend_backward(
        projected, projected, projected, (0, width, 2 * width), probs, grad_mixed,
        (grad_projected,) * 3, (0, width, 2 * width),
    )
    emit(place, outs, 3, dot_tn(mixed[...], grad_branch[...]))
    for u in range(3):
        copies[u].wait()
        grad = grad_projected[:, u * width : (u + 1) * width]
        emit(place, outs, u, dot_tn(normed[...], grad))
        if u == 0:
            total[...] = dot_nt(grad, whole_unit(held[u]))
        else:
            total[...] += dot_nt(grad, whole_unit(held[u]))
    wide = tokens[...].astype(jnp.float32)
    grad, gain_rows = rms_back(wide, rms_rate(wide), gains[0:1], total[...])
    grad_tokens[...] = grad_stream[...] + grad
    grad_gain[...] = jnp.sum(gain_rows, axis=0, keepdims=True)


def sum_kernel(*refs):
    total = refs[0][...].astype(jnp.float32)
    for ref in refs[1:-1]:
        total = total + ref[...].astype(jnp.float32)
    refs[-1][...] = total.astype(jnp.bfloat16)


def swap(values, axis, count, mate):
    return lax.ppermute(values, axis, [(i, mate(i)) for i in range(count)])


def place_parts():
    place = lax.axis_index("fsdp")
    return place // 4, (place // 2) % 2, place % 2


def ring_gather(block):
    z, y, core = place_parts()
    shifted = [swap(block, "fsdp", 16, lambda i, d=d: (i + 4 * d) % 16) for d in (3, 2, 1)]
    line = jnp.stack(shifted[:1] + shifted[1:] + [block])
    line = lax.dynamic_slice_in_dim(jnp.concatenate([line, line]), 3 - z, 4, 0)
    other = swap(line, "fsdp", 16, lambda i: i ^ 2)
    both = jnp.stack([jnp.where(y == 0, line, other), jnp.where(y == 0, other, line)], axis=1)
    other = swap(both, "fsdp", 16, lambda i: i ^ 1)
    whole = jnp.stack([jnp.where(core == 0, both, other), jnp.where(core == 0, other, both)], axis=2)
    return whole.reshape((16,) + block.shape)


def add_low(left, right):
    return (left.astype(jnp.float32) + right.astype(jnp.float32)).astype(jnp.bfloat16)


def core_swap(sent):
    return swap(sent, "fsdp", 16, lambda i: i ^ 1)


def y_swap(sent):
    return swap(sent, "fsdp", 16, lambda i: i ^ 2)


def x_swap(sent):
    return swap(sent, "dp", 2, lambda i: i ^ 1)


def z_parts(kept, got):
    return [add_low(kept[d], got[d]) for d in range(4)]


def z_swaps(parts):
    return [swap(parts[d], "fsdp", 16, lambda i, d=d: (i + 4 * d) % 16) for d in (1, 2, 3)]


def z_total(parts, far):
    total = parts[0].astype(jnp.float32)
    for part in far:
        total = total + part.astype(jnp.float32)
    return total.astype(jnp.bfloat16)


def both_halves(total, other, first_x):
    return jnp.concatenate(
        [jnp.where(first_x, total, other), jnp.where(first_x, other, total)]
    ).astype(jnp.float32)


def after(values, *others):
    return lax.optimization_barrier((values, others))[0]


def ring_sum(values):
    for bit in (1, 2, 4, 8):
        values = values + swap(values, "fsdp", 16, lambda i, bit=bit: i ^ bit)
    return values


def gather_shards(block, ring):
    return ring_gather(block) if ring else lax.all_gather(block, "fsdp", axis=0)


def block_share(blocks):
    part = lax.psum_scatter(blocks, "fsdp", scatter_dimension=0, tiled=False)
    return lax.psum(part.astype(jnp.float32), "dp")


def ring_order(blocks):
    z, y, core = place_parts()
    parts = blocks.reshape((4, 2, 2) + blocks.shape[1:])
    line = lax.dynamic_slice_in_dim(jnp.concatenate([parts, parts]), z, 4, 0)
    ordered = [jnp.where(y == 0, line[:, b], line[:, 1 - b]) for b in (0, 1)]
    sent = jnp.stack([jnp.where(core == 0, part[:, 1], part[:, 0]) for part in ordered])
    kept = jnp.stack([jnp.where(core == 0, part[:, 0], part[:, 1]) for part in ordered])
    return sent, kept


def share_of(grads, devices, by_rows):
    whole = grads[0][0, 0]
    count, width = whole.shape[0], whole.shape[-1]
    if by_rows:
        return block_share(whole.reshape(devices, count, -1, width))
    blocks = jnp.transpose(whole.reshape(count, devices, -1, width), (1, 0, 2, 3))
    return block_share(blocks)


def sum_shards(values, ring):
    return ring_sum(values) if ring else lax.psum(values, "fsdp")


def units_of(shard, width):
    rows, columns = shard.shape
    return jnp.transpose(shard.reshape(rows, columns // width, width), (1, 0, 2))


def joined(units):
    return jnp.transpose(units, (1, 0, 2)).reshape(units.shape[1], -1)


def call(kernel, operands, shapes, scratch, flops, packed_at=None, place_first=False):
    specs = [pl.BlockSpec(memory_space=pltpu.VMEM) for _ in operands]
    if packed_at is not None:
        specs[packed_at] = pl.BlockSpec(memory_space=pl.ANY)
    if place_first:
        specs[0] = pl.BlockSpec(memory_space=pltpu.SMEM)
    outs = [jax.ShapeDtypeStruct(shape, dtype) for shape, dtype in shapes]
    moved = sum(math.prod(shape) * jnp.dtype(dtype).itemsize for shape, dtype in shapes)
    moved += sum(operand.size * operand.dtype.itemsize for operand in operands)
    return pl.pallas_call(
        kernel,
        out_shape=outs,
        in_specs=specs,
        out_specs=[pl.BlockSpec(memory_space=pltpu.VMEM) for _ in outs],
        scratch_shapes=scratch,
        compiler_params=pltpu.CompilerParams(vmem_limit_bytes=60 * 1024 * 1024),
        cost_estimate=pl.CostEstimate(flops=flops, bytes_accessed=moved, transcendentals=0),
    )(*operands)


def per_device(
    devices,
    ring,
    tokens,
    memory,
    out_grad,
    target_len,
    source_len,
    task_ids,
    norm_gains,
    self_qkv,
    self_out,
    cross_query,
    cross_keyval,
    cross_out,
    feed_in,
    feed_out,
    task_table,
    hyper_in,
    maker_down,
    maker_up,
    maker_norm,
):
    width = tokens.shape[1]
    tasks = task_table.shape[0]
    embed = hyper_in.shape[0]
    table_width = task_table.shape[1]
    hyper_width = hyper_in.shape[1]
    gain_width = norm_gains.shape[1]
    down_span = maker_down.shape[1]
    norm_span = maker_norm.shape[1]
    bottleneck = down_span * devices // (3 * width)
    down_rows = 3 * width // devices
    piece = math.gcd(width, down_span)
    down_flat = down_span * tasks // piece
    small = jnp.concatenate(
        [
            jnp.pad(task_table.T, ((0, 0), (0, 128 - tasks))),
            jnp.pad(hyper_in.T, ((0, 0), (0, 128 - embed))),
            jnp.pad(norm_gains, ((0, 0), (0, 128 - gain_width))),
            jnp.zeros((-(table_width + hyper_width + 3) % 16, 128), jnp.bfloat16),
        ]
    )
    small = gather_shards(small, ring)
    whole_table = small[:, :table_width, :tasks].reshape(-1, tasks).T
    whole_hyper = small[:, table_width : table_width + hyper_width, :embed].reshape(-1, embed).T
    first = table_width + hyper_width
    whole_gains = jnp.transpose(small[:, first : first + 3, :gain_width], (1, 0, 2)).reshape(3, width)
    packed = jnp.concatenate(
        [
            units_of(shard, width).reshape(-1, width)
            for shard in (self_qkv, self_out, cross_query, cross_keyval, cross_out, feed_in, feed_out)
        ]
    )
    packed = lax.all_gather(packed, "fsdp", axis=0)
    unit = width // devices
    ff_units = feed_in.shape[1] // width
    packed = packed.reshape(devices, -1, unit, width)
    if not ring:
        layer = jnp.transpose(packed[:, : 8 + ff_units], (1, 0, 2, 3)).reshape(-1, width, width)
        last = packed[:, 8 + ff_units :].reshape(-1, width, width)
        packed = jnp.concatenate([layer, last])[None]
    pre_hidden = matmul(whole_table, whole_hyper)
    hidden = jax.nn.silu(pre_hidden).astype(jnp.bfloat16)
    own_down = matmul(hidden, maker_down).astype(jnp.bfloat16)
    own_up = matmul(hidden, maker_up).astype(jnp.bfloat16)
    own_norm = matmul(hidden, maker_norm).astype(jnp.bfloat16)
    own_down = jnp.transpose(own_down.reshape(tasks, down_rows, bottleneck), (1, 0, 2))
    made = jnp.concatenate(
        [
            own_down.reshape(down_flat, piece),
            own_up.reshape(down_flat, piece),
            jnp.pad(own_norm, ((0, 0), (0, max(piece, norm_span) - norm_span))).reshape(-1, piece),
        ]
    )
    made = gather_shards(made, ring)
    made_down = made[:, :down_flat].reshape(3, width, tasks * bottleneck)
    made_up = made[:, down_flat : 2 * down_flat].reshape(devices, tasks, down_span // piece, piece)
    made_up = jnp.transpose(made_up, (1, 0, 2, 3)).reshape(tasks, 3, bottleneck, width)
    made_up = jnp.transpose(made_up, (1, 0, 2, 3)).reshape(3, tasks * bottleneck, width)
    made_cond = made[:, 2 * down_flat :].reshape(devices, tasks, -1)[:, :, :norm_span]
    made_cond = jnp.transpose(made_cond, (1, 0, 2)).reshape(tasks, 3, width)
    made_cond = jnp.pad(jnp.transpose(made_cond, (1, 0, 2)), ((0, 0), (0, 128 - tasks), (0, 0)))
    tok_seg = segment_rows(target_len[0], tokens.shape[0])
    mem_seg = segment_rows(source_len[0], memory.shape[0])
    sequences = jnp.arange(target_len.shape[1], dtype=jnp.int32)
    row_task = jnp.sum(
        jnp.where(tok_seg[:, None] == sequences[None, :], task_ids[0][None, :], 0), axis=1
    )
    onehot = (row_task[:, None] == jnp.arange(128, dtype=jnp.int32)[None, :]).astype(jnp.bfloat16)
    mask = jnp.repeat(onehot[:, :tasks], bottleneck, axis=1)
    places = jnp.arange(tokens.shape[0], dtype=jnp.int32)
    self_allowed = (tok_seg[:, None] == tok_seg[None, :]) & (places[:, None] <= places[None, :])
    cross_allowed = mem_seg[:, None] == tok_seg[None, :]
    self_cap = jnp.where(self_allowed, -masked_score * 1e20, masked_score).astype(jnp.float32)
    cross_cap = jnp.where(cross_allowed, -masked_score * 1e20, masked_score).astype(jnp.float32)
    gains = jnp.pad(whole_gains.astype(jnp.float32), ((0, 5), (0, 0)))
    place = lax.axis_index("fsdp")
    here = jnp.stack([place // 4, (place // 2) % 2, place % 2, lax.axis_index("dp")]).astype(jnp.int32)
    adapters = (onehot, made_cond, made_down, made_up, mask)
    rows, memory_rows = tokens.shape[0], memory.shape[0]
    heads = width // 64
    low, full = jnp.bfloat16, jnp.float32
    span = tasks * bottleneck
    held_unit = packed.shape[:1] + packed.shape[2:]

    def held(count):
        return pltpu.VMEM((count,) + held_unit, low)

    def grad_shapes(count, by_x=False):
        if ring and by_x:
            return [((2, 2, 4, count // 2, unit, width), low)] * 2
        if ring:
            return [((2, 4, count, unit, width), low)] * 2
        return [((1, 1, count, width, width), low)]

    made_shapes = [((width, span), low), ((span, width), low), ((128, width), full)]
    gain_shape = [((1, width), full)]
    busy = 1700000000
    normed1, projected, probs1, mixed1, branch1, squeezed1, stream1 = call(
        first_kernel,
        (tokens, gains, packed, self_cap) + adapters,
        [
            ((rows, width), low),
            ((rows, 3 * width), low),
            ((heads, rows, rows), low),
            ((rows, width), low),
            ((rows, width), full),
            ((rows, span), full),
            ((rows, width), full),
        ],
        [held(4), pltpu.SemaphoreType.DMA((4,))],
        16 * busy,
        packed_at=2,
    )
    normed2, query2, keyval2, probs2, mixed2, branch2, squeezed2, stream2 = call(
        second_kernel,
        (stream1, gains, packed, memory, cross_cap) + adapters,
        [
            ((rows, width), low),
            ((rows, width), low),
            ((memory_rows, 2 * width), low),
            ((heads, memory_rows, rows), low),
            ((rows, width), low),
            ((rows, width), full),
            ((rows, span), full),
            ((rows, width), full),
        ],
        [held(4), pltpu.SemaphoreType.DMA((4,))],
        21 * busy,
        packed_at=2,
    )
    held_out = (packed.shape[0], ff_units) + packed.shape[2:]
    result, normed3, before, grad_branch, *found = call(
        third_kernel,
        (here, stream2, gains, packed, out_grad) + adapters,
        [((rows, width), low), ((rows, width), low), ((ff_units, rows, width), full), ((rows, width), low)]
        + made_shapes
        + grad_shapes(ff_units, True),
        [
            held(ff_units),
            pltpu.VMEM(held_out, low),
            pltpu.VMEM((ff_units, rows, width), low),
            pltpu.VMEM((rows, width), full),
            pltpu.SemaphoreType.DMA((ff_units + 1,)),
        ],
        22 * busy,
        packed_at=3,
        place_first=True,
    )
    made_three, grads_out = found[:3], found[3:]
    if ring:
        got_out = core_swap(grads_out[0])
    grad_stream, grad_gain_three, *grads_in = call(
        fourth_kernel,
        (here, stream2, gains, packed, out_grad, normed3, before, grad_branch),
        [((rows, width), full)] + gain_shape + grad_shapes(ff_units),
        [
            held(ff_units),
            pltpu.VMEM(held_out, low),
            pltpu.VMEM((rows, width), full),
            pltpu.SemaphoreType.DMA((ff_units + 1,)),
        ],
        18 * busy,
        packed_at=3,
        place_first=True,
    )
    if ring:
        got_in = core_swap(grads_in[0])
        got_out = after(got_out, grad_gain_three)
        sent_out, kept_out = (add_low(grads_out[1][b], got_out[b]) for b in (1, 0))
        other_out = x_swap(sent_out)
        grad_stream = after(grad_stream, sent_out)

    def branch_back(index, unit_at, grad_result, branch, squeezed):
        return call(
            functools.partial(branch_kernel, index, unit_at),
            (grad_result, packed, branch, squeezed) + adapters,
            [((rows, width), low)] * 2 + made_shapes,
            [held(1), pltpu.SemaphoreType.DMA((1,))],
            30 * busy,
            packed_at=1,
        )

    grad_branch, grad_mixed, *made_two = branch_back(1, 7, grad_stream, branch2, squeezed2)
    if ring:
        got_in = after(got_in, grad_mixed)
        sent_in, kept_in = (add_low(grads_in[1][b], got_in[b]) for b in (1, 0))
        other_in = y_swap(sent_in)
        grad_mixed = after(grad_mixed, sent_in)
    grad_stream, grad_memory, grad_gain_two, *grads_cross = call(
        cross_kernel,
        (here, grad_stream, stream1, gains, packed, memory)
        + (normed2, query2, keyval2, probs2, mixed2, grad_branch, grad_mixed),
        [((rows, width), full), ((memory_rows, width), full)] + gain_shape + grad_shapes(4, True),
        [
            held(3),
            pltpu.VMEM((rows, width), low),
            pltpu.VMEM((memory_rows, 2 * width), low),
            pltpu.SemaphoreType.DMA((3,)),
        ],
        24 * busy,
        packed_at=4,
        place_first=True,
    )
    if ring:
        got_cross = core_swap(grads_cross[0])
        other_out, other_in = after((other_out, other_in), grad_gain_two)
        sum_out = add_low(kept_out, other_out)
        other_out = y_swap(sum_out[1])
        parts_in = z_parts(kept_in, other_in)
        far_in = z_swaps(parts_in)
        grad_stream = after(grad_stream, sum_out, parts_in)
    grad_branch, grad_mixed, *made_one = branch_back(0, 3, grad_stream, branch1, squeezed1)
    if ring:
        got_cross = after(got_cross, grad_mixed)
        sent_cross, kept_cross = (add_low(grads_cross[1][b], got_cross[b]) for b in (1, 0))
        other_cross = x_swap(sent_cross)
        grad_mixed = after(grad_mixed, sent_cross)
    grad_tokens, grad_gain_one, *grads_self = call(
        self_kernel,
        (here, grad_stream, tokens, gains, packed)
        + (normed1, projected, probs1, mixed1, grad_branch, grad_mixed),
        [((rows, width), full)] + gain_shape + grad_shapes(4),
        [
            held(3),
            pltpu.VMEM((rows, 3 * width), low),
            pltpu.VMEM((rows, width), full),
            pltpu.SemaphoreType.DMA((3,)),
        ],
        18 * busy,
        packed_at=4,
        place_first=True,
    )
    grad_down = jnp.stack([made_one[0], made_two[0], made_three[0]])
    grad_up = jnp.stack([made_one[1], made_two[1], made_three[1]])
    grad_up = jnp.transpose(grad_up.reshape(3, tasks, bottleneck, width), (1, 0, 2, 3))
    grad_up = grad_up.reshape(tasks, devices, down_span // piece, piece)
    grad_norm = jnp.concatenate([made_one[2], made_two[2], made_three[2]], axis=1)[:tasks]
    grad_norm = grad_norm.astype(jnp.bfloat16)
    grad_norm = jnp.transpose(grad_norm.reshape(tasks, devices, norm_span), (1, 0, 2))
    made_blocks = jnp.concatenate(
            [
                grad_down.reshape(devices, down_flat, piece),
                jnp.transpose(grad_up, (1, 0, 2, 3)).reshape(devices, down_flat, piece),
                jnp.pad(grad_norm, ((0, 0), (0, 0), (0, max(piece, norm_span) - norm_span))).reshape(
                    devices, -1, piece
                ),
            ],
            axis=1,
        )
    if ring:
        first_x = lax.axis_index("dp") == 0
        sent_made, kept_made = ring_order(made_blocks)
        got_self, got_made = core_swap(grads_self[0]), core_swap(sent_made)
        far_in, other_cross, other_out = after((far_in, other_cross, other_out), grad_gain_one)
        total_in = call(sum_kernel, (parts_in[0], *far_in), [(parts_in[0].shape, low)], [], 100 * busy)[0]
        got_self, got_made = after((got_self, got_made), total_in)
        sent_self, kept_self = (add_low(grads_self[1][b], got_self[b]) for b in (1, 0))
        sum_cross = add_low(kept_cross, other_cross)
        parts_out = z_parts(sum_out[0], other_out)
        sum_made = add_low(kept_made, got_made)
        sent_self, sum_cross, parts_out, total_in, sum_made = lax.optimization_barrier(
            (sent_self, sum_cross, parts_out, total_in, sum_made)
        )
        flight = (y_swap(sent_self), z_swaps(parts_out), x_swap(total_in), y_swap(sum_made[1]))
        other_self, far_out, other_in, other_made = lax.optimization_barrier(flight)
        share_in = total_in.astype(jnp.float32) + other_in.astype(jnp.float32)
        parts_self = z_parts(kept_self, other_self)
        total_out = z_total(parts_out, far_out)
        parts_made = z_parts(sum_made[0], other_made)
        parts_self, total_out, parts_made = lax.optimization_barrier((parts_self, total_out, parts_made))
        flight = (z_swaps(parts_self), y_swap(sum_cross[1]), x_swap(total_out), z_swaps(parts_made))
        far_self, other_cross, other_out, far_made = lax.optimization_barrier(flight)
        share_out = both_halves(total_out, other_out, first_x)
        total_self = z_total(parts_self, far_self)
        parts_cross = z_parts(sum_cross[0], other_cross)
        total_made = z_total(parts_made, far_made)
        total_self, parts_cross, total_made = lax.optimization_barrier((total_self, parts_cross, total_made))
        flight = (x_swap(total_self), z_swaps(parts_cross), x_swap(total_made))
        other_self, far_cross, other_made = lax.optimization_barrier(flight)
        share_self = total_self.astype(jnp.float32) + other_self.astype(jnp.float32)
        total_cross = z_total(parts_cross, far_cross)
        share_cross = both_halves(total_cross, x_swap(total_cross), first_x)
        share_made = total_made.astype(jnp.float32) + other_made.astype(jnp.float32)
    else:
        share_in, share_out, share_cross, share_self = (
            share_of(grads, devices, grads is grads_out)
            for grads in (grads_in, grads_out, grads_cross, grads_self)
        )
        share_made = block_share(made_blocks)
    out_feed_in = joined(share_in)
    out_feed_out = share_out.reshape(-1, width)
    out_query = share_cross[0]
    out_keyval = joined(share_cross[1:3])
    out_cross_out = share_cross[3]
    out_qkv = joined(share_self[:3])
    out_self_out = share_self[3]
    norm_rows = tasks * max(1, norm_span // piece)
    own_down = jnp.transpose(
        share_made[:down_flat].reshape(down_rows, tasks, bottleneck), (1, 0, 2)
    ).reshape(tasks, down_span)
    own_up = share_made[down_flat : 2 * down_flat].reshape(tasks, down_span)
    own_norm = share_made[2 * down_flat : 2 * down_flat + norm_rows].reshape(tasks, -1)[:, :norm_span]
    hidden_wide = hidden.astype(jnp.float32)
    grad_hidden = (
        exact_cols(own_down, maker_down.astype(jnp.float32))
        + exact_cols(own_up, maker_up.astype(jnp.float32))
        + exact_cols(own_norm, maker_norm.astype(jnp.float32))
    )
    grad_gains = jnp.concatenate([grad_gain_one, grad_gain_two, grad_gain_three])
    grad_gains = grad_gains + x_swap(grad_gains) if ring else lax.psum(grad_gains, "dp")
    sums = sum_shards(jnp.concatenate([grad_hidden, grad_gains.reshape(-1, 128)]), ring)
    grad_hidden = sums[:tasks]
    out_gains = lax.dynamic_slice_in_dim(
        sums[tasks:].reshape(3, width), place * gain_width, gain_width, 1
    )
    _, silu_pull = jax.vjp(jax.nn.silu, pre_hidden)
    grad_pre_hidden = silu_pull(grad_hidden)[0]
    own_hyper = lax.dynamic_slice_in_dim(whole_hyper, place * table_width, table_width, 0)
    out_table = exact_cols(grad_pre_hidden, own_hyper.astype(jnp.float32))
    own_pre = lax.dynamic_slice_in_dim(grad_pre_hidden, place * hyper_width, hyper_width, 1)
    out_hyper = exact_rows(whole_table.astype(jnp.float32), own_pre)
    out_down = exact_rows(hidden_wide, own_down)
    out_up = exact_rows(hidden_wide, own_up)
    out_norm = exact_rows(hidden_wide, own_norm)
    return (
        result.astype(jnp.bfloat16),
        grad_tokens,
        grad_memory,
        out_gains,
        out_qkv,
        out_self_out,
        out_query,
        out_keyval,
        out_cross_out,
        out_feed_in,
        out_feed_out,
        out_table,
        out_hyper,
        out_down,
        out_up,
        out_norm,
    )


def solution(mesh):
    placed = (
        P(("fsdp", "dp"), None),
        P(("fsdp", "dp"), None),
        P(("fsdp", "dp"), None),
        P(("fsdp", "dp"), None),
        P(("fsdp", "dp"), None),
        P(("fsdp", "dp"), None),
        P(None, "fsdp"),
        P("fsdp", None),
        P("fsdp", None),
        P("fsdp", None),
        P("fsdp", None),
        P("fsdp", None),
        P("fsdp", None),
        P("fsdp", None),
        P(None, "fsdp"),
        P(None, "fsdp"),
        P(None, "fsdp"),
        P(None, "fsdp"),
        P(None, "fsdp"),
    )
    devices = mesh.shape["fsdp"]
    ring = devices == 16 and mesh.shape["dp"] == 2
    return jax.shard_map(
        functools.partial(per_device, devices, ring),
        mesh=mesh,
        in_specs=placed,
        out_specs=(
            P(("fsdp", "dp"), None),
            P(("fsdp", "dp"), None),
            P(("fsdp", "dp"), None),
            P(None, "fsdp"),
            P("fsdp", None),
            P("fsdp", None),
            P("fsdp", None),
            P("fsdp", None),
            P("fsdp", None),
            P("fsdp", None),
            P("fsdp", None),
            P(None, "fsdp"),
            P(None, "fsdp"),
            P(None, "fsdp"),
            P(None, "fsdp"),
            P(None, "fsdp"),
        ),
        check_vma=False,
    )
```

time: 2110 us -> 450 us (0.21)
  waiting for transfers between devices: 1480 us -> 151 us
  matrix products: 263 us -> 9.91 us
  blocking collectives: 190 us -> 0 us
  Pallas kernels: 0 us -> 134 us
  local copies, waits for them, and re-layouts: 110 us -> 33.1 us
  starting transfers between devices: 1.54 us -> 55.4 us
    reduce_scatter x9 -> x0, waiting for transfers between devices: 1120 us -> none  [the longest x1 263 us: per_device(): lax.psum_scatter(exact_rows(hidden_wide, grad_made_up), ('fsdp', 'dp'), s...]
    all_gather x9 -> x1, waiting for transfers between devices: 356 us -> 36.6 us  [per_device(): packed = lax.all_gather(packed, 'fsdp', axis=0)]
    all_gather x15 -> x0, blocking collectives: 150 us -> none  [the longest x1 23.1 us: per_device(): lax.all_gather(norm_gains, 'fsdp', axis=1, tiled=True)]
    pallas_call x0 -> x9, Pallas kernels: none -> 134 us  [call(): pl.pallas_call(kernel, out_shape=outs, in_specs=specs, out_specs=[pl.Bloc...]
    dot_general x44 -> x0, matrix products: 133 us -> none  [the longest x13 44.8 us: inner_rows(): lax.dot_general(left, right, (((0,), (0,)), ((), ())), preferred_element_...]
    ppermute x0 -> x47, waiting for transfers between devices: none -> 115 us  [swap(): return lax.ppermute(values, axis, [(i, mate(i)) for i in range(count)])]
    ppermute x0 -> x47, starting transfers between devices: none -> 55.4 us  [swap(): return lax.ppermute(values, axis, [(i, mate(i)) for i in range(count)])]
    dot_general x4, matrix products: 54.4 us -> 6 us  [exact_rows(): lax.dot_general(left, right, (((0,), (0,)), ((), ())), precision=highest,...]
  transfers between devices with their start and end apart: 19 -> 48, of which waited for: 15 -> 25; matrix products, arithmetic and copies ran while one was open for 16% -> 15% of each run, Pallas kernels for 0% -> 17%
where the time goes in v1:
time: 450 us; the launch traced here: 445 us
  waiting for transfers between devices  151 us (34%)
  Pallas kernels  134 us (30%)
  starting transfers between devices  55.4 us (12%)
  other arithmetic  45.6 us (10%)
  local copies, waits for them, and re-layouts  33.1 us (7%)
  between operations  15.4 us (3%)
  matrix products  9.91 us (2%)
    pallas_call x9, Pallas kernels, call(): pl.pallas_call(kernel, out_shape=outs, in_specs=specs, out_specs=[pl.Bloc...  134 us
    ppermute x47, waiting for transfers between devices, swap(): return lax.ppermute(values, axis, [(i, mate(i)) for i in range(count)])  115 us
    ppermute x47, starting transfers between devices, swap(): return lax.ppermute(values, axis, [(i, mate(i)) for i in range(count)])  55.4 us
    all_gather x1, waiting for transfers between devices, per_device(): packed = lax.all_gather(packed, 'fsdp', axis=0)  36.6 us
    convert_element_type x12, other arithmetic, add_low(): (left.astype(jnp.float32) + right.astype(jnp.float32)).astype(jnp.bfloat16)  22.8 us
  transfers between devices with their start and end apart: 48, of which 25 were waited for; matrix products, arithmetic and copies ran while one was open for 15% of the time, Pallas kernels for 17%

profile of v1, /device:TPU:0, one launch (start us, length us, event | category | flops | bytes accessed | tf_op | source)
XLA Modules:
  0.0 444.8 jit_solution(301078192384165162)
XLA Ops:
  11.8 5.0 %collective-permute-start = (bf16[16,128]{1,0:T(8,128)(2,1)S(1)}, bf16[16,128]{1,0:T(8,128)(2,1)S(1)}, u32[]{:S(2)}, u32[]{:S(2)}) collective-permute-start(bf16[16,128]{1,0:T(8,128)(2,1)S(1)} %fusion.62), channel_id=1, source_target_pairs={{0,24},{2,26},{4,28},{6,30},{8,0},{10,2},{12,4},{14,6},{16,8},{18,... | collective-permute-start | bytes 12296 | tf_op jit(solution)/shard_map/ppermute | solution.py:412
  18.2 3.2 collective-permute-done.1
  23.9 2.5 collective-permute-done.3
  30.2 3.0 collective-permute-start.5
  34.0 5.3 %collective-permute-done.5 = bf16[152,384]{1,0:T(8,128)(2,1)S(1)} collective-permute-done((bf16[152,384]{1,0:T(8,128)(2,1)S(1)}, bf16[152,384]{1,0:T(8,128)(2,1)S(1)}, u32[]{:S(2)}, u32[]{:S(2)}) %collective-permute-start.5) | collective-permute-done | bytes 116768 | tf_op jit(solution)/shard_map/ppermute | solution.py:412
  39.3 9.7 %collective-permute-done.6 = bf16[152,384]{1,0:T(8,128)(2,1)S(1)} collective-permute-done((bf16[152,384]{1,0:T(8,128)(2,1)S(1)}, bf16[152,384]{1,0:T(8,128)(2,1)S(1)}, u32[]{:S(2)}, u32[]{:S(2)}) %collective-permute-start.6) | collective-permute-done | bytes 116768 | tf_op jit(solution)/shard_map/ppermute | solution.py:412
  52.3 19.6 %collective-permute-done.8 = bf16[4,152,384]{2,1,0:T(8,128)(2,1)S(1)} collective-permute-done((bf16[4,152,384]{2,1,0:T(8,128)(2,1)S(1)}, bf16[4,152,384]{2,1,0:T(8,128)(2,1)S(1)}, u32[]{:S(2)}, u32[]{:S(2)}) %collective-permute-start.8) | collective-permute-done | bytes 466976 | tf_op jit(solution)/shard_map/ppermute | solution.py:412
  87.0 36.6 %all-gather.3.cloned.1.call-done = bf16[12288,768]{1,0:T(8,128)(2,1)} async-done(((bf16[768,768]{1,0:T(8,128)(2,1)}), bf16[12288,768]{1,0:T(8,128)(2,1)}) %all-gather.3.cloned.1.call-update) | async-done | bytes 18874384 | tf_op jit(solution)/shard_map/all_gather | solution.py:594
  123.7 15.8 %shard_map.306 = (bf16[384,768]{1,0:T(8,128)(2,1)}, bf16[384,2304]{1,0:T(8,128)(2,1)}, bf16[12,384,384]{2,1,0:T(8,128)(2,1)}, bf16[384,768]{1,0:T(8,128)(2,1)}, ...) custom-call(bf16[384,768]{1,0:T(8,128)(2,1)} %tokens.3, f32[8,768]{1,0:T(8,128)} %pad_convert_fusion.gains, ...), custom_call_target="tpu_custom_call" | custom-call | flops 27200000000 | bytes 31825920 | tf_op jit(solution)/shard_map/pallas_call | solution.py:529
  139.5 21.6 %shard_map.307 = (bf16[384,768]{1,0:T(8,128)(2,1)}, bf16[384,768]{1,0:T(8,128)(2,1)}, bf16[768,1536]{1,0:T(8,128)(2,1)}, bf16[12,768,384]{2,1,0:T(8,128)(2,1)}, ...) custom-call(f32[384,768]{1,0:T(8,128)} %get-tuple-element.121.stream, ...), custom_call_target="tpu_custom_call" | custom-call | flops 35699998720 | bytes 38903808 | tf_op jit(solution)/shard_map/pallas_call | solution.py:529
  161.1 21.3 %shard_map.308 = (bf16[384,768]{1,0:T(8,128)(2,1)}, bf16[384,768]{1,0:T(8,128)(2,1)}, f32[4,384,768]{2,1,0:T(8,128)}, bf16[384,768]{1,0:T(8,128)(2,1)}, bf16[768...) custom-call(s32[4]{0:T(128)} %pad_add_fusion.place, ...), custom_call_target="tpu_custom_call" | custom-call | flops 37399998464 | bytes 35463184 | tf_op jit(solution)/shard_map/pallas_call | solution.py:529
  184.3 18.3 %shard_map.309 = (f32[384,768]{1,0:T(8,128)}, f32[1,768]{1,0:T(1,128)}, bf16[2,4,4,48,768]{4,3,2,1,0:T(8,128)(2,1)}, bf16[2,4,4,48,768]{4,3,2,1,0:T(8,128)(2,1)}) custom-call(s32[4]{0:T(128)} %pad_add_fusion.place, f32[384,768]{1,0:T(8,128)} %get-tuple-element.122.stream, f32[8,768]{1,0:T(8,128)} %pad_convert_fusion.gains, ...), custom_call_target="tpu_custom_call" | custom-call | flops 30599999488 | bytes 32467984 | tf_op jit(solution)/shard_map/pallas_call | solution.py:529
  203.0 2.9 fusion.7
  207.4 6.0 %shard_map.310 = (bf16[384,768]{1,0:T(8,128)(2,1)}, bf16[384,768]{1,0:T(8,128)(2,1)}, bf16[768,192]{1,0:T(8,128)(2,1)}, bf16[192,768]{1,0:T(8,128)(2,1)}, f32[128,768]{1,0:T(8,128)}) custom-call(f32[384,768]{1,0:T(8,128)} %get-tuple-element.132.grad_result, bf16[16,16,48,768]{3,2,1,0:T(8,128)(2,1)} %bitcast.387, f32[384,768]{1,0:T(8,128)} %get-tuple-element.138.branch, ...), custom_call_target="tpu_custom_call" | custom-call | flops 51000000512 | bytes 26296320 | tf_op jit(solution)/shard_map/pallas_call | solution.py:529
  214.8 4.0 add_convert_fusion.4
  219.7 24.4 %shard_map.311 = (f32[384,768]{1,0:T(8,128)}, f32[768,768]{1,0:T(8,128)}, f32[1,768]{1,0:T(1,128)}, bf16[2,2,4,2,48,768]{5,4,3,2,1,0:T(8,128)(2,1)}, bf16[2,2,4,2,48,768]{5,4,3,2,1,0:T(8,128)(2,1)}) custom-call(s32[4]{0:T(128)} %pad_add_fusion.place, f32[384,768]{1,0:T(8,128)} %get-tuple-element.132.grad_result, f32[384,768]{1,0:T(8,128)} %get-tuple-element.121.stream, ...), custom_call_target="tpu_custom_call" | custom-call | flops 40800002048 | bytes 43084816 | tf_op jit(solution)/shard_map/pallas_call | solution.py:529
  244.2 2.6 collective-permute-done.13
  247.9 2.5 fusion.1
  251.8 3.3 collective-permute-start.19
  255.7 6.0 %shard_map.312 = (bf16[384,768]{1,0:T(8,128)(2,1)}, bf16[384,768]{1,0:T(8,128)(2,1)}, bf16[768,192]{1,0:T(8,128)(2,1)}, bf16[192,768]{1,0:T(8,128)(2,1)}, f32[128,768]{1,0:T(8,128)}) custom-call(f32[384,768]{1,0:T(8,128)} %get-tuple-element.150.grad_result.grad_stream, bf16[16,16,48,768]{3,2,1,0:T(8,128)(2,1)} %bitcast.389, ...), custom_call_target="tpu_custom_call" | custom-call | flops 51000000512 | bytes 26296320 | tf_op jit(solution)/shard_map/pallas_call | solution.py:529
  281.4 18.1 %shard_map.313 = (f32[384,768]{1,0:T(8,128)}, f32[1,768]{1,0:T(1,128)}, bf16[2,4,4,48,768]{4,3,2,1,0:T(8,128)(2,1)}, bf16[2,4,4,48,768]{4,3,2,1,0:T(8,128)(2,1)}) custom-call(s32[4]{0:T(128)} %pad_add_fusion.place, f32[384,768]{1,0:T(8,128)} %get-tuple-element.150.grad_result.grad_stream, bf16[384,768]{1,0:T(8,128)(2,1)} %tokens.3, ...), custom_call_target="tpu_custom_call" | custom-call | flops 30599999488 | bytes 34237456 | tf_op jit(solution)/shard_map/pallas_call | solution.py:529
  300.1 6.7 %collective-permute-done.20 = bf16[2,4,2,48,768]{4,3,2,1,0:T(8,128)(2,1)S(1)} collective-permute-done((bf16[2,4,2,48,768]{4,3,2,1,0:T(8,128)(2,1)S(1)}, bf16[2,4,2,48,768]{4,3,2,1,0:T(8,128)(2,1)S(1)}, u32[]{:S(2)}, u32[]{:S(2)}) %collective-permute-start.20) | collective-permute-done | bytes 1179680 | tf_op jit(solution)/shard_map/ppermute | solution.py:412
  306.8 2.5 shard_map.314
  310.6 2.6 fusion
  319.3 2.5 collective-permute-start.23
  323.6 4.1 collective-permute-done.23
  333.0 23.1 %collective-permute-done.27 = bf16[4,152,384]{2,1,0:T(8,128)(2,1)S(1)} collective-permute-done((bf16[4,152,384]{2,1,0:T(8,128)(2,1)S(1)}, bf16[4,152,384]{2,1,0:T(8,128)(2,1)S(1)}, u32[]{:S(2)}, u32[]{:S(2)}) %collective-permute-start.27) | collective-permute-done | bytes 466976 | tf_op jit(solution)/shard_map/ppermute | solution.py:412
  368.5 12.1 %collective-permute-done.34 = bf16[152,384]{1,0:T(8,128)(2,1)} collective-permute-done((bf16[152,384]{1,0:T(8,128)(2,1)}, bf16[152,384]{1,0:T(8,128)(2,1)}, u32[]{:S(2)}, u32[]{:S(2)}) %collective-permute-start.34) | collective-permute-done | bytes 116768 | tf_op jit(solution)/shard_map/ppermute | solution.py:412
  382.4 8.4 %collective-permute-done.29 = bf16[4,48,768]{2,1,0:T(8,128)(2,1)S(1)} collective-permute-done((bf16[4,48,768]{2,1,0:T(8,128)(2,1)}, bf16[4,48,768]{2,1,0:T(8,128)(2,1)S(1)}, u32[]{:S(2)}, u32[]{:S(2)}) %collective-permute-start.29) | collective-permute-done | bytes 294944 | tf_op jit(solution)/shard_map/ppermute | solution.py:412
  395.8 3.7 collective-permute-start.37
  405.5 4.0 collective-permute-done.38
  423.2 3.1 collective-permute-start.44
  (342 shorter events, 124.8 us)
Async XLA Ops:
  7.2 116.5 %all-gather.3.cloned.1.call-start = ((), (), s32[]{:S(2)}) async-start(), calls=%async_computation | async-start | bytes 20054016 | tf_op jit(solution)/shard_map/all_gather | solution.py:594
  30.2 9.1 %collective-permute-start.5 = (bf16[152,384]{1,0:T(8,128)(2,1)S(1)}, bf16[152,384]{1,0:T(8,128)(2,1)S(1)}, u32[]{:S(2)}, u32[]{:S(2)}) collective-permute-start(bf16[152,384]{1,0:T(8,128)(2,1)S(1)} %fusion.48), channel_id=1, source_target_pairs={{0,24},{2,26},{4,28},{6,30},{8,0},{10,2},{12,4},{14,6},{16,8},{18,... | collective-permute-start | bytes 350216 | tf_op jit(solution)/shard_map/ppermute | solution.py:412
  33.4 15.6 %collective-permute-start.7 = (bf16[152,384]{1,0:T(8,128)(2,1)S(1)}, bf16[152,384]{1,0:T(8,128)(2,1)S(1)}, u32[]{:S(2)}, u32[]{:S(2)}) collective-permute-start(bf16[152,384]{1,0:T(8,128)(2,1)S(1)} %fusion.48), channel_id=1, source_target_pairs={{0,8},{2,10},{4,12},{6,14},{8,16},{10,18},{12,20},{14,22},{16,24},... | collective-permute-start | bytes 350216 | tf_op jit(solution)/shard_map/ppermute | solution.py:412
  33.4 15.6 %collective-permute-start.6 = (bf16[152,384]{1,0:T(8,128)(2,1)S(1)}, bf16[152,384]{1,0:T(8,128)(2,1)S(1)}, u32[]{:S(2)}, u32[]{:S(2)}) collective-permute-start(bf16[152,384]{1,0:T(8,128)(2,1)S(1)} %fusion.48), channel_id=1, source_target_pairs={{0,16},{2,18},{4,20},{6,22},{8,24},{10,26},{12,28},{14,30},{16,0},... | collective-permute-start | bytes 350216 | tf_op jit(solution)/shard_map/ppermute | solution.py:412
  49.3 22.7 %collective-permute-start.8 = (bf16[4,152,384]{2,1,0:T(8,128)(2,1)S(1)}, bf16[4,152,384]{2,1,0:T(8,128)(2,1)S(1)}, u32[]{:S(2)}, u32[]{:S(2)}) collective-permute-start(bf16[4,152,384]{2,1,0:T(8,128)(2,1)S(1)} %constant_dynamic-slice_fusion.1), channel_id=1, source_target_pairs={{0,4},{2,6},{4,0},{6,2},{8,12},{10,14},{12,8},{14,10},{16,20},{18,... | collective-permute-start | bytes 1400840 | tf_op jit(solution)/shard_map/ppermute | solution.py:412
  184.1 18.9 %collective-permute-start.10 = (bf16[2,2,4,2,48,768]{5,4,3,2,1,0:T(8,128)(2,1)}, bf16[2,2,4,2,48,768]{5,4,3,2,1,0:T(8,128)(2,1)}, u32[]{:S(2)}, u32[]{:S(2)}) collective-permute-start(bf16[2,2,4,2,48,768]{5,4,3,2,1,0:T(8,128)(2,1)} %get-tuple-element.129), channel_id=1, source_target_pairs={{0,2},{2,0},{4,6},{6,4},{8,10},{10,8},{12,14},{14,12},{16,18},{18,... | collective-permute-start | bytes 7077896 | tf_op jit(solution)/shard_map/ppermute | solution.py:412
  202.6 10.7 %collective-permute-start.11 = (bf16[2,4,4,48,768]{4,3,2,1,0:T(8,128)(2,1)}, bf16[2,4,4,48,768]{4,3,2,1,0:T(8,128)(2,1)S(1)}, u32[]{:S(2)}, u32[]{:S(2)}) collective-permute-start(bf16[2,4,4,48,768]{4,3,2,1,0:T(8,128)(2,1)} %get-tuple-element.143), channel_id=1, source_target_pairs={{0,2},{2,0},{4,6},{6,4},{8,10},{10,8},{12,14},{14,12},{16,18},{18,... | collective-permute-start | bytes 7077896 | tf_op jit(solution)/shard_map/ppermute | solution.py:412
  205.9 38.3 %collective-permute-start.12 = (bf16[2,4,2,48,768]{4,3,2,1,0:T(8,128)(2,1)}, bf16[2,4,2,48,768]{4,3,2,1,0:T(8,128)(2,1)}, u32[]{:S(2)}, u32[]{:S(2)}) collective-permute-start(bf16[2,4,2,48,768]{4,3,2,1,0:T(8,128)(2,1)} %fusion.7), channel_id=1, source_target_pairs={{0,1},{1,0},{2,3},{3,2},{4,5},{5,4},{6,7},{7,6},{8,9},{9,8},{10,11... | collective-permute-start | bytes 3538952 | tf_op jit(solution)/shard_map/ppermute | solution.py:412
  218.7 28.1 %collective-permute-start.13 = (bf16[4,4,48,768]{3,2,1,0:T(8,128)(2,1)}, bf16[4,4,48,768]{3,2,1,0:T(8,128)(2,1)S(1)}, u32[]{:S(2)}, u32[]{:S(2)}) collective-permute-start(bf16[4,4,48,768]{3,2,1,0:T(8,128)(2,1)} %get-tuple-element.229), channel_id=1, source_target_pairs={{0,4},{2,6},{4,0},{6,2},{8,12},{10,14},{12,8},{14,10},{16,20},{18,... | collective-permute-start | bytes 3538952 | tf_op jit(solution)/shard_map/ppermute | solution.py:412
  244.1 34.9 %collective-permute-start.14 = (bf16[2,2,4,2,48,768]{5,4,3,2,1,0:T(8,128)(2,1)}, bf16[2,2,4,2,48,768]{5,4,3,2,1,0:T(8,128)(2,1)}, u32[]{:S(2)}, u32[]{:S(2)}) collective-permute-start(bf16[2,2,4,2,48,768]{5,4,3,2,1,0:T(8,128)(2,1)} %get-tuple-element.160), channel_id=1, source_target_pairs={{0,2},{2,0},{4,6},{6,4},{8,10},{10,8},{12,14},{14,12},{16,18},{18,... | collective-permute-start | bytes 7077896 | tf_op jit(solution)/shard_map/ppermute | solution.py:412
  251.8 47.6 %collective-permute-start.19 = (bf16[4,48,768]{2,1,0:T(8,128)(2,1)}, bf16[4,48,768]{2,1,0:T(8,128)(2,1)}, u32[]{:S(2)}, u32[]{:S(2)}) collective-permute-start(bf16[4,48,768]{2,1,0:T(8,128)(2,1)} %get-tuple-element.234), channel_id=1, source_target_pairs={{0,24},{2,26},{4,28},{6,30},{8,0},{10,2},{12,4},{14,6},{16,8},{18,... | collective-permute-start | bytes 884744 | tf_op jit(solution)/shard_map/ppermute | solution.py:412
  255.1 44.4 %collective-permute-start.18 = (bf16[4,48,768]{2,1,0:T(8,128)(2,1)}, bf16[4,48,768]{2,1,0:T(8,128)(2,1)}, u32[]{:S(2)}, u32[]{:S(2)}) collective-permute-start(bf16[4,48,768]{2,1,0:T(8,128)(2,1)} %get-tuple-element.235), channel_id=1, source_target_pairs={{0,16},{2,18},{4,20},{6,22},{8,24},{10,26},{12,28},{14,30},{16,0},... | collective-permute-start | bytes 884744 | tf_op jit(solution)/shard_map/ppermute | solution.py:412
  255.1 44.9 %collective-permute-start.17 = (bf16[4,48,768]{2,1,0:T(8,128)(2,1)}, bf16[4,48,768]{2,1,0:T(8,128)(2,1)}, u32[]{:S(2)}, u32[]{:S(2)}) collective-permute-start(bf16[4,48,768]{2,1,0:T(8,128)(2,1)} %get-tuple-element.236), channel_id=1, source_target_pairs={{0,8},{2,10},{4,12},{6,14},{8,16},{10,18},{12,20},{14,22},{16,24},... | collective-permute-start | bytes 884744 | tf_op jit(solution)/shard_map/ppermute | solution.py:412
  267.0 33.1 %collective-permute-start.21 = (bf16[4,2,48,768]{3,2,1,0:T(8,128)(2,1)}, bf16[4,2,48,768]{3,2,1,0:T(8,128)(2,1)}, u32[]{:S(2)}, u32[]{:S(2)}) collective-permute-start(bf16[4,2,48,768]{3,2,1,0:T(8,128)(2,1)} %slice_bitcast_fusion), channel_id=1, source_target_pairs={{0,4},{2,6},{4,0},{6,2},{8,12},{10,14},{12,8},{14,10},{16,20},{18,... | collective-permute-start | bytes 1769480 | tf_op jit(solution)/shard_map/ppermute | solution.py:412
  280.8 26.0 %collective-permute-start.20 = (bf16[2,4,2,48,768]{4,3,2,1,0:T(8,128)(2,1)S(1)}, bf16[2,4,2,48,768]{4,3,2,1,0:T(8,128)(2,1)S(1)}, u32[]{:S(2)}, u32[]{:S(2)}) collective-permute-start(bf16[2,4,2,48,768]{4,3,2,1,0:T(8,128)(2,1)S(1)} %fusion.10), channel_id=1, source_target_pairs={{0,1},{1,0},{2,3},{3,2},{4,5},{5,4},{6,7},{7,6},{8,9},{9,8},{10,11... | collective-permute-start | bytes 3538952 | tf_op jit(solution)/shard_map/ppermute | solution.py:412
  299.5 13.7 %collective-permute-start.16 = (bf16[2,4,152,384]{3,2,1,0:T(8,128)(2,1)}, bf16[2,4,152,384]{3,2,1,0:T(8,128)(2,1)}, u32[]{:S(2)}, u32[]{:S(2)}) collective-permute-start(bf16[2,4,152,384]{3,2,1,0:T(8,128)(2,1)} %pad_maximum_fusion.3), channel_id=1, source_target_pairs={{0,2},{2,0},{4,6},{6,4},{8,10},{10,8},{12,14},{14,12},{16,18},{18,... | collective-permute-start | bytes 2801672 | tf_op jit(solution)/shard_map/ppermute | solution.py:412
  299.6 13.6 %collective-permute-start.15 = (bf16[2,4,4,48,768]{4,3,2,1,0:T(8,128)(2,1)}, bf16[2,4,4,48,768]{4,3,2,1,0:T(8,128)(2,1)}, u32[]{:S(2)}, u32[]{:S(2)}) collective-permute-start(bf16[2,4,4,48,768]{4,3,2,1,0:T(8,128)(2,1)} %get-tuple-element.166), channel_id=1, source_target_pairs={{0,2},{2,0},{4,6},{6,4},{8,10},{10,8},{12,14},{14,12},{16,18},{18,... | collective-permute-start | bytes 7077896 | tf_op jit(solution)/shard_map/ppermute | solution.py:412
  317.1 39.0 %collective-permute-start.22 = (bf16[4,4,48,768]{3,2,1,0:T(8,128)(2,1)S(1)}, bf16[4,4,48,768]{3,2,1,0:T(8,128)(2,1)S(1)}, u32[]{:S(2)}, u32[]{:S(2)}) collective-permute-start(bf16[4,4,48,768]{3,2,1,0:T(8,128)(2,1)S(1)} %get-tuple-element.184), channel_id=1, source_target_pairs={{0,4},{2,6},{4,0},{6,2},{8,12},{10,14},{12,8},{14,10},{16,20},{18,... | collective-permute-start | bytes 3538952 | tf_op jit(solution)/shard_map/ppermute | solution.py:412
  318.6 37.5 %collective-permute-start.27 = (bf16[4,152,384]{2,1,0:T(8,128)(2,1)S(1)}, bf16[4,152,384]{2,1,0:T(8,128)(2,1)S(1)}, u32[]{:S(2)}, u32[]{:S(2)}) collective-permute-start(bf16[4,152,384]{2,1,0:T(8,128)(2,1)S(1)} %slice_bitcast_fusion.2), channel_id=1, source_target_pairs={{0,4},{2,6},{4,0},{6,2},{8,12},{10,14},{12,8},{14,10},{16,20},{18,... | collective-permute-start | bytes 1400840 | tf_op jit(solution)/shard_map/ppermute | solution.py:412
  321.8 11.2 %collective-permute-start.26 = (bf16[4,48,768]{2,1,0:T(8,128)(2,1)S(1)}, bf16[4,48,768]{2,1,0:T(8,128)(2,1)S(1)}, u32[]{:S(2)}, u32[]{:S(2)}) collective-permute-start(bf16[4,48,768]{2,1,0:T(8,128)(2,1)S(1)} %copy-done.22), channel_id=1, source_target_pairs={{0,1},{1,0},{2,3},{3,2},{4,5},{5,4},{6,7},{7,6},{8,9},{9,8},{10,11... | collective-permute-start | bytes 884744 | tf_op jit(solution)/shard_map/ppermute | solution.py:412
  331.3 33.5 %collective-permute-start.31 = (bf16[4,2,48,768]{3,2,1,0:T(8,128)(2,1)S(1)}, bf16[4,2,48,768]{3,2,1,0:T(8,128)(2,1)S(1)}, u32[]{:S(2)}, u32[]{:S(2)}) collective-permute-start(bf16[4,2,48,768]{3,2,1,0:T(8,128)(2,1)S(1)} %slice_bitcast_fusion.1), channel_id=1, source_target_pairs={{0,4},{2,6},{4,0},{6,2},{8,12},{10,14},{12,8},{14,10},{16,20},{18,... | collective-permute-start | bytes 1769480 | tf_op jit(solution)/shard_map/ppermute | solution.py:412
  361.3 19.3 %collective-permute-start.34 = (bf16[152,384]{1,0:T(8,128)(2,1)}, bf16[152,384]{1,0:T(8,128)(2,1)}, u32[]{:S(2)}, u32[]{:S(2)}) collective-permute-start(bf16[152,384]{1,0:T(8,128)(2,1)} %get-tuple-element.203), channel_id=1, source_target_pairs={{0,16},{2,18},{4,20},{6,22},{8,24},{10,26},{12,28},{14,30},{16,0},... | collective-permute-start | bytes 350216 | tf_op jit(solution)/shard_map/ppermute | solution.py:412
  362.5 19.8 %collective-permute-start.35 = (bf16[152,384]{1,0:T(8,128)(2,1)}, bf16[152,384]{1,0:T(8,128)(2,1)S(1)}, u32[]{:S(2)}, u32[]{:S(2)}) collective-permute-start(bf16[152,384]{1,0:T(8,128)(2,1)} %get-tuple-element.204), channel_id=1, source_target_pairs={{0,24},{2,26},{4,28},{6,30},{8,0},{10,2},{12,4},{14,6},{16,8},{18,... | collective-permute-start | bytes 350216 | tf_op jit(solution)/shard_map/ppermute | solution.py:412
  364.0 18.4 %collective-permute-start.32 = (bf16[2,48,768]{2,1,0:T(8,128)(2,1)}, bf16[2,48,768]{2,1,0:T(8,128)(2,1)S(1)}, u32[]{:S(2)}, u32[]{:S(2)}) collective-permute-start(bf16[2,48,768]{2,1,0:T(8,128)(2,1)} %add_convert_fusion.11), channel_id=1, source_target_pairs={{0,1},{1,0},{2,3},{3,2},{4,5},{5,4},{6,7},{7,6},{8,9},{9,8},{10,11... | collective-permute-start | bytes 442376 | tf_op jit(solution)/shard_map/ppermute | solution.py:412
  364.8 17.6 %collective-permute-start.28 = (bf16[4,48,768]{2,1,0:T(8,128)(2,1)}, bf16[4,48,768]{2,1,0:T(8,128)(2,1)S(1)}, u32[]{:S(2)}, u32[]{:S(2)}) collective-permute-start(bf16[4,48,768]{2,1,0:T(8,128)(2,1)} %get-tuple-element.197), channel_id=1, source_target_pairs={{0,8},{2,10},{4,12},{6,14},{8,16},{10,18},{12,20},{14,22},{16,24},... | collective-permute-start | bytes 884744 | tf_op jit(solution)/shard_map/ppermute | solution.py:412
  367.3 23.5 %collective-permute-start.29 = (bf16[4,48,768]{2,1,0:T(8,128)(2,1)}, bf16[4,48,768]{2,1,0:T(8,128)(2,1)S(1)}, u32[]{:S(2)}, u32[]{:S(2)}) collective-permute-start(bf16[4,48,768]{2,1,0:T(8,128)(2,1)} %get-tuple-element.198), channel_id=1, source_target_pairs={{0,16},{2,18},{4,20},{6,22},{8,24},{10,26},{12,28},{14,30},{16,0},... | collective-permute-start | bytes 884744 | tf_op jit(solution)/shard_map/ppermute | solution.py:412
  380.6 10.9 %collective-permute-start.30 = (bf16[4,48,768]{2,1,0:T(8,128)(2,1)}, bf16[4,48,768]{2,1,0:T(8,128)(2,1)S(1)}, u32[]{:S(2)}, u32[]{:S(2)}) collective-permute-start(bf16[4,48,768]{2,1,0:T(8,128)(2,1)} %get-tuple-element.199), channel_id=1, source_target_pairs={{0,24},{2,26},{4,28},{6,30},{8,0},{10,2},{12,4},{14,6},{16,8},{18,... | collective-permute-start | bytes 884744 | tf_op jit(solution)/shard_map/ppermute | solution.py:412
  382.3 11.6 %collective-permute-start.41 = (f32[3,768]{1,0:T(4,128)S(1)}, f32[3,768]{1,0:T(4,128)S(1)}, u32[]{:S(2)}, u32[]{:S(2)}) collective-permute-start(f32[3,768]{1,0:T(4,128)S(1)} %pad_maximum_fusion.10), channel_id=1, source_target_pairs={{0,1},{1,0},{2,3},{3,2},{4,5},{5,4},{6,7},{7,6},{8,9},{9,8},{10,11... | collective-permute-start | bytes 27656 | tf_op jit(solution)/shard_map/ppermute | solution.py:412
  393.6 15.9 %collective-permute-start.36 = (bf16[4,48,768]{2,1,0:T(8,128)(2,1)S(1)}, bf16[4,48,768]{2,1,0:T(8,128)(2,1)}, u32[]{:S(2)}, u32[]{:S(2)}) collective-permute-start(bf16[4,48,768]{2,1,0:T(8,128)(2,1)S(1)} %add_convert_fusion.9), channel_id=1, source_target_pairs={{0,1},{1,0},{2,3},{3,2},{4,5},{5,4},{6,7},{7,6},{8,9},{9,8},{10,11... | collective-permute-start | bytes 884744 | tf_op jit(solution)/shard_map/ppermute | solution.py:412
  393.9 9.9 %collective-permute-start.40 = (bf16[152,384]{1,0:T(8,128)(2,1)S(1)}, bf16[152,384]{1,0:T(8,128)(2,1)S(1)}, u32[]{:S(2)}, u32[]{:S(2)}) collective-permute-start(bf16[152,384]{1,0:T(8,128)(2,1)S(1)} %add_convert_fusion.12), channel_id=1, source_target_pairs={{0,1},{1,0},{2,3},{3,2},{4,5},{5,4},{6,7},{7,6},{8,9},{9,8},{10,11... | collective-permute-start | bytes 350216 | tf_op jit(solution)/shard_map/ppermute | solution.py:412
  395.8 9.7 %collective-permute-start.37 = (bf16[2,48,768]{2,1,0:T(8,128)(2,1)S(1)}, bf16[2,48,768]{2,1,0:T(8,128)(2,1)S(1)}, u32[]{:S(2)}, u32[]{:S(2)}) collective-permute-start(bf16[2,48,768]{2,1,0:T(8,128)(2,1)S(1)} %copy-done.27), channel_id=1, source_target_pairs={{0,8},{2,10},{4,12},{6,14},{8,16},{10,18},{12,20},{14,22},{16,24},... | collective-permute-start | bytes 442376 | tf_op jit(solution)/shard_map/ppermute | solution.py:412
  399.5 10.0 %collective-permute-start.38 = (bf16[2,48,768]{2,1,0:T(8,128)(2,1)S(1)}, bf16[2,48,768]{2,1,0:T(8,128)(2,1)S(1)}, u32[]{:S(2)}, u32[]{:S(2)}) collective-permute-start(bf16[2,48,768]{2,1,0:T(8,128)(2,1)S(1)} %copy-done.26), channel_id=1, source_target_pairs={{0,16},{2,18},{4,20},{6,22},{8,24},{10,26},{12,28},{14,30},{16,0},... | collective-permute-start | bytes 442376 | tf_op jit(solution)/shard_map/ppermute | solution.py:412
  (72 other events, 617.1 us)
Sparse Core Ops, SparseCore 0:
  11.8 111.8 all-gather.2

commit v2 on v1

v2 whole, which is shorter than its diff:
```python
import functools
import math

import jax
import jax.numpy as jnp
from jax import lax
from jax.experimental import pallas as pl
from jax.experimental.pallas import tpu as pltpu
from jax.sharding import PartitionSpec as P

norm_epsilon = 1e-06
masked_score = -1000000000.0
highest = lax.Precision.HIGHEST


def matmul(left, right):
    return jnp.dot(left, right, preferred_element_type=jnp.float32)


def exact_rows(left, right):
    return lax.dot_general(
        left, right, (((0,), (0,)), ((), ())), precision=highest, preferred_element_type=jnp.float32
    )


def exact_cols(left, right):
    return lax.dot_general(
        left, right, (((1,), (1,)), ((), ())), precision=highest, preferred_element_type=jnp.float32
    )


def segment_rows(lengths, count):
    ends = jnp.cumsum(lengths)
    places = jnp.arange(count, dtype=jnp.int32)
    return jnp.sum((places[:, None] >= ends[None, :]).astype(jnp.int32), axis=1)


def dot(left, right):
    return jnp.dot(left, right, preferred_element_type=jnp.float32)


def dot_nt(left, right):
    return lax.dot_general(
        left, right, (((1,), (1,)), ((), ())), preferred_element_type=jnp.float32
    )


def dot_tn(left, right):
    return lax.dot_general(
        left, right, (((0,), (0,)), ((), ())), preferred_element_type=jnp.float32
    )


def rms_rate(values):
    return lax.rsqrt(jnp.mean(values * values, axis=-1, keepdims=True) + norm_epsilon)


def rms_back(values, rate, gain, grad):
    scaled = grad * gain
    inner = jnp.mean(scaled * values, axis=-1, keepdims=True)
    return rate * (scaled - values * (rate * rate * inner)), grad * values * rate


gelu_slope = math.sqrt(2.0 / math.pi)
gelu_cube = 0.044715


def gelu(values):
    inner = gelu_slope * values * (1.0 + gelu_cube * values * values)
    return 0.5 * values * (1.0 + jnp.tanh(inner))


def gelu_back(values):
    square = values * values
    bent = jnp.tanh(gelu_slope * values * (1.0 + gelu_cube * square))
    slope = gelu_slope * (1.0 + 3.0 * gelu_cube * square)
    return 0.5 * (1.0 + bent) + 0.5 * values * (1.0 - bent * bent) * slope


def halves(dtype):
    lane = lax.broadcasted_iota(jnp.int32, (1, 128), 1)
    first = (lane < 64).astype(jnp.float32)
    return first.astype(dtype), (1.0 - first).astype(dtype)


def lanes(start):
    return pl.ds(pl.multiple_of(start, 128), 128)


class Fetched:
    def __init__(self, source, held, sems, count):
        self.source, self.held, self.sems, self.count = source, held, sems, count
        self.waiting, self.shape, self.started = count == 1, held.shape, False

    def start(self):
        if not self.started:
            for k in range(self.count):
                self.part(k).start()
        self.started = True

    def part(self, k):
        if self.count == 1:
            return pltpu.make_async_copy(self.source, self.held, self.sems.at[0])
        size = self.shape[0] // self.count
        at = pl.ds(k * size, size)
        return pltpu.make_async_copy(self.source.at[at], self.held.at[at], self.sems.at[k])

    def ready(self):
        self.start()
        if self.waiting:
            self.part(0).wait()
            self.waiting = False
        return self.held

    def __getitem__(self, at):
        return self.ready()[at]

    @property
    def at(self):
        return self.ready().at


class Shipped:
    def __init__(self, target, held, sems):
        self.target, self.held, self.sems = target, held, sems
        self.shape, self.parts = held.shape, None

    def __getitem__(self, at):
        return self.held[at]

    def __setitem__(self, at, values):
        self.held[at] = values

    @property
    def at(self):
        return self.held.at

    def copy(self, k, part):
        return pltpu.make_async_copy(part(self.held, k), part(self.target, k), self.sems.at[k])

    def ship(self):
        self.leave(0, lambda ref, k: ref)

    def leave(self, k, part):
        self.parts = part
        self.copy(k, part).start()

    def settle(self):
        if self.parts is None:
            self.ship()
        if self.sems.shape[0] == 1:
            self.copy(0, self.parts).wait()
        else:
            lax.fori_loop(0, self.sems.shape[0], lambda k, _: self.copy(k, self.parts).wait() or 0, 0)


def ready(*refs):
    return [ref.ready() if isinstance(ref, Fetched) else ref for ref in refs]


def sides(turned):
    none = jnp.zeros_like(turned[:64])
    return jnp.concatenate(
        [jnp.concatenate([turned[:64], none], axis=0), jnp.concatenate([none, turned[64:]], axis=0)], axis=1
    )


def own_sides(both):
    half = both.shape[1] // 2
    return jnp.concatenate([both[:64, :half], both[64:, half:]], axis=0)


def attend_forward(queries, keys, values, starts, cap, weights, scales, mixed):
    factor = math.log2(math.e) / 8.0
    for p in range(mixed.shape[1] // 128):
        query, key, value = (
            ref[:, start + p * 128 : start + p * 128 + 128]
            for ref, start in zip((queries, keys, values), starts)
        )
        limit = cap[...]
        scores = dot(key, sides(query.T)) * factor
        scores = jnp.minimum(scores, jnp.concatenate([limit, limit], axis=1))
        powers = jnp.exp2(scores - jnp.max(scores, axis=0, keepdims=True))
        scale = 1.0 / jnp.sum(powers, axis=0, keepdims=True)
        powers = powers.astype(jnp.bfloat16)
        weights[p] = powers
        weights.leave(p, one_pair)
        scales[p] = scale
        found = own_sides(dot(value.T, powers) * scale)
        mixed[:, p * 128 : p * 128 + 128] = found.T.astype(jnp.bfloat16)
    mixed.ship()
    scales.ship()


def one_pair(ref, k):
    return ref.at[k]


def attend_backward(queries, keys, values, starts, weights, scales, grad_mixed, grads, places, beside):
    marks = halves(jnp.bfloat16)
    pairs = grad_mixed.shape[1] // 128
    weights.started = True
    for p in (0, 1):
        weights.part(p).start()
    for p in range(pairs):
        query, key, value = (
            ref[:, start + p * 128 : start + p * 128 + 128]
            for ref, start in zip((queries, keys, values), starts)
        )
        scale = scales[p]
        grad = sides(grad_mixed[:, p * 128 : p * 128 + 128].T)
        grad = (grad.astype(jnp.float32) * scale).astype(jnp.bfloat16)
        if p == 1:
            beside()
        if p + 2 < pairs:
            weights.part(p + 2).start()
        weights.part(p).wait()
        powers = weights.held[p]
        wide = powers.astype(jnp.float32)
        product = wide * dot(value, grad)
        total = jnp.sum(product, axis=0, keepdims=True) * scale
        product = (product - wide * total).astype(jnp.bfloat16)
        query = jnp.concatenate([query * marks[0], query * marks[1]], axis=0)
        columns = [slice(place + p * 128, place + p * 128 + 128) for place in places]
        grads[2][:, columns[2]] = dot(powers, grad.T).astype(jnp.bfloat16)
        grads[1][:, columns[1]] = (dot(product, query) * 0.125).astype(jnp.bfloat16)
        grads[0][:, columns[0]] = (own_sides(dot(key.T, product)).T * 0.125).astype(jnp.bfloat16)


def adapter_forward(branch, index, tasks, cond, down, up, mask):
    gain = 1.0 + dot(tasks[...], cond[index])
    normed = (branch * rms_rate(branch) * gain).astype(jnp.bfloat16)
    squeezed = dot(normed, down[index]) * mask[...].astype(jnp.float32)
    return branch + dot(gelu(squeezed).astype(jnp.bfloat16), up[index]), squeezed


def adapter_backward(branch, squeezed, index, tasks, cond, down, up, mask, grad, outs):
    low = grad.astype(jnp.bfloat16)
    outs[1][...] = dot_tn(gelu(squeezed).astype(jnp.bfloat16), low)
    grad_squeezed = (gelu_back(squeezed) * dot_nt(low, up[index])).astype(jnp.bfloat16) * mask[...]
    gain = 1.0 + dot(tasks[...], cond[index])
    rate = rms_rate(branch)
    normed = (branch * rate * gain).astype(jnp.bfloat16)
    outs[0][...] = dot_tn(normed, grad_squeezed).astype(jnp.bfloat16)
    grad_branch, grad_gain = rms_back(branch, rate, gain, dot_nt(grad_squeezed, down[index]))
    outs[2][...] = dot_tn(tasks[...], grad_gain.astype(jnp.bfloat16))[: outs[2].shape[0]]
    return grad + grad_branch


def whole_unit(weight):
    return weight.reshape(-1, weight.shape[-1])


def unit_copy(packed, first, held, sems, u):
    return pltpu.make_async_copy(packed.at[:, first + u], held.at[u], sems.at[u])


def load_units(packed, first, held, sems):
    copies = [unit_copy(packed, first, held, sems, u) for u in range(held.shape[0])]
    for copy in copies:
        copy.start()
    return copies


def rows_copy(packed, held, sems, u):
    units = held.shape[1]
    if held.shape[0] == 1:
        return pltpu.make_async_copy(packed.at[:, 8 + units + u], held.at[:, u], sems.at[units + u])
    share = held.shape[0] // units
    at = pl.ds(u * share, share)
    return pltpu.make_async_copy(packed.at[at, 8 + units :], held.at[at], sems.at[units + u])


def out_rows(held, u):
    units = held.shape[1]
    if held.shape[0] == 1:
        return whole_unit(held[0, u])
    share = held.shape[0] // units
    return whole_unit(held[pl.ds(u * share, share)])


def emit(place, outs, unit, grad):
    if len(outs) == 1:
        outs[0][0, 0, unit] = grad.astype(jnp.bfloat16)
    else:
        rows = outs[0].shape[-2]
        grad = grad.astype(jnp.bfloat16)
        for j in range(8):
            even = grad[2 * j * rows : (2 * j + 1) * rows]
            odd = grad[(2 * j + 1) * rows : (2 * j + 2) * rows]
            emit_block(place, outs, unit, j, even, odd)
    for out in outs:
        out.leave(unit, functools.partial(unit_part, place))


def unit_part(place, ref, unit):
    return ref.at[:, :, :, unit] if len(ref.shape) == 6 else ref.at[:, :, unit]


def emit_block(place, outs, unit, j, even, odd):
    at = ((j & 1) ^ place[1], (j // 2 - place[0]) & 3, unit)
    for out, block in zip(outs, (jnp.where(place[2] == 0, odd, even), jnp.where(place[2] == 0, even, odd))):
        if len(out.shape) == 6:
            half = out.shape[5]
            for x in (0, 1):
                out[(x ^ place[3],) + at] = block[:, x * half : (x + 1) * half]
        else:
            out[at] = block


def attention_kernel(
    tokens, gains, packed, self_cap, tasks, cond, down, up, mask, memory, cross_cap,
    first_normed, projected, first_weights, first_scales, first_mixed, first_branch, first_squeezed, stream,
    normed, query, keyval, weights, scales, mixed, branch, squeezed, result,
    held, sems,
):
    made = (tasks, cond, down, up, mask)
    copies = [unit_copy(packed, 0, held, sems, u) for u in range(8)]
    copies[0].start()
    wide = tokens[...].astype(jnp.float32)
    first_normed[...] = (wide * rms_rate(wide) * gains[0:1]).astype(jnp.bfloat16)
    first_normed.ship()
    width = wide.shape[1]
    copies[1].start()
    for u in range(3):
        copies[u + 2].start()
        copies[u].wait()
        projected[:, u * width : (u + 1) * width] = dot(first_normed[...], whole_unit(held[u])).astype(
            jnp.bfloat16
        )
    projected.ship()
    for operand in (*made, memory, cross_cap):
        operand.start()
    for copy in copies[5:]:
        copy.start()
    attend_forward(
        projected, projected, projected, (0, width, 2 * width), self_cap, first_weights, first_scales, first_mixed
    )
    copies[3].wait()
    first_branch[...] = dot(first_mixed[...], whole_unit(held[3]))
    first_branch.ship()
    adapted, first_squeezed[...] = adapter_forward(first_branch[...], 0, *made)
    first_squeezed.ship()
    wide = tokens[...].astype(jnp.float32) + adapted
    stream[...] = wide
    stream.ship()
    normed[...] = (wide * rms_rate(wide) * gains[1:2]).astype(jnp.bfloat16)
    normed.ship()
    copies[4].wait()
    query[...] = dot(normed[...], whole_unit(held[4])).astype(jnp.bfloat16)
    query.ship()
    for u in range(2):
        copies[5 + u].wait()
        keyval[:, u * width : (u + 1) * width] = dot(memory[...], whole_unit(held[5 + u])).astype(
            jnp.bfloat16
        )
    keyval.ship()
    attend_forward(query, keyval, keyval, (0, 0, width), cross_cap, weights, scales, mixed)
    copies[7].wait()
    branch[...] = dot(mixed[...], whole_unit(held[7]))
    branch.ship()
    adapted, squeezed[...] = adapter_forward(branch[...], 1, *made)
    result[...] = stream[...] + adapted


def feed_kernel(
    place, stream, gains, packed, tasks, cond, down, up, mask, out_grad,
    result, grad_stream, grad_down, grad_up, grad_cond, grad_gain, *rest,
):
    made = (tasks, cond, down, up, mask)
    outs, (held_in, held_out, normed, before, active, grad_branch, total, sems) = rest[:-8], rest[-8:]
    ahead, outs = outs[: len(outs) // 2], outs[len(outs) // 2 :]
    units = active.shape[0]

    def start(u):
        unit_copy(packed, 8, held_in, sems, u).start()
        rows_copy(packed, held_out, sems, u).start()

    start(0)
    wide = stream[...]
    normed[...] = (wide * rms_rate(wide) * gains[2:3]).astype(jnp.bfloat16)
    total[...] = jnp.zeros_like(total)
    for u in range(units):
        if u + 1 < units:
            start(u + 1)
        else:
            for operand in (*made, out_grad):
                operand.start()
        unit_copy(packed, 8, held_in, sems, u).wait()
        value = dot(normed[...], whole_unit(held_in[u]))
        before[u] = value
        active[u] = gelu(value).astype(jnp.bfloat16)
        rows_copy(packed, held_out, sems, u).wait()
        total[...] += dot(active[u], out_rows(held_out, u))
    branch = total[...]
    adapted, squeezed = adapter_forward(branch, 0, *made)
    result[...] = (stream[...] + adapted).astype(jnp.bfloat16)
    result.ship()
    grad_branch[...] = adapter_backward(
        branch, squeezed, 0, *made, out_grad[...].astype(jnp.float32), (grad_down, grad_up, grad_cond)
    ).astype(jnp.bfloat16)
    for out in (grad_down, grad_up, grad_cond):
        out.ship()
    half = active.shape[2] // 2

    def row_part(ref, j):
        if len(outs) == 1:
            return ref.at[0, 0, j // 2, pl.ds((j & 1) * half, half)]
        return ref.at[:, (j & 1) ^ place[1], (j // 2 - place[0]) & 3]

    for j in range(2 * units):
        columns = slice((j & 1) * half, (j & 1) * half + half)
        grad = dot_tn(active[j // 2, :, columns], grad_branch[...]).astype(jnp.bfloat16)
        if len(outs) == 1:
            ahead[0][0, 0, j // 2, columns] = grad
        else:
            rows = outs[0].shape[-2]
            for u in range(4):
                emit_block(
                    place, ahead, u, j,
                    grad[u * rows : (u + 1) * rows], grad[(4 + u) * rows : (5 + u) * rows],
                )
        for out in ahead:
            out.leave(j, row_part)
    total[...] = jnp.zeros_like(total)
    for u in range(units):
        grad = dot_nt(grad_branch[...], out_rows(held_out, u))
        grad = (grad * gelu_back(before[u])).astype(jnp.bfloat16)
        emit(place, outs, u, dot_tn(normed[...], grad))
        total[...] += dot_nt(grad, whole_unit(held_in[u]))
    wide = stream[...]
    grad, gain_rows = rms_back(wide, rms_rate(wide), gains[2:3], total[...])
    grad_stream[...] = out_grad[...].astype(jnp.float32) + grad
    grad_gain[...] = jnp.sum(gain_rows, axis=0, keepdims=True)


def branch_kernel(unit, place, grad_result, packed, squeezed, branch, tasks, cond, down, up, mask, *rest):
    *rest, held, sems = rest
    (copy,) = load_units(packed, unit, held, sems)
    others = 12 if len(rest) > 5 else 0
    others, (grad_branch, grad_mixed, *found) = rest[:others], rest[others:]
    low = grad_result[...]
    for operand in others[6:]:
        operand.start()
    grad_branch[...] = adapter_backward(
        branch[...], squeezed[...], 0, tasks, cond, down, up, mask, low, found[:3]
    ).astype(jnp.bfloat16)
    for out in (grad_branch, *found[:3]):
        out.ship()
    copy.wait()
    grad_mixed[...] = dot_nt(grad_branch[...], whole_unit(held[0])).astype(jnp.bfloat16)
    grad_mixed.ship()
    if others:
        emit_made(place, [found[:3], others[:3], others[3:6]], found[3:5], found[-1])
        own, sent, *parts = found[5:-1]
        for z in range(4):
            sent[z] = low_sum(*(part[1, z] for part in others[6:9]))
        sent.ship()
        for z in range(4):
            parts[z][...] = low_sum(*(part[z] for part in others[9:]))
            parts[z].ship()
        for z in range(4):
            own[z] = low_sum(*(part[0, z] for part in others[6:9]))


def low_sum(*parts):
    total = parts[0].astype(jnp.float32)
    for part in parts[1:]:
        total = total + part.astype(jnp.float32)
    return total.astype(jnp.bfloat16)


def first_sums(kept_cross, got_cross, other_cross, kept_made, got_made, other_made, own_out, other_out, sent_cross, *parts):
    half = other_out.shape[-1]
    for z in range(4):
        parts[z][:2] = low_sum(kept_made[z], got_made[z], other_made[z])
        for u in range(4):
            columns = slice((u & 1) * half, (u & 1) * half + half)
            parts[z][2 + u // 2, :, columns] = low_sum(own_out[z, u], other_out[z, u])
        parts[z].ship()
    for z in range(4):
        sent_cross[z] = low_sum(kept_cross[z], got_cross[z], other_cross[z])


def kept_sums(kept, got, other, *rest):
    for z in range(4):
        rest[-1][z] = low_sum(kept[z], got[z], other[z])
    if len(rest) > 1:
        rest[-2][...] = low_sum(*(ref[...] for ref in rest[:4]))


def second_sums(*refs):
    total_in, kept_self, got_self, other_self, own_cross, other_cross = refs[4:10]
    totals, made, sent_self, *parts = refs[10:]
    for z in range(4):
        sent_self[z] = low_sum(kept_self[z], got_self[z], other_self[z])
    sent_self.ship()
    made[...] = low_sum(*(ref[:2] for ref in refs[:4]))
    made.ship()
    for z in range(4):
        parts[z][...] = low_sum(own_cross[z], other_cross[z])
        parts[z].ship()
    units = total_in.shape[0]
    totals[units:] = low_sum(*(ref[2:] for ref in refs[:4]))
    totals[:units] = total_in[...]


def feed_outs(place, total, other, out_in, out_out):
    wide = total.shape[-1]
    units, rows, half = out_in.shape[1] // wide, out_in.shape[0], wide // 2
    for u in range(units):
        out_in[:, u * wide : (u + 1) * wide] = total[u].astype(jnp.float32) + other[u].astype(jnp.float32)
    for u in range(units):
        at = (units + u // 2, slice(None), slice((u & 1) * half, (u & 1) * half + half))
        join(place, total[at], other[at], out_out, slice(u * rows, (u + 1) * rows), 0)


def join(place, own, other, out, rows, column):
    own, other = own.astype(jnp.float32), other.astype(jnp.float32)
    half = own.shape[-1]
    out[rows, column : column + half] = jnp.where(place[3] == 0, own, other)
    out[rows, column + half : column + 2 * half] = jnp.where(place[3] == 0, other, own)


def unit_outs(place, total, other, *outs):
    unit, wide = 0, 2 * total.shape[-1]
    for out in outs:
        for column in range(0, out.shape[1], wide):
            join(place, total[unit], other[unit], out, slice(None), column)
            unit += 1


def third_sums(*refs):
    own_self, other_self, total_cross, *parts = refs[4:]
    for z in range(4):
        parts[z][...] = low_sum(own_self[z], other_self[z])
        parts[z].ship()
    total_cross[...] = low_sum(*(ref[...] for ref in refs[:4]))


def emit_made(place, made, outs, block):
    rows, wide = outs[0].shape[3], block.shape[2]
    piece, span = wide // 2, wide // 3
    block[...] = jnp.zeros_like(block)
    cond = jnp.concatenate([part[2][...] for part in made], axis=1)
    columns = cond.shape[1] // 16
    for j in range(8):
        for core in (0, 1):
            for slot in range(3):
                at = 3 * (2 * j + core) + slot
                part = made[at // 16][0][(at % 16) * rows : (at % 16 + 1) * rows]
                block[core, :, slot * span : slot * span + part.shape[1]] = part.astype(jnp.float32)
        emit_block(place, outs, 0, j, *(block[core].astype(jnp.bfloat16) for core in (0, 1)))
    for out in outs:
        out.leave(0, functools.partial(unit_part, place))
    block[...] = jnp.zeros_like(block)
    for j in range(8):
        for core in (0, 1):
            owner = 2 * j + core
            for slot in range(9):
                at = 9 * owner + slot
                row, half = (at % 48) // 2, at % 2
                part = made[at // 48][1][row * 8 : row * 8 + 8, half * piece : (half + 1) * piece]
                block[core, slot // 2 * 8 : slot // 2 * 8 + 8, slot % 2 * piece : (slot % 2 + 1) * piece] = part
            turned = pltpu.roll(cond, (cond.shape[1] - owner * columns) % cond.shape[1], 1)
            block[core, 40:48, :span] = turned[:, :span]
        emit_block(place, outs, 1, j, *(block[core].astype(jnp.bfloat16) for core in (0, 1)))
    for out in outs:
        out.leave(1, functools.partial(unit_part, place))


def cross_kernel(
    place, grad_mixed, packed, query, keyval, weights, scales, mixed, grad_branch, normed, memory, stream, gains, grad_result,
    grad_stream, grad_memory, grad_gain, *rest,
):
    outs, (held, grad_query, grad_keyval, sems) = rest[:-4], rest[-4:]
    copies = [unit_copy(packed, 4, held, sems, u) for u in range(3)]
    width = stream.shape[1]

    def beside():
        for copy in (mixed, grad_branch, normed, memory, *copies, stream, gains, grad_result):
            copy.start()

    attend_backward(
        query, keyval, keyval, (0, 0, width), weights, scales, grad_mixed,
        (grad_query, grad_keyval, grad_keyval), (0, 0, width), beside,
    )
    emit(place, outs, 3, dot_tn(mixed[...], grad_branch[...]))
    emit(place, outs, 0, dot_tn(normed[...], grad_query[...]))
    for copy in copies:
        copy.wait()
    for u in range(2):
        grad = grad_keyval[:, u * width : (u + 1) * width]
        emit(place, outs, 1 + u, dot_tn(memory[...], grad))
        if u == 0:
            grad_memory[...] = dot_nt(grad, whole_unit(held[1 + u]))
        else:
            grad_memory[...] += dot_nt(grad, whole_unit(held[1 + u]))
    grad_memory.ship()
    wide = stream[...]
    grad, gain_rows = rms_back(
        wide, rms_rate(wide), gains[1:2], dot_nt(grad_query[...], whole_unit(held[0]))
    )
    grad_stream[...] = grad_result[...] + grad
    grad_gain[...] = jnp.sum(gain_rows, axis=0, keepdims=True)


def self_kernel(
    place, grad_mixed, packed, projected, weights, scales, mixed, grad_branch, normed, tokens, gains, grad_stream,
    grad_tokens, grad_gain, *rest,
):
    outs, (held, grad_projected, total, sems) = rest[:-4], rest[-4:]
    copies = [unit_copy(packed, 0, held, sems, u) for u in range(3)]
    width = tokens.shape[1]

    def beside():
        for copy in (mixed, grad_branch, normed, *copies, tokens, gains, grad_stream):
            copy.start()

    attend_backward(
        projected, projected, projected, (0, width, 2 * width), weights, scales, grad_mixed,
        (grad_projected,) * 3, (0, width, 2 * width), beside,
    )
    emit(place, outs, 3, dot_tn(mixed[...], grad_branch[...]))
    for u in range(3):
        copies[u].wait()
        grad = grad_projected[:, u * width : (u + 1) * width]
        emit(place, outs, u, dot_tn(normed[...], grad))
        if u == 0:
            total[...] = dot_nt(grad, whole_unit(held[u]))
        else:
            total[...] += dot_nt(grad, whole_unit(held[u]))
    wide = tokens[...].astype(jnp.float32)
    grad, gain_rows = rms_back(wide, rms_rate(wide), gains[0:1], total[...])
    grad_tokens[...] = grad_stream[...] + grad
    grad_gain[...] = jnp.sum(gain_rows, axis=0, keepdims=True)


def sum_kernel(*refs):
    refs[-1][...] = low_sum(*(ref[...] for ref in refs[:-1]))


def swap(values, axis, count, mate):
    return lax.ppermute(values, axis, [(i, mate(i)) for i in range(count)])


def place_parts():
    place = lax.axis_index("fsdp")
    return place // 4, (place // 2) % 2, place % 2


def ring_gather(block):
    z, y, core = place_parts()
    shifted = [swap(block, "fsdp", 16, lambda i, d=d: (i + 4 * d) % 16) for d in (3, 2, 1)]
    line = jnp.stack(shifted[:1] + shifted[1:] + [block])
    line = lax.dynamic_slice_in_dim(jnp.concatenate([line, line]), 3 - z, 4, 0)
    other = swap(line, "fsdp", 16, lambda i: i ^ 2)
    both = jnp.stack([jnp.where(y == 0, line, other), jnp.where(y == 0, other, line)], axis=1)
    other = swap(both, "fsdp", 16, lambda i: i ^ 1)
    whole = jnp.stack([jnp.where(core == 0, both, other), jnp.where(core == 0, other, both)], axis=2)
    return whole.reshape((16,) + block.shape)


def add_low(left, right):
    return (left.astype(jnp.float32) + right.astype(jnp.float32)).astype(jnp.bfloat16)


def core_swap(sent):
    return swap(sent, "fsdp", 16, lambda i: i ^ 1)


def y_swap(sent):
    return swap(sent, "fsdp", 16, lambda i: i ^ 2)


def x_swap(sent):
    return swap(sent, "dp", 2, lambda i: i ^ 1)


def z_swaps(parts):
    return [swap(parts[d], "fsdp", 16, lambda i, d=d: (i + 4 * d) % 16) for d in (1, 2, 3)]


def both_halves(own, other, first_x):
    return jnp.concatenate([jnp.where(first_x, own, other), jnp.where(first_x, other, own)], axis=-1)


def after(values, *others):
    return lax.optimization_barrier((values, others))[0]


def ring_step(values, bit):
    return values + swap(values, "fsdp", 16, lambda i: i ^ bit)


def gather_shards(block, ring):
    return ring_gather(block) if ring else lax.all_gather(block, "fsdp", axis=0)


def block_share(blocks):
    part = lax.psum_scatter(blocks, "fsdp", scatter_dimension=0, tiled=False)
    return lax.psum(part.astype(jnp.float32), "dp")


def share_of(grads, devices, by_rows):
    whole = grads[0][0, 0]
    count, width = whole.shape[0], whole.shape[-1]
    if by_rows:
        return block_share(whole.reshape(devices, count, -1, width))
    blocks = jnp.transpose(whole.reshape(count, devices, -1, width), (1, 0, 2, 3))
    return block_share(blocks)


def sum_shards(values, ring):
    return ring_sum(values) if ring else lax.psum(values, "fsdp")


def units_of(shard, width):
    rows, columns = shard.shape
    return jnp.transpose(shard.reshape(rows, columns // width, width), (1, 0, 2))


def joined(units):
    return jnp.transpose(units, (1, 0, 2)).reshape(units.shape[1], -1)


def view_shape(shape, view):
    return tuple(at.size for at in view if not isinstance(at, int)) + tuple(shape[len(view) :])


def call(kernel, operands, shapes, scratch, flops, raw=(), split=None, parts=None, later=(), views=None):
    split, parts, views = split or {}, parts or {}, views or {}
    scalars = operands[0].ndim == 1
    moved_in = [i for i in range(int(scalars), len(operands)) if i not in raw]
    specs = [pl.BlockSpec(memory_space=pl.ANY) for _ in operands]
    if scalars:
        specs[0] = pl.BlockSpec(memory_space=pltpu.SMEM)
    outs = [jax.ShapeDtypeStruct(shape, dtype) for shape, dtype in shapes]
    buffers = [pltpu.VMEM(view_shape(operands[i].shape, views.get(i, ())), operands[i].dtype) for i in moved_in]
    buffers += [pltpu.VMEM(shape, dtype) for shape, dtype in shapes]
    buffers += [pltpu.SemaphoreType.DMA((split.get(i, 1),)) for i in moved_in]
    buffers += [pltpu.SemaphoreType.DMA((parts.get(k, 1),)) for k in range(len(outs))]

    def body(*refs):
        ins, results = list(refs[: len(operands)]), refs[len(operands) : len(operands) + len(outs)]
        own = refs[len(operands) + len(outs) : len(refs) - len(buffers)]
        held = refs[len(refs) - len(buffers) :]
        held, sems = held[: len(buffers) // 2], held[len(buffers) // 2 :]
        for k, i in enumerate(moved_in):
            source = ins[i].at[views[i]] if i in views else ins[i]
            ins[i] = Fetched(source, held[k], sems[k], split.get(i, 1))
            if i not in later:
                ins[i].start()
        results = [
            Shipped(target, *rest) for target, *rest in zip(results, held[len(moved_in) :], sems[len(moved_in) :])
        ]
        kernel(*ins, *results, *own)
        for operand in ins:
            ready(operand)
        for result in results:
            result.settle()

    moved = sum(math.prod(shape) * jnp.dtype(dtype).itemsize for shape, dtype in shapes)
    moved += sum(operand.size * operand.dtype.itemsize for operand in operands)
    return pl.pallas_call(
        body,
        out_shape=outs,
        in_specs=specs,
        out_specs=[pl.BlockSpec(memory_space=pl.ANY) for _ in outs],
        scratch_shapes=list(scratch) + buffers,
        compiler_params=pltpu.CompilerParams(vmem_limit_bytes=60 * 1024 * 1024),
        cost_estimate=pl.CostEstimate(flops=flops, bytes_accessed=moved, transcendentals=0),
    )(*operands)


def per_device(
    devices,
    ring,
    tokens,
    memory,
    out_grad,
    target_len,
    source_len,
    task_ids,
    norm_gains,
    self_qkv,
    self_out,
    cross_query,
    cross_keyval,
    cross_out,
    feed_in,
    feed_out,
    task_table,
    hyper_in,
    maker_down,
    maker_up,
    maker_norm,
):
    width = tokens.shape[1]
    tasks = task_table.shape[0]
    embed = hyper_in.shape[0]
    table_width = task_table.shape[1]
    hyper_width = hyper_in.shape[1]
    gain_width = norm_gains.shape[1]
    down_span = maker_down.shape[1]
    norm_span = maker_norm.shape[1]
    bottleneck = down_span * devices // (3 * width)
    down_rows = 3 * width // devices
    unit = width // devices
    ff_units = feed_in.shape[1] // width
    small = jnp.concatenate(
        [
            jnp.pad(task_table.T, ((0, 0), (0, 128 - tasks))),
            jnp.pad(hyper_in.T, ((0, 0), (0, 128 - embed))),
            jnp.pad(norm_gains, ((0, 0), (0, 128 - gain_width))),
            jnp.zeros((-(table_width + hyper_width + 3) % 16, 128), jnp.bfloat16),
        ]
    )
    small = gather_shards(small, ring)
    whole_table = small[:, :table_width, :tasks].reshape(-1, tasks).T
    whole_hyper = small[:, table_width : table_width + hyper_width, :embed].reshape(-1, embed).T
    first = table_width + hyper_width
    whole_gains = jnp.transpose(small[:, first : first + 3, :gain_width], (1, 0, 2)).reshape(3, width)
    layer = [self_qkv, self_out, cross_query, cross_keyval, cross_out, feed_in]
    layer = [units_of(w, width) for w in layer] + [feed_out.reshape(ff_units, unit, width)]
    packed = jnp.concatenate([w.reshape(-1, width) for w in layer])
    packed = lax.all_gather(packed, "fsdp", axis=0).reshape(devices, -1, unit, width)
    if not ring:
        first = jnp.transpose(packed[:, : 8 + ff_units], (1, 0, 2, 3)).reshape(-1, width, width)
        last = packed[:, 8 + ff_units :].reshape(-1, width, width)
        packed = jnp.concatenate([first, last])[None]
    pre_hidden = matmul(whole_table, whole_hyper)
    hidden = jax.nn.silu(pre_hidden).astype(jnp.bfloat16)
    own_down = matmul(hidden, maker_down).astype(jnp.bfloat16)
    own_up = matmul(hidden, maker_up).astype(jnp.bfloat16)
    own_norm = matmul(hidden, maker_norm).astype(jnp.bfloat16)
    span = tasks * bottleneck
    own_down = jnp.transpose(own_down.reshape(tasks, down_rows, bottleneck), (1, 2, 0)).reshape(-1, span)
    if ring:
        third, piece = width // 3, width // 2
        own_down = jnp.pad(own_down.reshape(3, unit, span), ((0, 0), (0, 0), (0, third - span)))
        own_down = jnp.transpose(own_down, (1, 0, 2)).reshape(unit, width)
        own_up = jnp.pad(own_up, ((0, 0), (0, 10 * piece - down_span))).reshape(tasks, 5, width)
        own_up = jnp.transpose(own_up, (1, 0, 2)).reshape(5 * tasks, width)
        own_norm = jnp.pad(own_norm, ((0, 0), (0, width - norm_span)))
        made = jnp.concatenate([own_down, own_up, own_norm])
        first_x = lax.axis_index("dp") == 0
        made = ring_gather(jnp.where(first_x, made[:, : width // 2], made[:, width // 2 :]))
        made = both_halves(made, x_swap(made), first_x)
        made_down = made[:, :unit].reshape(devices, unit, 3, third)[..., :span]
        made_down = jnp.transpose(made_down, (0, 2, 1, 3)).reshape(3, width, span)
        made_up = made[:, unit : unit + 5 * tasks].reshape(devices, 5, tasks, 2, piece)
        made_up = jnp.transpose(made_up, (0, 1, 3, 2, 4)).reshape(devices, 10, tasks, piece)[:, :9]
        made_up = jnp.transpose(made_up.reshape(3, bottleneck, 2, tasks, piece), (0, 1, 3, 2, 4))
        made_up = made_up.reshape(3, span, width)
        made_cond = made[:, unit + 5 * tasks :, :norm_span]
    else:
        made_down = lax.all_gather(own_down, "fsdp", axis=0, tiled=True).reshape(3, width, span)
        made_up = lax.all_gather(own_up, "fsdp", axis=1, tiled=True).reshape(tasks, 3, bottleneck, width)
        made_up = jnp.transpose(made_up, (1, 2, 0, 3)).reshape(3, span, width)
        made_cond = lax.all_gather(own_norm, "fsdp", axis=0)
    made_cond = jnp.transpose(made_cond, (1, 0, 2)).reshape(tasks, 3, width)
    made_cond = jnp.pad(jnp.transpose(made_cond, (1, 0, 2)), ((0, 0), (0, 128 - tasks), (0, 0)))
    tok_seg = segment_rows(target_len[0], tokens.shape[0])
    mem_seg = segment_rows(source_len[0], memory.shape[0])
    sequences = jnp.arange(target_len.shape[1], dtype=jnp.int32)
    row_task = jnp.sum(
        jnp.where(tok_seg[:, None] == sequences[None, :], task_ids[0][None, :], 0), axis=1
    )
    onehot = (row_task[:, None] == jnp.arange(128, dtype=jnp.int32)[None, :]).astype(jnp.bfloat16)
    mask = jnp.tile(onehot[:, :tasks], (1, bottleneck))
    places = jnp.arange(tokens.shape[0], dtype=jnp.int32)
    self_allowed = (tok_seg[:, None] == tok_seg[None, :]) & (places[:, None] <= places[None, :])
    cross_allowed = mem_seg[:, None] == tok_seg[None, :]
    self_cap = jnp.where(self_allowed, -masked_score * 1e20, masked_score).astype(jnp.float32)
    cross_cap = jnp.where(cross_allowed, -masked_score * 1e20, masked_score).astype(jnp.float32)
    gains = jnp.pad(whole_gains.astype(jnp.float32), ((0, 5), (0, 0)))
    place = lax.axis_index("fsdp")
    here = jnp.stack([place // 4, (place // 2) % 2, place % 2, lax.axis_index("dp")]).astype(jnp.int32)
    adapters = (onehot, made_cond, made_down, made_up, mask)
    rows, memory_rows = tokens.shape[0], memory.shape[0]
    pairs = width // 128
    low, full = jnp.bfloat16, jnp.float32
    held_unit = packed.shape[:1] + packed.shape[2:]

    def held(count):
        return pltpu.VMEM((count,) + held_unit, low)

    def grad_shapes(count, by_x=False):
        if ring and by_x:
            return [((2, 2, 4, count, unit, width // 2), low)] * 2
        if ring:
            return [((2, 4, count, unit, width), low)] * 2
        return [((1, 1, count, width, width), low)]

    made_shapes = [((width, span), low), ((span, width), full), ((tasks, width), full)]
    gain_shape = [((1, width), full)]
    busy = 1700000000
    scale_shape = ((pairs, 1, 2 * rows), full)
    float_rows, low_rows = ((rows, width), full), ((rows, width), low)
    found = call(
        attention_kernel,
        (tokens, gains, packed, self_cap) + adapters + (memory, cross_cap),
        [low_rows, ((rows, 3 * width), low), ((pairs, rows, 2 * rows), low), scale_shape, low_rows, float_rows]
        + [((rows, span), full), float_rows, low_rows, low_rows, ((memory_rows, 2 * width), low)]
        + [((pairs, memory_rows, 2 * rows), low), scale_shape, low_rows, float_rows]
        + [((rows, span), full), float_rows],
        [held(8), pltpu.SemaphoreType.DMA((8,))],
        37 * busy,
        raw=(2,),
        parts={2: pairs, 11: pairs},
        later=(4, 5, 6, 7, 8, 9, 10),
    )
    normed1, projected, weights1, scales1, mixed1, branch1, squeezed1, stream1, *found = found
    normed2, query2, keyval2, weights2, scales2, mixed2, branch2, squeezed2, stream2 = found
    held_out = (packed.shape[0], ff_units) + packed.shape[2:]
    sets = 2 if ring else 1
    result, grad_stream, *found = call(
        feed_kernel,
        (here, stream2, gains, packed) + adapters + (out_grad,),
        [low_rows, float_rows] + made_shapes + gain_shape + grad_shapes(ff_units, True) + grad_shapes(ff_units),
        [
            held(ff_units),
            pltpu.VMEM(held_out, low),
            pltpu.VMEM((rows, width), low),
            pltpu.VMEM((ff_units, rows, width), full),
            pltpu.VMEM((ff_units, rows, width), low),
            pltpu.VMEM((rows, width), low),
            pltpu.VMEM((rows, width), full),
            pltpu.SemaphoreType.DMA((2 * ff_units,)),
        ],
        36 * busy,
        raw=(3,),
        parts={6 + k: (2 if k < sets else 1) * ff_units for k in range(2 * sets)},
        later=(4, 5, 6, 7, 8, 9),
        views=dict.fromkeys((5, 6, 7), (pl.ds(2, 1),)),
    )
    made_three, grad_gain_three, grads_out, grads_in = found[:3], found[3], found[4 : 4 + sets], found[4 + sets :]

    def branch_back(index, unit_at, grad_result, branch, squeezed, others, shapes):
        return call(
            functools.partial(branch_kernel, unit_at),
            (here, grad_result, packed, squeezed, branch) + adapters + others,
            [low_rows] * 2 + made_shapes + shapes,
            [pltpu.VMEM((2, unit, width), full)] * int(bool(others)) + [held(1), pltpu.SemaphoreType.DMA((1,))],
            30 * busy,
            raw=(2,),
            parts={5: 2, 6: 2} if others else {},
            later=tuple(range(16, 22)) if others else (),
            views=dict.fromkeys((6, 7, 8), (pl.ds(index, 1),))
            | (dict.fromkeys((16, 17, 19, 20), (0,)) if others else {}),
        )

    if ring:
        got_out, got_in = core_swap(grads_out[0]), core_swap(grads_in[0])
    grad_branch, grad_mixed, *made_two = branch_back(1, 7, grad_stream, branch2, squeezed2, (), [])
    if ring:
        got_out, got_in = after((got_out, got_in), grad_mixed)
        sent_out, sent_in = (add_low(kept[1], got[1]) for (_, kept), got in ((grads_out, got_out), (grads_in, got_in)))
        other_out, other_in = x_swap(sent_out), y_swap(sent_in)
        grad_mixed = after(grad_mixed, sent_out, sent_in)
    grad_stream, grad_memory, grad_gain_two, *grads_cross = call(
        cross_kernel,
        (here, grad_mixed, packed, query2, keyval2, weights2, scales2, mixed2, grad_branch, normed2)
        + (memory, stream1, gains, grad_stream),
        [float_rows, ((memory_rows, width), full)] + gain_shape + grad_shapes(4, True),
        [
            held(3),
            pltpu.VMEM((rows, width), low),
            pltpu.VMEM((memory_rows, 2 * width), low),
            pltpu.SemaphoreType.DMA((3,)),
        ],
        24 * busy,
        raw=(2,),
        split={5: pairs},
        parts={3: 4, 4: 4},
        later=(5,) + tuple(range(7, 14)),
    )
    others, shapes = (), []
    if ring:
        got_cross = core_swap(grads_cross[0])
        others = (*made_two, *made_three, grads_out[1], got_out, other_out, grads_in[1], got_in, other_in)
        shapes = [((2, 4, 2, unit, width), low)] * 2
        shapes += [((4, ff_units, unit, width // 2), low)] * 2 + [((ff_units, unit, width), low)] * 4
    grad_branch, grad_mixed, *made_one = branch_back(0, 3, grad_stream, branch1, squeezed1, others, shapes)
    if ring:
        sent_made, kept_made, own_out, sent_out, *parts_in = made_one[3:]
        got_made = core_swap(sent_made)
        got_cross = after(got_cross, grad_mixed)
        sent_cross = add_low(grads_cross[1][1], got_cross[1])
        other_cross = x_swap(sent_cross)
        sent_out, parts_in = after((sent_out, parts_in), sent_cross)
        other_out, far_in = y_swap(sent_out), z_swaps(parts_in)
        sent_made = add_low(kept_made[1], after(got_made, sent_cross)[1])
        other_made = y_swap(sent_made)
        grad_mixed = after(grad_mixed, sent_made)
    grad_tokens, grad_gain_one, *grads_self = call(
        self_kernel,
        (here, grad_mixed, packed, projected, weights1, scales1, mixed1, grad_branch, normed1, tokens, gains)
        + (grad_stream,),
        [float_rows] + gain_shape + grad_shapes(4, True),
        [
            held(3),
            pltpu.VMEM((rows, 3 * width), low),
            pltpu.VMEM((rows, width), full),
            pltpu.SemaphoreType.DMA((3,)),
        ],
        18 * busy,
        raw=(2,),
        split={4: pairs},
        parts={2: 4, 3: 4},
        later=(4,) + tuple(range(6, 12)),
    )

    def own_made(share):
        own_down = share[0].reshape(unit, 3, third)[:, :, :span]
        own_down = jnp.transpose(own_down, (1, 0, 2)).reshape(down_rows, bottleneck, tasks)
        own_down = jnp.transpose(own_down, (2, 0, 1)).reshape(tasks, down_span)
        own_up = share[1, : 5 * tasks].reshape(5, tasks, width)
        own_up = jnp.transpose(own_up, (1, 0, 2)).reshape(tasks, 5 * width)[:, :down_span]
        return own_down, own_up, share[1, 5 * tasks :, :norm_span]

    def hidden_of(own_down, own_up, own_norm):
        return (
            dot_nt(own_down.astype(jnp.bfloat16), maker_down)
            + dot_nt(own_up.astype(jnp.bfloat16), maker_up)
            + dot_nt(own_norm.astype(jnp.bfloat16), maker_norm)
        )

    grad_gains = jnp.concatenate([grad_gain_one, grad_gain_two, grad_gain_three]).reshape(-1, 128)
    if ring:
        got_self = core_swap(grads_self[0])
        flight = (far_in, other_cross, other_made, other_out)
        far_in, other_cross, other_made, other_out = after(flight, grad_gain_one)
        halves_y, column_half = ((4, 4, unit, width // 2), low), ((4, unit, width // 2), low)
        whole_part = ((4, unit, width), low)
        sent_cross, *parts = call(
            first_sums,
            (grads_cross[1], got_cross, other_cross, kept_made, got_made, other_made, own_out, other_out),
            [halves_y] + [whole_part] * 4,
            [],
            100 * busy,
            views={0: (0, 1), 1: (0, 1), 2: (1,), 3: (0,), 4: (0,)},
        )
        sent_self = add_low(grads_self[1][1], after(got_self, sent_cross)[1])
        other_self = x_swap(sent_self)
        parts, sent_cross = after((parts, sent_cross), sent_self)
        far = z_swaps(parts)
        kept_cross, far_in = after((grads_cross[1], far_in), sent_self)
        total_in, own_cross = call(
            kept_sums,
            (kept_cross, got_cross, other_cross, parts_in[0], *far_in),
            [whole_part, halves_y],
            [],
            100 * busy,
            views={0: (0, 0), 1: (0, 0), 2: (0,)},
        )
        other_cross = y_swap(sent_cross)
        totals, total_made, sent_self, *parts = call(
            second_sums,
            (parts[0], *far, total_in, grads_self[1], got_self, other_self, own_cross, other_cross),
            [((6, unit, width), low), ((2, unit, width), low), halves_y] + [column_half] * 4,
            [],
            5 * busy,
            views={5: (0, 1), 6: (0, 1), 7: (1,)},
        )
        other_made, far, other_totals = x_swap(total_made), z_swaps(parts), x_swap(totals)
        (own_self,) = call(
            kept_sums,
            (after(grads_self[1], other_made), got_self, other_self),
            [halves_y],
            [],
            100 * busy,
            views={0: (0, 0), 1: (0, 0), 2: (0,)},
        )
        other_self = y_swap(sent_self)
        other_gains = x_swap(after(grad_gains, total_made))
        share_made = total_made.astype(jnp.float32) + other_made.astype(jnp.float32)
        own_down, own_up, own_norm = own_made(share_made)
        sums = jnp.concatenate([hidden_of(own_down, own_up, own_norm), grad_gains + other_gains])
        sums = ring_step(sums, 1)
        total_cross, *parts = call(
            third_sums, (parts[0], *far, own_self, other_self), [column_half] * 5, [], 5 * busy
        )
        other_cross, far = x_swap(total_cross), z_swaps(parts)
        sums = ring_step(after(sums, total_cross), 2)
        shapes = [((unit, ff_units * width), full), ((ff_units * unit, width), full)]
        out_feed_in, out_feed_out = call(
            feed_outs, (here, totals, after(other_totals, sums)), shapes, [], 100 * busy
        )
        for part in z_swaps([sums] * 4):
            sums = sums + part
        far = after(far, sums)
        total_self = call(sum_kernel, (parts[0], *far), [column_half], [], 5 * busy)[0]
        other_self, other_cross = x_swap(total_self), after(other_cross, total_self)
        shapes = [((unit, count * width), full) for count in (1, 2, 1)]
        out_query, out_keyval, out_cross_out = call(
            unit_outs, (here, total_cross, other_cross), shapes, [], 100 * busy
        )
        shapes = [((unit, count * width), full) for count in (3, 1)]
        out_qkv, out_self_out = call(unit_outs, (here, total_self, other_self), shapes, [], busy)
    else:
        share_in, share_out, share_cross, share_self = (
            share_of(grads, devices, grads is grads_out)
            for grads in (grads_in, grads_out, grads_cross, grads_self)
        )
        made = (made_one, made_two, made_three)
        grad_down = jnp.concatenate([part[0] for part in made]).reshape(devices, -1)
        grad_up = jnp.stack([part[1] for part in made]).reshape(3, bottleneck, tasks, width)
        grad_up = jnp.transpose(grad_up, (2, 0, 1, 3)).reshape(tasks, devices, down_span)
        grad_norm = jnp.concatenate([part[2] for part in made], axis=1)
        grad_norm = grad_norm.reshape(tasks, devices, norm_span)
        blocks = [grad_down.astype(jnp.bfloat16)] + [
            jnp.transpose(part.astype(jnp.bfloat16), (1, 0, 2)).reshape(devices, -1)
            for part in (grad_up, grad_norm)
        ]
        out_feed_in, out_feed_out = joined(share_in), share_out.reshape(-1, width)
        out_query, out_keyval, out_cross_out = share_cross[0], joined(share_cross[1:3]), share_cross[3]
        out_qkv, out_self_out = joined(share_self[:3]), share_self[3]
        share_made = block_share(jnp.concatenate(blocks, axis=1))
        sizes = (0, tasks * down_span, 2 * tasks * down_span, share_made.shape[0])
        own_down, own_up, own_norm = (share_made[a:b] for a, b in zip(sizes, sizes[1:]))
        own_down = jnp.transpose(own_down.reshape(down_rows, bottleneck, tasks), (2, 0, 1))
        own_down, own_up = own_down.reshape(tasks, down_span), own_up.reshape(tasks, down_span)
        own_norm = own_norm.reshape(tasks, norm_span)
        sums = jnp.concatenate([hidden_of(own_down, own_up, own_norm), lax.psum(grad_gains, "dp")])
        sums = lax.psum(sums, "fsdp")
    grad_hidden = sums[:tasks]
    out_gains = lax.dynamic_slice_in_dim(
        sums[tasks:].reshape(3, width), place * gain_width, gain_width, 1
    )
    _, silu_pull = jax.vjp(jax.nn.silu, pre_hidden)
    grad_pre_hidden = silu_pull(grad_hidden)[0]
    own_hyper = lax.dynamic_slice_in_dim(whole_hyper, place * table_width, table_width, 0)
    out_table = exact_cols(grad_pre_hidden, own_hyper.astype(jnp.float32))
    own_pre = lax.dynamic_slice_in_dim(grad_pre_hidden, place * hyper_width, hyper_width, 1)
    out_hyper = exact_rows(whole_table.astype(jnp.float32), own_pre)
    out_down, out_up, out_norm = (
        dot_tn(hidden, own.astype(jnp.bfloat16)) for own in (own_down, own_up, own_norm)
    )
    return (
        result.astype(jnp.bfloat16),
        grad_tokens,
        grad_memory,
        out_gains,
        out_qkv,
        out_self_out,
        out_query,
        out_keyval,
        out_cross_out,
        out_feed_in,
        out_feed_out,
        out_table,
        out_hyper,
        out_down,
        out_up,
        out_norm,
    )


def solution(mesh):
    placed = (
        P(("fsdp", "dp"), None),
        P(("fsdp", "dp"), None),
        P(("fsdp", "dp"), None),
        P(("fsdp", "dp"), None),
        P(("fsdp", "dp"), None),
        P(("fsdp", "dp"), None),
        P(None, "fsdp"),
        P("fsdp", None),
        P("fsdp", None),
        P("fsdp", None),
        P("fsdp", None),
        P("fsdp", None),
        P("fsdp", None),
        P("fsdp", None),
        P(None, "fsdp"),
        P(None, "fsdp"),
        P(None, "fsdp"),
        P(None, "fsdp"),
        P(None, "fsdp"),
    )
    devices = mesh.shape["fsdp"]
    ring = devices == 16 and mesh.shape["dp"] == 2
    return jax.shard_map(
        functools.partial(per_device, devices, ring),
        mesh=mesh,
        in_specs=placed,
        out_specs=(
            P(("fsdp", "dp"), None),
            P(("fsdp", "dp"), None),
            P(("fsdp", "dp"), None),
            P(None, "fsdp"),
            P("fsdp", None),
            P("fsdp", None),
            P("fsdp", None),
            P("fsdp", None),
            P("fsdp", None),
            P("fsdp", None),
            P("fsdp", None),
            P(None, "fsdp"),
            P(None, "fsdp"),
            P(None, "fsdp"),
            P(None, "fsdp"),
            P(None, "fsdp"),
        ),
        check_vma=False,
    )
```

time: 450 us -> 363 us (0.81)
  waiting for transfers between devices: 151 us -> 104 us
  other arithmetic: 45.6 us -> 20.9 us
  local copies, waits for them, and re-layouts: 33.1 us -> 18.5 us
    ppermute x47 -> x46, waiting for transfers between devices: 115 us -> 83.6 us  [swap(): return lax.ppermute(values, axis, [(i, mate(i)) for i in range(count)])]
    all_gather x1, waiting for transfers between devices: 36.6 us -> 19.9 us  [per_device(): lax.all_gather(packed, 'fsdp', axis=0).reshape(devices, -1, unit, width)]
    convert_element_type x12 -> x5, other arithmetic: 22.8 us -> 9.51 us  [add_low(): (left.astype(jnp.float32) + right.astype(jnp.float32)).astype(jnp.bfloat16)]
    dot_general x0 -> x6, matrix products: none -> 6.25 us  [the longest x3 4.85 us: dot_tn(): lax.dot_general(left, right, (((0,), (0,)), ((), ())), preferred_element_...]
    reshape x14 -> x2, local copies, waits for them, and re-layouts: 8.75 us -> 3.13 us  [the longest x1 2.53 us: per_device(): made_down = made[:, :unit].reshape(devices, unit, 3, third)[..., :span]]
    concatenate x4 -> x1, local copies, waits for them, and re-layouts: 5.49 us -> 0.02 us  [per_device(): packed = jnp.concatenate([w.reshape(-1, width) for w in layer])]
    dot_general x4 -> x1, matrix products: 6 us -> 0.87 us  [exact_rows(): lax.dot_general(left, right, (((0,), (0,)), ((), ())), precision=highest,...]
    pallas_call x9 -> x15, Pallas kernels: 134 us -> 132 us  [call(): pl.pallas_call(body, out_shape=outs, in_specs=specs, out_specs=[pl.BlockS...]
  transfers between devices with their start and end apart: 48 -> 47, of which waited for: 25 -> 23; matrix products, arithmetic and copies ran while one was open for 15% -> 10% of each run, Pallas kernels for 17% -> 21%
where the time goes in v2:
time: 363 us; the launch traced here: 357 us
  Pallas kernels  132 us (36%)
  waiting for transfers between devices  104 us (29%)
  starting transfers between devices  57.6 us (16%)
  other arithmetic  20.9 us (6%)
  local copies, waits for them, and re-layouts  18.5 us (5%)
  between operations  15.4 us (4%)
  matrix products  9.3 us (3%)
    pallas_call x15, Pallas kernels, call(): pl.pallas_call(body, out_shape=outs, in_specs=specs, out_specs=[pl.BlockS...  132 us
    ppermute x46, waiting for transfers between devices, swap(): return lax.ppermute(values, axis, [(i, mate(i)) for i in range(count)])  83.6 us
    ppermute x46, starting transfers between devices, swap(): return lax.ppermute(values, axis, [(i, mate(i)) for i in range(count)])  57.5 us
    all_gather x1, waiting for transfers between devices, per_device(): lax.all_gather(packed, 'fsdp', axis=0).reshape(devices, -1, unit, width)  19.9 us
    convert_element_type x5, other arithmetic, add_low(): (left.astype(jnp.float32) + right.astype(jnp.float32)).astype(jnp.bfloat16)  9.51 us
  transfers between devices with their start and end apart: 47, of which 23 were waited for; matrix products, arithmetic and copies ran while one was open for 10% of the time, Pallas kernels for 21%

profile of v2, /device:TPU:0, one launch (start us, length us, event | category | flops | bytes accessed | tf_op | source)
XLA Modules:
  0.0 357.0 jit_solution(9290382085932387919)
XLA Ops:
  11.6 5.0 %collective-permute-start = (bf16[16,128]{1,0:T(8,128)(2,1)S(1)}, bf16[16,128]{1,0:T(8,128)(2,1)S(1)}, u32[]{:S(2)}, u32[]{:S(2)}) collective-permute-start(bf16[16,128]{1,0:T(8,128)(2,1)S(1)} %fusion.24), channel_id=1, source_target_pairs={{0,24},{2,26},{4,28},{6,30},{8,0},{10,2},{12,4},{14,6},{16,8},{18,... | collective-permute-start | bytes 12296 | tf_op jit(solution)/shard_map/ppermute | solution.py:644
  18.0 3.2 collective-permute-done.1
  23.7 2.5 collective-permute-done.3
  30.2 3.0 collective-permute-start.5
  33.8 3.6 collective-permute-done.5
  37.4 6.0 %collective-permute-done.6 = bf16[96,384]{1,0:T(8,128)(2,1)S(1)} collective-permute-done((bf16[96,384]{1,0:T(8,128)(2,1)S(1)}, bf16[96,384]{1,0:T(8,128)(2,1)S(1)}, u32[]{:S(2)}, u32[]{:S(2)}) %collective-permute-start.6) | collective-permute-done | bytes 73760 | tf_op jit(solution)/shard_map/ppermute | solution.py:644
  45.3 14.1 %collective-permute-done.8 = bf16[4,96,384]{2,1,0:T(8,128)(2,1)S(1)} collective-permute-done((bf16[4,96,384]{2,1,0:T(8,128)(2,1)S(1)}, bf16[4,96,384]{2,1,0:T(8,128)(2,1)S(1)}, u32[]{:S(2)}, u32[]{:S(2)}) %collective-permute-start.8) | collective-permute-done | bytes 294944 | tf_op jit(solution)/shard_map/ppermute | solution.py:644
  68.0 22.2 %collective-permute-done.10 = bf16[16,96,384]{2,1,0:T(8,128)(2,1)} collective-permute-done((bf16[16,96,384]{2,1,0:T(8,128)(2,1)S(1)}, bf16[16,96,384]{2,1,0:T(8,128)(2,1)}, u32[]{:S(2)}, u32[]{:S(2)}) %collective-permute-start.10) | collective-permute-done | bytes 1179680 | tf_op jit(solution)/shard_map/ppermute | solution.py:644
  95.5 2.5 reshape.210
  99.8 19.9 %all-gather.3.cloned.1.call-done = bf16[12288,768]{1,0:T(8,128)(2,1)} async-done(((bf16[768,768]{1,0:T(8,128)(2,1)}), bf16[12288,768]{1,0:T(8,128)(2,1)}) %all-gather.3.cloned.1.call-update) | async-done | bytes 18874384 | tf_op jit(solution)/shard_map/all_gather | solution.py:827
  119.7 24.1 %shard_map.306 = (bf16[384,768]{1,0:T(8,128)(2,1)}, bf16[384,2304]{1,0:T(8,128)(2,1)}, bf16[6,384,768]{2,1,0:T(8,128)(2,1)}, f32[6,1,768]{2,1,0:T(1,128)}, bf16[...) custom-call(bf16[384,768]{1,0:T(8,128)(2,1)} %refs_9_.5, ...), custom_call_target="tpu_custom_call" | custom-call | flops 62899998720 | bytes 48082944 | tf_op jit(solution)/shard_map/pallas_call | solution.py:765
  143.8 25.0 %shard_map.307 = (bf16[384,768]{1,0:T(8,128)(2,1)}, f32[384,768]{1,0:T(8,128)}, bf16[768,192]{1,0:T(8,128)(2,1)}, f32[192,768]{1,0:T(8,128)}, f32[8,768]{1,0:T(8...) custom-call(s32[4]{0:T(128)} %pad_add_fusion.refs_0_, ...), custom_call_target="tpu_custom_call" | custom-call | flops 61199998976 | bytes 35392528 | tf_op jit(solution)/shard_map/pallas_call | solution.py:765
  169.4 7.0 %shard_map.308 = (bf16[384,768]{1,0:T(8,128)(2,1)}, bf16[384,768]{1,0:T(8,128)(2,1)}, bf16[768,192]{1,0:T(8,128)(2,1)}, f32[192,768]{1,0:T(8,128)}, f32[8,768]{1,0:T(8,128)}) custom-call(s32[4]{0:T(128)} %pad_add_fusion.refs_0_, f32[384,768]{1,0:T(8,128)} %get-tuple-element.130.refs_1_.refs_13_, bf16[16,16,48,768]{3,2,1,0:T(8,128)(2,1)} %bitcast.197, ...), custom_call_target="tpu_custom_call" | custom-call | flops 51000000512 | bytes 26222608 | tf_op jit(solution)/shard_map/pallas_call | solution.py:765
  183.8 21.5 %shard_map.309 = (f32[384,768]{1,0:T(8,128)}, f32[768,768]{1,0:T(8,128)}, f32[1,768]{1,0:T(1,128)}, bf16[2,2,4,4,48,384]{5,4,3,2,1,0:T(8,128)(2,1)}, bf16[2,2,4,4,48,384]{5,4,3,2,1,0:T(8,128)(2,1)}) custom-call(s32[4]{0:T(128)} %pad_add_fusion.refs_0_, bf16[384,768]{1,0:T(8,128)(2,1)} %get-tuple-element.140.refs_1_, bf16[16,16,48,768]{3,2,1,0:T(8,128)(2,1)} %bitcast.198, ...), custom_call_target="tpu_custom_call" | custom-call | flops 40800002048 | bytes 43103248 | tf_op jit(solution)/shard_map/pallas_call | solution.py:765
  205.4 2.7 collective-permute-done.14.refs_21_
  210.1 9.0 %shard_map.310 = (bf16[384,768]{1,0:T(8,128)(2,1)}, bf16[384,768]{1,0:T(8,128)(2,1)}, bf16[768,192]{1,0:T(8,128)(2,1)}, f32[192,768]{1,0:T(8,128)}, f32[8,768]{1...) custom-call(s32[4]{0:T(128)} %pad_add_fusion.refs_0_, ...), custom_call_target="tpu_custom_call" | custom-call | flops 51000000512 | bytes 44556304 | tf_op jit(solution)/shard_map/pallas_call | solution.py:765
  227.9 2.6 collective-permute-start.18
  234.6 16.6 %shard_map.311 = (f32[384,768]{1,0:T(8,128)}, f32[1,768]{1,0:T(1,128)}, bf16[2,2,4,4,48,384]{5,4,3,2,1,0:T(8,128)(2,1)}, bf16[2,2,4,4,48,384]{5,4,3,2,1,0:T(8,128)(2,1)}) custom-call(s32[4]{0:T(128)} %pad_add_fusion.refs_0_, bf16[384,768]{1,0:T(8,128)(2,1)} %get-tuple-element.165.refs_1_, bf16[16,16,48,768]{3,2,1,0:T(8,128)(2,1)} %bitcast.200, ...), custom_call_target="tpu_custom_call" | custom-call | flops 30599999488 | bytes 34255888 | tf_op jit(solution)/shard_map/pallas_call | solution.py:765
  254.4 3.9 %shard_map.312 = (bf16[4,4,48,384]{3,2,1,0:T(8,128)(2,1)}, bf16[4,48,768]{2,1,0:T(8,128)(2,1)}, bf16[4,48,768]{2,1,0:T(8,128)(2,1)}, bf16[4,48,768]{2,1,0:T(8,128)(2,1)}, bf16[4,48,768]{2,1,0:T(8,128)(2,1)}) custom-call(bf16[2,2,4,4,48,384]{5,4,3,2,1,0:T(8,128)(2,1)} %get-tuple-element.203.refs_0_, ...), custom_call_target="tpu_custom_call" | custom-call | flops 170000007168 | bytes 11796480 | tf_op jit(solution)/shard_map/pallas_call | solution.py:765
  258.3 2.6 fusion.3
  263.4 2.6 collective-permute-start.25
  268.6 3.5 shard_map.313
  274.5 10.9 %collective-permute-done.25.refs_2_ = bf16[4,48,768]{2,1,0:T(8,128)(2,1)} collective-permute-done((bf16[4,48,768]{2,1,0:T(8,128)(2,1)}, bf16[4,48,768]{2,1,0:T(8,128)(2,1)}, u32[]{:S(2)}, u32[]{:S(2)}) %collective-permute-start.25) | collective-permute-done | bytes 294944 | tf_op jit(solution)/shard_map/ppermute | solution.py:644
  285.4 3.1 collective-permute-done.27.refs_7_.refs_2_
  288.5 3.5 shard_map.314
  294.7 3.0 collective-permute-start.32
  313.8 2.5 shard_map.316
  321.9 2.7 collective-permute-start.39
  325.4 3.7 %shard_map.320 = (f32[48,3072]{1,0:T(8,128)}, f32[192,768]{1,0:T(8,128)}) custom-call(s32[4]{0:T(128)} %pad_add_fusion.refs_0_, bf16[6,48,768]{2,1,0:T(8,128)(2,1)} %get-tuple-element.236.refs_1_, bf16[6,48,768]{2,1,0:T(8,128)(2,1)} %copy-done.41), custom_call_target="tpu_custom_call" | custom-call | flops 170000007168 | bytes 2064400 | tf_op jit(solution)/shard_map/pallas_call | solution.py:765
  329.1 3.0 collective-permute-start.41
  342.6 3.7 %shard_map.319 = (f32[48,768]{1,0:T(8,128)}, f32[48,1536]{1,0:T(8,128)}, f32[48,768]{1,0:T(8,128)}) custom-call(s32[4]{0:T(128)} %pad_add_fusion.refs_0_, bf16[4,48,384]{2,1,0:T(8,128)(2,1)} %get-tuple-element.221.refs_1_, bf16[4,48,384]{2,1,0:T(8,128)(2,1)} %collective-permute-done.44.refs_2_), custom_call_target="tpu_custom_call" | custom-call | flops 170000007168 | bytes 884752 | tf_op jit(solution)/shard_map/pallas_call | solution.py:765
  346.6 3.3 shard_map.318
  (292 shorter events, 99.0 us)
Async XLA Ops:
  7.2 112.5 %all-gather.3.cloned.1.call-start = ((), (), s32[]{:S(2)}) async-start(), calls=%async_computation | async-start | bytes 20054016 | tf_op jit(solution)/shard_map/all_gather | solution.py:827
  33.2 10.3 %collective-permute-start.7 = (bf16[96,384]{1,0:T(8,128)(2,1)S(1)}, bf16[96,384]{1,0:T(8,128)(2,1)S(1)}, u32[]{:S(2)}, u32[]{:S(2)}) collective-permute-start(bf16[96,384]{1,0:T(8,128)(2,1)S(1)} %slice_select_fusion), channel_id=1, source_target_pairs={{0,8},{2,10},{4,12},{6,14},{8,16},{10,18},{12,20},{14,22},{16,24},... | collective-permute-start | bytes 221192 | tf_op jit(solution)/shard_map/ppermute | solution.py:644
  33.2 10.2 %collective-permute-start.6 = (bf16[96,384]{1,0:T(8,128)(2,1)S(1)}, bf16[96,384]{1,0:T(8,128)(2,1)S(1)}, u32[]{:S(2)}, u32[]{:S(2)}) collective-permute-start(bf16[96,384]{1,0:T(8,128)(2,1)S(1)} %slice_select_fusion), channel_id=1, source_target_pairs={{0,16},{2,18},{4,20},{6,22},{8,24},{10,26},{12,28},{14,30},{16,0},... | collective-permute-start | bytes 221192 | tf_op jit(solution)/shard_map/ppermute | solution.py:644
  43.7 15.7 %collective-permute-start.8 = (bf16[4,96,384]{2,1,0:T(8,128)(2,1)S(1)}, bf16[4,96,384]{2,1,0:T(8,128)(2,1)S(1)}, u32[]{:S(2)}, u32[]{:S(2)}) collective-permute-start(bf16[4,96,384]{2,1,0:T(8,128)(2,1)S(1)} %constant_dynamic-slice_fusion.1), channel_id=1, source_target_pairs={{0,4},{2,6},{4,0},{6,2},{8,12},{10,14},{12,8},{14,10},{16,20},{18,... | collective-permute-start | bytes 884744 | tf_op jit(solution)/shard_map/ppermute | solution.py:644
  62.1 28.2 %collective-permute-start.10 = (bf16[16,96,384]{2,1,0:T(8,128)(2,1)S(1)}, bf16[16,96,384]{2,1,0:T(8,128)(2,1)}, u32[]{:S(2)}, u32[]{:S(2)}) collective-permute-start(bf16[16,96,384]{2,1,0:T(8,128)(2,1)S(1)} %bitcast.159), channel_id=1, source_target_pairs={{0,1},{1,0},{2,3},{3,2},{4,5},{5,4},{6,7},{7,6},{8,9},{9,8},{10,11... | collective-permute-start | bytes 3538952 | tf_op jit(solution)/shard_map/ppermute | solution.py:644
  168.8 7.6 %collective-permute-start.11 = (bf16[2,2,4,4,48,384]{5,4,3,2,1,0:T(8,128)(2,1)}, bf16[2,2,4,4,48,384]{5,4,3,2,1,0:T(8,128)(2,1)S(1)}, u32[]{:S(2)}, u32[]{:S(2)}) collective-permute-start(bf16[2,2,4,4,48,384]{5,4,3,2,1,0:T(8,128)(2,1)} %get-tuple-element.135), channel_id=1, source_target_pairs={{0,2},{2,0},{4,6},{6,4},{8,10},{10,8},{12,14},{14,12},{16,18},{18,... | collective-permute-start | bytes 7077896 | tf_op jit(solution)/shard_map/ppermute | solution.py:644
  169.1 8.0 %collective-permute-start.12 = (bf16[2,4,4,48,768]{4,3,2,1,0:T(8,128)(2,1)}, bf16[2,4,4,48,768]{4,3,2,1,0:T(8,128)(2,1)}, u32[]{:S(2)}, u32[]{:S(2)}) collective-permute-start(bf16[2,4,4,48,768]{4,3,2,1,0:T(8,128)(2,1)} %get-tuple-element.136), channel_id=1, source_target_pairs={{0,2},{2,0},{4,6},{6,4},{8,10},{10,8},{12,14},{14,12},{16,18},{18,... | collective-permute-start | bytes 7077896 | tf_op jit(solution)/shard_map/ppermute | solution.py:644
  179.9 28.3 %collective-permute-start.14 = (bf16[4,4,48,768]{3,2,1,0:T(8,128)(2,1)S(1)}, bf16[4,4,48,768]{3,2,1,0:T(8,128)(2,1)}, u32[]{:S(2)}, u32[]{:S(2)}) collective-permute-start(bf16[4,4,48,768]{3,2,1,0:T(8,128)(2,1)S(1)} %fusion.1), channel_id=1, source_target_pairs={{0,4},{2,6},{4,0},{6,2},{8,12},{10,14},{12,8},{14,10},{16,20},{18,... | collective-permute-start | bytes 3538952 | tf_op jit(solution)/shard_map/ppermute | solution.py:644
  182.1 28.0 %collective-permute-start.13 = (bf16[2,4,4,48,384]{4,3,2,1,0:T(8,128)(2,1)S(1)}, bf16[2,4,4,48,384]{4,3,2,1,0:T(8,128)(2,1)}, u32[]{:S(2)}, u32[]{:S(2)}) collective-permute-start(bf16[2,4,4,48,384]{4,3,2,1,0:T(8,128)(2,1)S(1)} %fusion), channel_id=1, source_target_pairs={{0,1},{1,0},{2,3},{3,2},{4,5},{5,4},{6,7},{7,6},{8,9},{9,8},{10,11... | collective-permute-start | bytes 3538952 | tf_op jit(solution)/shard_map/ppermute | solution.py:644
  205.4 13.8 %collective-permute-start.16 = (bf16[2,2,4,4,48,384]{5,4,3,2,1,0:T(8,128)(2,1)}, bf16[2,2,4,4,48,384]{5,4,3,2,1,0:T(8,128)(2,1)}, u32[]{:S(2)}, u32[]{:S(2)}) collective-permute-start(bf16[2,2,4,4,48,384]{5,4,3,2,1,0:T(8,128)(2,1)} %get-tuple-element.162), channel_id=1, source_target_pairs={{0,2},{2,0},{4,6},{6,4},{8,10},{10,8},{12,14},{14,12},{16,18},{18,... | collective-permute-start | bytes 7077896 | tf_op jit(solution)/shard_map/ppermute | solution.py:644
  221.1 12.0 %collective-permute-start.17 = (bf16[4,48,768]{2,1,0:T(8,128)(2,1)}, bf16[4,48,768]{2,1,0:T(8,128)(2,1)S(1)}, u32[]{:S(2)}, u32[]{:S(2)}) collective-permute-start(bf16[4,48,768]{2,1,0:T(8,128)(2,1)} %get-tuple-element.179), channel_id=1, source_target_pairs={{0,8},{2,10},{4,12},{6,14},{8,16},{10,18},{12,20},{14,22},{16,24},... | collective-permute-start | bytes 884744 | tf_op jit(solution)/shard_map/ppermute | solution.py:644
  225.7 26.8 %collective-permute-start.21 = (bf16[4,2,48,768]{3,2,1,0:T(8,128)(2,1)S(1)}, bf16[4,2,48,768]{3,2,1,0:T(8,128)(2,1)S(1)}, u32[]{:S(2)}, u32[]{:S(2)}) collective-permute-start(bf16[4,2,48,768]{3,2,1,0:T(8,128)(2,1)S(1)} %fusion.5), channel_id=1, source_target_pairs={{0,4},{2,6},{4,0},{6,2},{8,12},{10,14},{12,8},{14,10},{16,20},{18,... | collective-permute-start | bytes 1769480 | tf_op jit(solution)/shard_map/ppermute | solution.py:644
  226.5 27.9 %collective-permute-start.20 = (bf16[2,4,4,48,384]{4,3,2,1,0:T(8,128)(2,1)S(1)}, bf16[2,4,4,48,384]{4,3,2,1,0:T(8,128)(2,1)}, u32[]{:S(2)}, u32[]{:S(2)}) collective-permute-start(bf16[2,4,4,48,384]{4,3,2,1,0:T(8,128)(2,1)S(1)} %fusion.2), channel_id=1, source_target_pairs={{0,1},{1,0},{2,3},{3,2},{4,5},{5,4},{6,7},{7,6},{8,9},{9,8},{10,11... | collective-permute-start | bytes 3538952 | tf_op jit(solution)/shard_map/ppermute | solution.py:644
  227.9 24.5 %collective-permute-start.18 = (bf16[4,48,768]{2,1,0:T(8,128)(2,1)}, bf16[4,48,768]{2,1,0:T(8,128)(2,1)}, u32[]{:S(2)}, u32[]{:S(2)}) collective-permute-start(bf16[4,48,768]{2,1,0:T(8,128)(2,1)} %get-tuple-element.180), channel_id=1, source_target_pairs={{0,16},{2,18},{4,20},{6,22},{8,24},{10,26},{12,28},{14,30},{16,0},... | collective-permute-start | bytes 884744 | tf_op jit(solution)/shard_map/ppermute | solution.py:644
  230.5 22.0 %collective-permute-start.19 = (bf16[4,48,768]{2,1,0:T(8,128)(2,1)}, bf16[4,48,768]{2,1,0:T(8,128)(2,1)}, u32[]{:S(2)}, u32[]{:S(2)}) collective-permute-start(bf16[4,48,768]{2,1,0:T(8,128)(2,1)} %get-tuple-element.181), channel_id=1, source_target_pairs={{0,24},{2,26},{4,28},{6,30},{8,0},{10,2},{12,4},{14,6},{16,8},{18,... | collective-permute-start | bytes 884744 | tf_op jit(solution)/shard_map/ppermute | solution.py:644
  233.1 20.8 %collective-permute-start.22 = (bf16[4,4,48,384]{3,2,1,0:T(8,128)(2,1)}, bf16[4,4,48,384]{3,2,1,0:T(8,128)(2,1)}, u32[]{:S(2)}, u32[]{:S(2)}) collective-permute-start(bf16[4,4,48,384]{3,2,1,0:T(8,128)(2,1)} %get-tuple-element.182), channel_id=1, source_target_pairs={{0,4},{2,6},{4,0},{6,2},{8,12},{10,14},{12,8},{14,10},{16,20},{18,... | collective-permute-start | bytes 1769480 | tf_op jit(solution)/shard_map/ppermute | solution.py:644
  260.9 27.6 %collective-permute-start.27 = (bf16[2,4,4,48,384]{4,3,2,1,0:T(8,128)(2,1)}, bf16[2,4,4,48,384]{4,3,2,1,0:T(8,128)(2,1)}, u32[]{:S(2)}, u32[]{:S(2)}) collective-permute-start(bf16[2,4,4,48,384]{4,3,2,1,0:T(8,128)(2,1)} %fusion.3), channel_id=1, source_target_pairs={{0,1},{1,0},{2,3},{3,2},{4,5},{5,4},{6,7},{7,6},{8,9},{9,8},{10,11... | collective-permute-start | bytes 3538952 | tf_op jit(solution)/shard_map/ppermute | solution.py:644
  262.4 12.2 %collective-permute-start.24 = (bf16[4,48,768]{2,1,0:T(8,128)(2,1)}, bf16[4,48,768]{2,1,0:T(8,128)(2,1)}, u32[]{:S(2)}, u32[]{:S(2)}) collective-permute-start(bf16[4,48,768]{2,1,0:T(8,128)(2,1)} %get-tuple-element.197), channel_id=1, source_target_pairs={{0,8},{2,10},{4,12},{6,14},{8,16},{10,18},{12,20},{14,22},{16,24},... | collective-permute-start | bytes 884744 | tf_op jit(solution)/shard_map/ppermute | solution.py:644
  263.4 22.0 %collective-permute-start.25 = (bf16[4,48,768]{2,1,0:T(8,128)(2,1)}, bf16[4,48,768]{2,1,0:T(8,128)(2,1)}, u32[]{:S(2)}, u32[]{:S(2)}) collective-permute-start(bf16[4,48,768]{2,1,0:T(8,128)(2,1)} %get-tuple-element.198), channel_id=1, source_target_pairs={{0,16},{2,18},{4,20},{6,22},{8,24},{10,26},{12,28},{14,30},{16,0},... | collective-permute-start | bytes 884744 | tf_op jit(solution)/shard_map/ppermute | solution.py:644
  265.9 19.5 %collective-permute-start.26 = (bf16[4,48,768]{2,1,0:T(8,128)(2,1)}, bf16[4,48,768]{2,1,0:T(8,128)(2,1)}, u32[]{:S(2)}, u32[]{:S(2)}) collective-permute-start(bf16[4,48,768]{2,1,0:T(8,128)(2,1)} %get-tuple-element.199), channel_id=1, source_target_pairs={{0,24},{2,26},{4,28},{6,30},{8,0},{10,2},{12,4},{14,6},{16,8},{18,... | collective-permute-start | bytes 884744 | tf_op jit(solution)/shard_map/ppermute | solution.py:644
  268.1 17.3 %collective-permute-start.28 = (bf16[4,4,48,384]{3,2,1,0:T(8,128)(2,1)}, bf16[4,4,48,384]{3,2,1,0:T(8,128)(2,1)}, u32[]{:S(2)}, u32[]{:S(2)}) collective-permute-start(bf16[4,4,48,384]{3,2,1,0:T(8,128)(2,1)} %get-tuple-element.210), channel_id=1, source_target_pairs={{0,4},{2,6},{4,0},{6,2},{8,12},{10,14},{12,8},{14,10},{16,20},{18,... | collective-permute-start | bytes 1769480 | tf_op jit(solution)/shard_map/ppermute | solution.py:644
  292.0 9.9 %collective-permute-start.29 = (bf16[2,48,768]{2,1,0:T(8,128)(2,1)}, bf16[2,48,768]{2,1,0:T(8,128)(2,1)S(1)}, u32[]{:S(2)}, u32[]{:S(2)}) collective-permute-start(bf16[2,48,768]{2,1,0:T(8,128)(2,1)} %get-tuple-element.211), channel_id=1, source_target_pairs={{0,1},{1,0},{2,3},{3,2},{4,5},{5,4},{6,7},{7,6},{8,9},{9,8},{10,11... | collective-permute-start | bytes 442376 | tf_op jit(solution)/shard_map/ppermute | solution.py:644
  294.7 17.2 %collective-permute-start.32 = (bf16[4,48,384]{2,1,0:T(8,128)(2,1)}, bf16[4,48,384]{2,1,0:T(8,128)(2,1)}, u32[]{:S(2)}, u32[]{:S(2)}) collective-permute-start(bf16[4,48,384]{2,1,0:T(8,128)(2,1)} %get-tuple-element.216), channel_id=1, source_target_pairs={{0,8},{2,10},{4,12},{6,14},{8,16},{10,18},{12,20},{14,22},{16,24},... | collective-permute-start | bytes 442376 | tf_op jit(solution)/shard_map/ppermute | solution.py:644
  297.7 14.3 %collective-permute-start.33 = (bf16[4,48,384]{2,1,0:T(8,128)(2,1)}, bf16[4,48,384]{2,1,0:T(8,128)(2,1)}, u32[]{:S(2)}, u32[]{:S(2)}) collective-permute-start(bf16[4,48,384]{2,1,0:T(8,128)(2,1)} %get-tuple-element.217), channel_id=1, source_target_pairs={{0,16},{2,18},{4,20},{6,22},{8,24},{10,26},{12,28},{14,30},{16,0},... | collective-permute-start | bytes 442376 | tf_op jit(solution)/shard_map/ppermute | solution.py:644
  299.6 12.4 %collective-permute-start.34 = (bf16[4,48,384]{2,1,0:T(8,128)(2,1)}, bf16[4,48,384]{2,1,0:T(8,128)(2,1)}, u32[]{:S(2)}, u32[]{:S(2)}) collective-permute-start(bf16[4,48,384]{2,1,0:T(8,128)(2,1)} %get-tuple-element.218), channel_id=1, source_target_pairs={{0,24},{2,26},{4,28},{6,30},{8,0},{10,2},{12,4},{14,6},{16,8},{18,... | collective-permute-start | bytes 442376 | tf_op jit(solution)/shard_map/ppermute | solution.py:644
  300.1 13.7 %collective-permute-start.35 = (bf16[4,4,48,384]{3,2,1,0:T(8,128)(2,1)}, bf16[4,4,48,384]{3,2,1,0:T(8,128)(2,1)}, u32[]{:S(2)}, u32[]{:S(2)}) collective-permute-start(bf16[4,4,48,384]{3,2,1,0:T(8,128)(2,1)} %get-tuple-element.220), channel_id=1, source_target_pairs={{0,4},{2,6},{4,0},{6,2},{8,12},{10,14},{12,8},{14,10},{16,20},{18,... | collective-permute-start | bytes 1769480 | tf_op jit(solution)/shard_map/ppermute | solution.py:644
  311.4 13.3 %collective-permute-start.45 = (bf16[6,48,768]{2,1,0:T(8,128)(2,1)S(1)}, bf16[6,48,768]{2,1,0:T(8,128)(2,1)S(1)}, u32[]{:S(2)}, u32[]{:S(2)}) collective-permute-start(bf16[6,48,768]{2,1,0:T(8,128)(2,1)S(1)} %copy-done.40), channel_id=1, source_target_pairs={{0,1},{1,0},{2,3},{3,2},{4,5},{5,4},{6,7},{7,6},{8,9},{9,8},{10,11... | collective-permute-start | bytes 1327112 | tf_op jit(solution)/shard_map/ppermute | solution.py:644
  319.6 23.0 %collective-permute-start.44 = (bf16[4,48,384]{2,1,0:T(8,128)(2,1)}, bf16[4,48,384]{2,1,0:T(8,128)(2,1)}, u32[]{:S(2)}, u32[]{:S(2)}) collective-permute-start(bf16[4,48,384]{2,1,0:T(8,128)(2,1)} %get-tuple-element.221.refs_1_), channel_id=1, source_target_pairs={{0,1},{1,0},{2,3},{3,2},{4,5},{5,4},{6,7},{7,6},{8,9},{9,8},{10,11... | collective-permute-start | bytes 442376 | tf_op jit(solution)/shard_map/ppermute | solution.py:644
  320.2 17.3 %collective-permute-start.40 = (bf16[4,48,384]{2,1,0:T(8,128)(2,1)}, bf16[4,48,384]{2,1,0:T(8,128)(2,1)}, u32[]{:S(2)}, u32[]{:S(2)}) collective-permute-start(bf16[4,48,384]{2,1,0:T(8,128)(2,1)} %get-tuple-element.224), channel_id=1, source_target_pairs={{0,8},{2,10},{4,12},{6,14},{8,16},{10,18},{12,20},{14,22},{16,24},... | collective-permute-start | bytes 442376 | tf_op jit(solution)/shard_map/ppermute | solution.py:644
  324.6 7.5 %collective-permute-start.38 = (f32[26,128]{1,0:T(8,128)}, f32[26,128]{1,0:T(8,128)}, u32[]{:S(2)}, u32[]{:S(2)}) collective-permute-start(f32[26,128]{1,0:T(8,128)} %add.110), channel_id=1, source_target_pairs={{0,16},{2,18},{4,20},{6,22},{8,24},{10,26},{12,28},{14,30},{16,0},... | collective-permute-start | bytes 39944 | tf_op jit(solution)/shard_map/ppermute | solution.py:644
  324.6 9.6 %collective-permute-start.37 = (f32[26,128]{1,0:T(8,128)}, f32[26,128]{1,0:T(8,128)}, u32[]{:S(2)}, u32[]{:S(2)}) collective-permute-start(f32[26,128]{1,0:T(8,128)} %add.110), channel_id=1, source_target_pairs={{0,8},{2,10},{4,12},{6,14},{8,16},{10,18},{12,20},{14,22},{16,24},... | collective-permute-start | bytes 39944 | tf_op jit(solution)/shard_map/ppermute | solution.py:644
  329.1 9.4 %collective-permute-start.41 = (bf16[4,48,384]{2,1,0:T(8,128)(2,1)S(1)}, bf16[4,48,384]{2,1,0:T(8,128)(2,1)S(1)}, u32[]{:S(2)}, u32[]{:S(2)}) collective-permute-start(bf16[4,48,384]{2,1,0:T(8,128)(2,1)S(1)} %copy-done.44), channel_id=1, source_target_pairs={{0,16},{2,18},{4,20},{6,22},{8,24},{10,26},{12,28},{14,30},{16,0},... | collective-permute-start | bytes 442376 | tf_op jit(solution)/shard_map/ppermute | solution.py:644
  (64 other events, 364.8 us)
Sparse Core Ops, SparseCore 0:
  11.6 108.1 all-gather.2

commit v3 on v2

--- a/solution.py
+++ b/solution.py
@@ -172,10 +172,11 @@
 
 def attend_forward(queries, keys, values, starts, cap, weights, scales, mixed):
     factor = math.log2(math.e) / 8.0
-    for p in range(mixed.shape[1] // 128):
+    queries, keys, values, cap = ready(queries, keys, values, cap)
+
+    def pair(p, _):
         query, key, value = (
-            ref[:, start + p * 128 : start + p * 128 + 128]
-            for ref, start in zip((queries, keys, values), starts)
+            ref[:, lanes(start + p * 128)] for ref, start in zip((queries, keys, values), starts)
         )
         limit = cap[...]
         scores = dot(key, sides(query.T)) * factor
@@ -187,7 +188,10 @@
         weights.leave(p, one_pair)
         scales[p] = scale
         found = own_sides(dot(value.T, powers) * scale)
-        mixed[:, p * 128 : p * 128 + 128] = found.T.astype(jnp.bfloat16)
+        mixed[:, lanes(p * 128)] = found.T.astype(jnp.bfloat16)
+        return 0
+
+    lax.fori_loop(0, mixed.shape[1] // 128, pair, 0, unroll=3)
     mixed.ship()
     scales.ship()
 
@@ -453,14 +457,17 @@
     if others:
         emit_made(place, [found[:3], others[:3], others[3:6]], found[3:5], found[-1])
         own, sent, *parts = found[5:-1]
-        for z in range(4):
-            sent[z] = low_sum(*(part[1, z] for part in others[6:9]))
+        half = others[6].shape[-1]
+        pairs = [(z, u, (z, u // 2, slice(None), slice((u & 1) * half, (u & 1) * half + half)))
+                 for z in range(4) for u in range(others[6].shape[2])]
+        for z, u, at in pairs:
+            sent[at] = low_sum(*(part[1, z, u] for part in others[6:9]))
         sent.ship()
         for z in range(4):
             parts[z][...] = low_sum(*(part[z] for part in others[9:]))
             parts[z].ship()
-        for z in range(4):
-            own[z] = low_sum(*(part[0, z] for part in others[6:9]))
+        for z, u, at in pairs:
+            own[at] = low_sum(*(part[0, z, u] for part in others[6:9]))
 
 
 def low_sum(*parts):
@@ -470,13 +477,11 @@
     return total.astype(jnp.bfloat16)
 
 
-def first_sums(kept_cross, got_cross, other_cross, kept_made, got_made, other_made, own_out, other_out, sent_cross, *parts):
-    half = other_out.shape[-1]
+def first_sums(kept_cross, got_cross, other_cross, kept_made, got_made, own_out, other_y, sent_cross, *parts):
+    units = own_out.shape[1]
     for z in range(4):
-        parts[z][:2] = low_sum(kept_made[z], got_made[z], other_made[z])
-        for u in range(4):
-            columns = slice((u & 1) * half, (u & 1) * half + half)
-            parts[z][2 + u // 2, :, columns] = low_sum(own_out[z, u], other_out[z, u])
+        parts[z][:2] = low_sum(kept_made[z], got_made[z], other_y[z, units:])
+        parts[z][2:] = low_sum(own_out[z], other_y[z, :units])
         parts[z].ship()
     for z in range(4):
         sent_cross[z] = low_sum(kept_cross[z], got_cross[z], other_cross[z])
@@ -491,11 +496,14 @@
 
 def second_sums(*refs):
     total_in, kept_self, got_self, other_self, own_cross, other_cross = refs[4:10]
-    totals, made, sent_self, *parts = refs[10:]
+    gains, totals, made, sent_self, *parts = refs[10:]
     for z in range(4):
         sent_self[z] = low_sum(kept_self[z], got_self[z], other_self[z])
     sent_self.ship()
-    made[...] = low_sum(*(ref[:2] for ref in refs[:4]))
+    made[:2] = low_sum(*(ref[:2] for ref in refs[:4]))
+    rows = gains.shape[0]
+    below = jnp.zeros((made.shape[1] - rows, made.shape[2]), jnp.float32)
+    made[2] = jnp.concatenate([gains[...], below], axis=0).astype(jnp.bfloat16)
     made.ship()
     for z in range(4):
         parts[z][...] = low_sum(own_cross[z], other_cross[z])
@@ -505,16 +513,6 @@
     totals[:units] = total_in[...]
 
 
-def feed_outs(place, total, other, out_in, out_out):
-    wide = total.shape[-1]
-    units, rows, half = out_in.shape[1] // wide, out_in.shape[0], wide // 2
-    for u in range(units):
-        out_in[:, u * wide : (u + 1) * wide] = total[u].astype(jnp.float32) + other[u].astype(jnp.float32)
-    for u in range(units):
-        at = (units + u // 2, slice(None), slice((u & 1) * half, (u & 1) * half + half))
-        join(place, total[at], other[at], out_out, slice(u * rows, (u + 1) * rows), 0)
-
-
 def join(place, own, other, out, rows, column):
     own, other = own.astype(jnp.float32), other.astype(jnp.float32)
     half = own.shape[-1]
@@ -522,20 +520,41 @@
     out[rows, column + half : column + 2 * half] = jnp.where(place[3] == 0, other, own)
 
 
-def unit_outs(place, total, other, *outs):
-    unit, wide = 0, 2 * total.shape[-1]
+def out_kernel(
+    place, total, other, total_self, other_self,
+    out_in, out_out, *outs,
+):
+    wide = total.shape[-1]
+    units, rows, half = out_in.shape[1] // wide, out_in.shape[0], wide // 2
+    for u in range(units):
+        out_in[:, u * wide : (u + 1) * wide] = total[u].astype(jnp.float32) + other[u].astype(jnp.float32)
+    out_in.ship()
+
+    def pair(ref, first, u):
+        return ref[first + u // 2, :, (u & 1) * half : (u & 1) * half + half]
+
+    for u in range(units):
+        join(place, pair(total, units, u), pair(other, units, u), out_out, slice(u * rows, (u + 1) * rows), 0)
+    out_out.ship()
+    first = units + units // 2
+    columns = [(pair(total, first, u), pair(other, first, u)) for u in range(4)]
+    columns += [(total_self[u], other_self[u]) for u in range(4)]
     for out in outs:
         for column in range(0, out.shape[1], wide):
-            join(place, total[unit], other[unit], out, slice(None), column)
-            unit += 1
+            join(place, *columns.pop(0), out, slice(None), column)
+        out.ship()
 
 
 def third_sums(*refs):
-    own_self, other_self, total_cross, *parts = refs[4:]
+    own_self, other_self, totals, both, *parts = refs[4:]
     for z in range(4):
         parts[z][...] = low_sum(own_self[z], other_self[z])
         parts[z].ship()
-    total_cross[...] = low_sum(*(ref[...] for ref in refs[:4]))
+    count, half = totals.shape[0], own_self.shape[-1]
+    for u in range(4):
+        at = (count + u // 2, slice(None), slice((u & 1) * half, (u & 1) * half + half))
+        both[at] = low_sum(*(ref[u] for ref in refs[:4]))
+    both[:count] = totals[...]
 
 
 def emit_made(place, made, outs, block):
@@ -634,6 +653,17 @@
     grad, gain_rows = rms_back(wide, rms_rate(wide), gains[0:1], total[...])
     grad_tokens[...] = grad_stream[...] + grad
     grad_gain[...] = jnp.sum(gain_rows, axis=0, keepdims=True)
+
+
+def pack_kernel(*refs):
+    shards, packed = refs[:-1], refs[-1]
+    rows, width = packed.shape[1:]
+    unit = 0
+    for shard in shards:
+        for row in range(0, shard.shape[0], rows):
+            for column in range(0, shard.shape[1], width):
+                packed[unit] = shard[row : row + rows, column : column + width]
+                unit += 1
 
 
 def sum_kernel(*refs):
@@ -822,8 +852,13 @@
     first = table_width + hyper_width
     whole_gains = jnp.transpose(small[:, first : first + 3, :gain_width], (1, 0, 2)).reshape(3, width)
     layer = [self_qkv, self_out, cross_query, cross_keyval, cross_out, feed_in]
-    layer = [units_of(w, width) for w in layer] + [feed_out.reshape(ff_units, unit, width)]
-    packed = jnp.concatenate([w.reshape(-1, width) for w in layer])
+    if ring:
+        shape = ((8 + 2 * ff_units, unit, width), jnp.bfloat16)
+        (packed,) = call(pack_kernel, (*layer, feed_out), [shape], [], 1)
+        packed = packed.reshape(-1, width)
+    else:
+        layer = [units_of(w, width) for w in layer] + [feed_out.reshape(ff_units, unit, width)]
+        packed = jnp.concatenate([w.reshape(-1, width) for w in layer])
     packed = lax.all_gather(packed, "fsdp", axis=0).reshape(devices, -1, unit, width)
     if not ring:
         first = jnp.transpose(packed[:, : 8 + ff_units], (1, 0, 2, 3)).reshape(-1, width, width)
@@ -981,7 +1016,7 @@
         got_cross = core_swap(grads_cross[0])
         others = (*made_two, *made_three, grads_out[1], got_out, other_out, grads_in[1], got_in, other_in)
         shapes = [((2, 4, 2, unit, width), low)] * 2
-        shapes += [((4, ff_units, unit, width // 2), low)] * 2 + [((ff_units, unit, width), low)] * 4
+        shapes += [((4, ff_units // 2, unit, width), low)] * 2 + [((ff_units, unit, width), low)] * 4
     grad_branch, grad_mixed, *made_one = branch_back(0, 3, grad_stream, branch1, squeezed1, others, shapes)
     if ring:
         sent_made, kept_made, own_out, sent_out, *parts_in = made_one[3:]
@@ -989,10 +1024,9 @@
         got_cross = after(got_cross, grad_mixed)
         sent_cross = add_low(grads_cross[1][1], got_cross[1])
         other_cross = x_swap(sent_cross)
-        sent_out, parts_in = after((sent_out, parts_in), sent_cross)
-        other_out, far_in = y_swap(sent_out), z_swaps(parts_in)
+        far_in = z_swaps(after(parts_in, sent_cross))
         sent_made = add_low(kept_made[1], after(got_made, sent_cross)[1])
-        other_made = y_swap(sent_made)
+        other_y = y_swap(jnp.concatenate([sent_out, sent_made], axis=1))
         grad_mixed = after(grad_mixed, sent_made)
     grad_tokens, grad_gain_one, *grads_self = call(
         self_kernel,
@@ -1005,7 +1039,7 @@
             pltpu.VMEM((rows, width), full),
             pltpu.SemaphoreType.DMA((3,)),
         ],
-        18 * busy,
+        busy,
         raw=(2,),
         split={4: pairs},
         parts={2: 4, 3: 4},
@@ -1027,16 +1061,16 @@
             + dot_nt(own_norm.astype(jnp.bfloat16), maker_norm)
         )
 
-    grad_gains = jnp.concatenate([grad_gain_one, grad_gain_two, grad_gain_three]).reshape(-1, 128)
+    grad_gains = jnp.concatenate([grad_gain_one, grad_gain_two, grad_gain_three])
     if ring:
         got_self = core_swap(grads_self[0])
-        flight = (far_in, other_cross, other_made, other_out)
-        far_in, other_cross, other_made, other_out = after(flight, grad_gain_one)
+        flight = (far_in, other_cross, other_y)
+        far_in, other_cross, other_y = after(flight, grad_gain_one)
         halves_y, column_half = ((4, 4, unit, width // 2), low), ((4, unit, width // 2), low)
         whole_part = ((4, unit, width), low)
         sent_cross, *parts = call(
             first_sums,
-            (grads_cross[1], got_cross, other_cross, kept_made, got_made, other_made, own_out, other_out),
+            (grads_cross[1], got_cross, other_cross, kept_made, got_made, own_out, other_y),
             [halves_y] + [whole_part] * 4,
             [],
             100 * busy,
@@ -1058,13 +1092,14 @@
         other_cross = y_swap(sent_cross)
         totals, total_made, sent_self, *parts = call(
             second_sums,
-            (parts[0], *far, total_in, grads_self[1], got_self, other_self, own_cross, other_cross),
-            [((6, unit, width), low), ((2, unit, width), low), halves_y] + [column_half] * 4,
+            (parts[0], *far, total_in, grads_self[1], got_self, other_self, own_cross, other_cross)
+            + (grad_gains,),
+            [((6, unit, width), low), ((3, unit, width), low), halves_y] + [column_half] * 4,
             [],
             5 * busy,
             views={5: (0, 1), 6: (0, 1), 7: (1,)},
         )
-        other_made, far, other_totals = x_swap(total_made), z_swaps(parts), x_swap(totals)
+        other_made, far = x_swap(total_made), z_swaps(parts)
         (own_self,) = call(
             kept_sums,
             (after(grads_self[1], other_made), got_self, other_self),
@@ -1074,31 +1109,32 @@
             views={0: (0, 0), 1: (0, 0), 2: (0,)},
         )
         other_self = y_swap(sent_self)
-        other_gains = x_swap(after(grad_gains, total_made))
         share_made = total_made.astype(jnp.float32) + other_made.astype(jnp.float32)
-        own_down, own_up, own_norm = own_made(share_made)
-        sums = jnp.concatenate([hidden_of(own_down, own_up, own_norm), grad_gains + other_gains])
+        own_down, own_up, own_norm = own_made(share_made[:2])
+        sums = jnp.concatenate(
+            [hidden_of(own_down, own_up, own_norm), share_made[2, :3].reshape(-1, 128)]
+        )
         sums = ring_step(sums, 1)
-        total_cross, *parts = call(
-            third_sums, (parts[0], *far, own_self, other_self), [column_half] * 5, [], 5 * busy
-        )
-        other_cross, far = x_swap(total_cross), z_swaps(parts)
-        sums = ring_step(after(sums, total_cross), 2)
-        shapes = [((unit, ff_units * width), full), ((ff_units * unit, width), full)]
-        out_feed_in, out_feed_out = call(
-            feed_outs, (here, totals, after(other_totals, sums)), shapes, [], 100 * busy
-        )
+        totals, *parts = call(
+            third_sums,
+            (parts[0], *far, own_self, other_self, totals),
+            [((8, unit, width), low)] + [column_half] * 4,
+            [],
+            5 * busy,
+        )
+        other_totals, far = x_swap(totals), z_swaps(parts)
+        sums = ring_step(after(sums, totals), 2)
         for part in z_swaps([sums] * 4):
             sums = sums + part
         far = after(far, sums)
         total_self = call(sum_kernel, (parts[0], *far), [column_half], [], 5 * busy)[0]
-        other_self, other_cross = x_swap(total_self), after(other_cross, total_self)
-        shapes = [((unit, count * width), full) for count in (1, 2, 1)]
-        out_query, out_keyval, out_cross_out = call(
-            unit_outs, (here, total_cross, other_cross), shapes, [], 100 * busy
-        )
-        shapes = [((unit, count * width), full) for count in (3, 1)]
-        out_qkv, out_self_out = call(unit_outs, (here, total_self, other_self), shapes, [], busy)
+        other_self = x_swap(total_self)
+        sums, own_down, own_up, own_norm = after((sums, own_down, own_up, own_norm), total_self)
+        shapes = [((unit, ff_units * width), full), ((ff_units * unit, width), full)]
+        shapes += [((unit, count * width), full) for count in (1, 2, 1, 3, 1)]
+        out_feed_in, out_feed_out, out_query, out_keyval, out_cross_out, out_qkv, out_self_out = call(
+            out_kernel, (here, totals, other_totals, total_self, other_self), shapes, [], busy
+        )
     else:
         share_in, share_out, share_cross, share_self = (
             share_of(grads, devices, grads is grads_out)
@@ -1123,7 +1159,7 @@
         own_down = jnp.transpose(own_down.reshape(down_rows, bottleneck, tasks), (2, 0, 1))
         own_down, own_up = own_down.reshape(tasks, down_span), own_up.reshape(tasks, down_span)
         own_norm = own_norm.reshape(tasks, norm_span)
-        sums = jnp.concatenate([hidden_of(own_down, own_up, own_norm), lax.psum(grad_gains, "dp")])
+        sums = jnp.concatenate([hidden_of(own_down, own_up, own_norm), lax.psum(grad_gains, "dp").reshape(-1, 128)])
         sums = lax.psum(sums, "fsdp")
     grad_hidden = sums[:tasks]
     out_gains = lax.dynamic_slice_in_dim(

time: 363 us -> 361 us (level)
  waiting for transfers between devices: 104 us -> 116 us
  Pallas kernels: 132 us -> 128 us
  starting transfers between devices: 57.6 us -> 53.9 us
    ppermute x46 -> x43, waiting for transfers between devices: 83.6 us -> 96.2 us  [swap(): return lax.ppermute(values, axis, [(i, mate(i)) for i in range(count)])]
    pallas_call x15 -> x14, Pallas kernels: 132 us -> 128 us  [call(): pl.pallas_call(body, out_shape=outs, in_specs=specs, out_specs=[pl.BlockS...]
    ppermute x46 -> x43, starting transfers between devices: 57.5 us -> 53.9 us  [swap(): return lax.ppermute(values, axis, [(i, mate(i)) for i in range(count)])]
  transfers between devices with their start and end apart: 47 -> 44, of which waited for: 23 -> 26; matrix products, arithmetic and copies ran while one was open for 10% -> 10% of each run, Pallas kernels for 21% -> 19%
where the time goes in v3:
time: 361 us; the launch traced here: 356 us
  Pallas kernels  128 us (35%)
  waiting for transfers between devices  116 us (32%)
  starting transfers between devices  53.9 us (15%)
  other arithmetic  19.9 us (6%)
  local copies, waits for them, and re-layouts  15.6 us (4%)
  between operations  15.2 us (4%)
  matrix products  8.01 us (2%)
    pallas_call x14, Pallas kernels, call(): pl.pallas_call(body, out_shape=outs, in_specs=specs, out_specs=[pl.BlockS...  128 us
    ppermute x43, waiting for transfers between devices, swap(): return lax.ppermute(values, axis, [(i, mate(i)) for i in range(count)])  96.2 us
    ppermute x43, starting transfers between devices, swap(): return lax.ppermute(values, axis, [(i, mate(i)) for i in range(count)])  53.9 us
    all_gather x1, waiting for transfers between devices, per_device(): lax.all_gather(packed, 'fsdp', axis=0).reshape(devices, -1, unit, width)  19.6 us
    convert_element_type x5, other arithmetic, add_low(): (left.astype(jnp.float32) + right.astype(jnp.float32)).astype(jnp.bfloat16)  8.37 us
  transfers between devices with their start and end apart: 44, of which 26 were waited for; matrix products, arithmetic and copies ran while one was open for 10% of the time, Pallas kernels for 19%

profile of v3, /device:TPU:0, one launch (start us, length us, event | category | flops | bytes accessed | tf_op | source)
XLA Modules:
  0.0 356.2 jit_solution(4185843251738368864)
XLA Ops:
  10.5 5.0 %collective-permute-start = (bf16[16,128]{1,0:T(8,128)(2,1)S(1)}, bf16[16,128]{1,0:T(8,128)(2,1)S(1)}, u32[]{:S(2)}, u32[]{:S(2)}) collective-permute-start(bf16[16,128]{1,0:T(8,128)(2,1)S(1)} %fusion.28), channel_id=1, source_target_pairs={{0,24},{2,26},{4,28},{6,30},{8,0},{10,2},{12,4},{14,6},{16,8},{18,... | collective-permute-start | bytes 12296 | tf_op jit(solution)/shard_map/ppermute | solution.py:674
  16.9 3.2 collective-permute-done.1
  22.7 2.5 collective-permute-done.3
  29.1 3.1 collective-permute-start.5
  32.9 3.6 %collective-permute-done.5 = bf16[96,384]{1,0:T(8,128)(2,1)S(1)} collective-permute-done((bf16[96,384]{1,0:T(8,128)(2,1)S(1)}, bf16[96,384]{1,0:T(8,128)(2,1)S(1)}, u32[]{:S(2)}, u32[]{:S(2)}) %collective-permute-start.5) | collective-permute-done | bytes 73760 | tf_op jit(solution)/shard_map/ppermute | solution.py:674
  36.5 6.0 %collective-permute-done.6 = bf16[96,384]{1,0:T(8,128)(2,1)S(1)} collective-permute-done((bf16[96,384]{1,0:T(8,128)(2,1)S(1)}, bf16[96,384]{1,0:T(8,128)(2,1)S(1)}, u32[]{:S(2)}, u32[]{:S(2)}) %collective-permute-start.6) | collective-permute-done | bytes 73760 | tf_op jit(solution)/shard_map/ppermute | solution.py:674
  44.3 14.1 %collective-permute-done.8 = bf16[4,96,384]{2,1,0:T(8,128)(2,1)S(1)} collective-permute-done((bf16[4,96,384]{2,1,0:T(8,128)(2,1)S(1)}, bf16[4,96,384]{2,1,0:T(8,128)(2,1)S(1)}, u32[]{:S(2)}, u32[]{:S(2)}) %collective-permute-start.8) | collective-permute-done | bytes 294944 | tf_op jit(solution)/shard_map/ppermute | solution.py:674
  67.1 22.2 %collective-permute-done.10 = bf16[16,96,384]{2,1,0:T(8,128)(2,1)} collective-permute-done((bf16[16,96,384]{2,1,0:T(8,128)(2,1)S(1)}, bf16[16,96,384]{2,1,0:T(8,128)(2,1)}, u32[]{:S(2)}, u32[]{:S(2)}) %collective-permute-start.10) | collective-permute-done | bytes 1179680 | tf_op jit(solution)/shard_map/ppermute | solution.py:674
  98.8 19.6 %all-gather.2.cloned.1.call-done = bf16[16,768,768]{2,1,0:T(8,128)(2,1)} async-done(((bf16[1,768,768]{2,1,0:T(8,128)(2,1)}), bf16[16,768,768]{2,1,0:T(8,128)(2,1)}) %all-gather.2.cloned.1.call-update) | async-done | bytes 18874384 | tf_op jit(solution)/shard_map/all_gather | solution.py:862
  118.4 24.5 %shard_map.307 = (bf16[384,768]{1,0:T(8,128)(2,1)}, bf16[384,2304]{1,0:T(8,128)(2,1)}, bf16[6,384,768]{2,1,0:T(8,128)(2,1)}, f32[6,1,768]{2,1,0:T(1,128)}, bf16[...) custom-call(bf16[384,768]{1,0:T(8,128)(2,1)} %refs_9_.5, ...), custom_call_target="tpu_custom_call" | custom-call | flops 62899998720 | bytes 48082944 | tf_op jit(solution)/shard_map/pallas_call | solution.py:795
  142.8 25.0 %shard_map.308 = (bf16[384,768]{1,0:T(8,128)(2,1)}, f32[384,768]{1,0:T(8,128)}, bf16[768,192]{1,0:T(8,128)(2,1)}, f32[192,768]{1,0:T(8,128)}, f32[8,768]{1,0:T(8...) custom-call(s32[4]{0:T(128)} %pad_add_fusion.refs_0_, ...), custom_call_target="tpu_custom_call" | custom-call | flops 61199998976 | bytes 35392528 | tf_op jit(solution)/shard_map/pallas_call | solution.py:795
  168.4 7.0 %shard_map.309 = (bf16[384,768]{1,0:T(8,128)(2,1)}, bf16[384,768]{1,0:T(8,128)(2,1)}, bf16[768,192]{1,0:T(8,128)(2,1)}, f32[192,768]{1,0:T(8,128)}, f32[8,768]{1,0:T(8,128)}) custom-call(s32[4]{0:T(128)} %pad_add_fusion.refs_0_, f32[384,768]{1,0:T(8,128)} %get-tuple-element.128.refs_1_.refs_13_, bf16[16,16,48,768]{3,2,1,0:T(8,128)(2,1)} %bitcast.149, ...), custom_call_target="tpu_custom_call" | custom-call | flops 51000000512 | bytes 26222608 | tf_op jit(solution)/shard_map/pallas_call | solution.py:795
  182.9 21.5 %shard_map.310 = (f32[384,768]{1,0:T(8,128)}, f32[768,768]{1,0:T(8,128)}, f32[1,768]{1,0:T(1,128)}, bf16[2,2,4,4,48,384]{5,4,3,2,1,0:T(8,128)(2,1)}, bf16[2,2,4,4,48,384]{5,4,3,2,1,0:T(8,128)(2,1)}) custom-call(s32[4]{0:T(128)} %pad_add_fusion.refs_0_, bf16[384,768]{1,0:T(8,128)(2,1)} %get-tuple-element.138.refs_1_, bf16[16,16,48,768]{3,2,1,0:T(8,128)(2,1)} %bitcast.150, ...), custom_call_target="tpu_custom_call" | custom-call | flops 40800002048 | bytes 43103248 | tf_op jit(solution)/shard_map/pallas_call | solution.py:795
  204.5 2.8 collective-permute-done.14.refs_21_
  209.1 9.0 %shard_map.311 = (bf16[384,768]{1,0:T(8,128)(2,1)}, bf16[384,768]{1,0:T(8,128)(2,1)}, bf16[768,192]{1,0:T(8,128)(2,1)}, f32[192,768]{1,0:T(8,128)}, f32[8,768]{1...) custom-call(s32[4]{0:T(128)} %pad_add_fusion.refs_0_, ...), custom_call_target="tpu_custom_call" | custom-call | flops 51000000512 | bytes 44556304 | tf_op jit(solution)/shard_map/pallas_call | solution.py:795
  226.6 2.7 collective-permute-start.18
  229.7 16.6 %shard_map.312 = (f32[384,768]{1,0:T(8,128)}, f32[1,768]{1,0:T(1,128)}, bf16[2,2,4,4,48,384]{5,4,3,2,1,0:T(8,128)(2,1)}, bf16[2,2,4,4,48,384]{5,4,3,2,1,0:T(8,128)(2,1)}) custom-call(s32[4]{0:T(128)} %pad_add_fusion.refs_0_, bf16[384,768]{1,0:T(8,128)(2,1)} %get-tuple-element.163.refs_1_, bf16[16,16,48,768]{3,2,1,0:T(8,128)(2,1)} %bitcast.152, ...), custom_call_target="tpu_custom_call" | custom-call | flops 1700000000 | bytes 34255888 | tf_op jit(solution)/shard_map/pallas_call | solution.py:795
  251.6 4.0 %shard_map.313 = (bf16[4,4,48,384]{3,2,1,0:T(8,128)(2,1)}, bf16[4,48,768]{2,1,0:T(8,128)(2,1)}, bf16[4,48,768]{2,1,0:T(8,128)(2,1)}, bf16[4,48,768]{2,1,0:T(8,128)(2,1)}, bf16[4,48,768]{2,1,0:T(8,128)(2,1)}) custom-call(bf16[2,2,4,4,48,384]{5,4,3,2,1,0:T(8,128)(2,1)} %get-tuple-element.199.refs_0_, ...), custom_call_target="tpu_custom_call" | custom-call | flops 170000007168 | bytes 11796480 | tf_op jit(solution)/shard_map/pallas_call | solution.py:795
  255.7 2.6 fusion.3
  259.7 2.9 collective-permute-start.23
  265.7 3.5 shard_map.314
  269.2 2.7 collective-permute-done.23.refs_1_
  271.9 10.3 %collective-permute-done.24.refs_2_ = bf16[4,48,768]{2,1,0:T(8,128)(2,1)} collective-permute-done((bf16[4,48,768]{2,1,0:T(8,128)(2,1)}, bf16[4,48,768]{2,1,0:T(8,128)(2,1)}, u32[]{:S(2)}, u32[]{:S(2)}) %collective-permute-start.24) | collective-permute-done | bytes 294944 | tf_op jit(solution)/shard_map/ppermute | solution.py:674
  282.2 3.2 collective-permute-done.26.refs_7_.refs_2_
  285.4 3.5 shard_map.315
  290.4 3.9 %collective-permute-start.30 = (bf16[4,48,384]{2,1,0:T(8,128)(2,1)}, bf16[4,48,384]{2,1,0:T(8,128)(2,1)}, u32[]{:S(2)}, u32[]{:S(2)}) collective-permute-start(bf16[4,48,384]{2,1,0:T(8,128)(2,1)} %get-tuple-element.210), channel_id=1, source_target_pairs={{0,8},{2,10},{4,12},{6,14},{8,16},{10,18},{12,20},{14,22},{16,24},... | collective-permute-start | bytes 442376 | tf_op jit(solution)/shard_map/ppermute | solution.py:674
  305.8 4.8 %collective-permute-done.33.refs_5_ = bf16[4,4,48,384]{3,2,1,0:T(8,128)(2,1)} collective-permute-done((bf16[4,4,48,384]{3,2,1,0:T(8,128)(2,1)}, bf16[4,4,48,384]{3,2,1,0:T(8,128)(2,1)}, u32[]{:S(2)}, u32[]{:S(2)}) %collective-permute-start.33) | collective-permute-done | bytes 589856 | tf_op jit(solution)/shard_map/ppermute | solution.py:674
  310.6 2.7 shard_map.317
  314.3 2.9 collective-permute-done.34
  322.0 2.6 collective-permute-start.38
  329.3 4.3 %collective-permute-done.39.refs_2_ = bf16[4,48,384]{2,1,0:T(8,128)(2,1)S(1)} collective-permute-done((bf16[4,48,384]{2,1,0:T(8,128)(2,1)}, bf16[4,48,384]{2,1,0:T(8,128)(2,1)S(1)}, u32[]{:S(2)}, u32[]{:S(2)}) %collective-permute-start.39) | collective-permute-done | bytes 147488 | tf_op jit(solution)/shard_map/ppermute | solution.py:674
  345.6 3.5 shard_map.319
  (265 shorter events, 95.1 us)
Async XLA Ops:
  7.2 111.2 %all-gather.2.cloned.1.call-start = ((), (), s32[]{:S(2)}) async-start(), calls=%async_computation | async-start | bytes 20054016 | tf_op jit(solution)/shard_map/all_gather | solution.py:862
  32.3 10.3 %collective-permute-start.7 = (bf16[96,384]{1,0:T(8,128)(2,1)S(1)}, bf16[96,384]{1,0:T(8,128)(2,1)S(1)}, u32[]{:S(2)}, u32[]{:S(2)}) collective-permute-start(bf16[96,384]{1,0:T(8,128)(2,1)S(1)} %slice_select_fusion), channel_id=1, source_target_pairs={{0,8},{2,10},{4,12},{6,14},{8,16},{10,18},{12,20},{14,22},{16,24},... | collective-permute-start | bytes 221192 | tf_op jit(solution)/shard_map/ppermute | solution.py:674
  32.3 10.2 %collective-permute-start.6 = (bf16[96,384]{1,0:T(8,128)(2,1)S(1)}, bf16[96,384]{1,0:T(8,128)(2,1)S(1)}, u32[]{:S(2)}, u32[]{:S(2)}) collective-permute-start(bf16[96,384]{1,0:T(8,128)(2,1)S(1)} %slice_select_fusion), channel_id=1, source_target_pairs={{0,16},{2,18},{4,20},{6,22},{8,24},{10,26},{12,28},{14,30},{16,0},... | collective-permute-start | bytes 221192 | tf_op jit(solution)/shard_map/ppermute | solution.py:674
  42.8 15.7 %collective-permute-start.8 = (bf16[4,96,384]{2,1,0:T(8,128)(2,1)S(1)}, bf16[4,96,384]{2,1,0:T(8,128)(2,1)S(1)}, u32[]{:S(2)}, u32[]{:S(2)}) collective-permute-start(bf16[4,96,384]{2,1,0:T(8,128)(2,1)S(1)} %constant_dynamic-slice_fusion.1), channel_id=1, source_target_pairs={{0,4},{2,6},{4,0},{6,2},{8,12},{10,14},{12,8},{14,10},{16,20},{18,... | collective-permute-start | bytes 884744 | tf_op jit(solution)/shard_map/ppermute | solution.py:674
  61.1 28.2 %collective-permute-start.10 = (bf16[16,96,384]{2,1,0:T(8,128)(2,1)S(1)}, bf16[16,96,384]{2,1,0:T(8,128)(2,1)}, u32[]{:S(2)}, u32[]{:S(2)}) collective-permute-start(bf16[16,96,384]{2,1,0:T(8,128)(2,1)S(1)} %bitcast.153), channel_id=1, source_target_pairs={{0,1},{1,0},{2,3},{3,2},{4,5},{5,4},{6,7},{7,6},{8,9},{9,8},{10,11... | collective-permute-start | bytes 3538952 | tf_op jit(solution)/shard_map/ppermute | solution.py:674
  167.8 7.6 %collective-permute-start.11 = (bf16[2,2,4,4,48,384]{5,4,3,2,1,0:T(8,128)(2,1)}, bf16[2,2,4,4,48,384]{5,4,3,2,1,0:T(8,128)(2,1)S(1)}, u32[]{:S(2)}, u32[]{:S(2)}) collective-permute-start(bf16[2,2,4,4,48,384]{5,4,3,2,1,0:T(8,128)(2,1)} %get-tuple-element.133), channel_id=1, source_target_pairs={{0,2},{2,0},{4,6},{6,4},{8,10},{10,8},{12,14},{14,12},{16,18},{18,... | collective-permute-start | bytes 7077896 | tf_op jit(solution)/shard_map/ppermute | solution.py:674
  168.2 8.0 %collective-permute-start.12 = (bf16[2,4,4,48,768]{4,3,2,1,0:T(8,128)(2,1)}, bf16[2,4,4,48,768]{4,3,2,1,0:T(8,128)(2,1)}, u32[]{:S(2)}, u32[]{:S(2)}) collective-permute-start(bf16[2,4,4,48,768]{4,3,2,1,0:T(8,128)(2,1)} %get-tuple-element.134), channel_id=1, source_target_pairs={{0,2},{2,0},{4,6},{6,4},{8,10},{10,8},{12,14},{14,12},{16,18},{18,... | collective-permute-start | bytes 7077896 | tf_op jit(solution)/shard_map/ppermute | solution.py:674
  178.9 28.3 %collective-permute-start.14 = (bf16[4,4,48,768]{3,2,1,0:T(8,128)(2,1)S(1)}, bf16[4,4,48,768]{3,2,1,0:T(8,128)(2,1)}, u32[]{:S(2)}, u32[]{:S(2)}) collective-permute-start(bf16[4,4,48,768]{3,2,1,0:T(8,128)(2,1)S(1)} %fusion.1), channel_id=1, source_target_pairs={{0,4},{2,6},{4,0},{6,2},{8,12},{10,14},{12,8},{14,10},{16,20},{18,... | collective-permute-start | bytes 3538952 | tf_op jit(solution)/shard_map/ppermute | solution.py:674
  181.1 28.0 %collective-permute-start.13 = (bf16[2,4,4,48,384]{4,3,2,1,0:T(8,128)(2,1)S(1)}, bf16[2,4,4,48,384]{4,3,2,1,0:T(8,128)(2,1)}, u32[]{:S(2)}, u32[]{:S(2)}) collective-permute-start(bf16[2,4,4,48,384]{4,3,2,1,0:T(8,128)(2,1)S(1)} %fusion), channel_id=1, source_target_pairs={{0,1},{1,0},{2,3},{3,2},{4,5},{5,4},{6,7},{7,6},{8,9},{9,8},{10,11... | collective-permute-start | bytes 3538952 | tf_op jit(solution)/shard_map/ppermute | solution.py:674
  204.4 13.8 %collective-permute-start.16 = (bf16[2,2,4,4,48,384]{5,4,3,2,1,0:T(8,128)(2,1)}, bf16[2,2,4,4,48,384]{5,4,3,2,1,0:T(8,128)(2,1)}, u32[]{:S(2)}, u32[]{:S(2)}) collective-permute-start(bf16[2,2,4,4,48,384]{5,4,3,2,1,0:T(8,128)(2,1)} %get-tuple-element.160), channel_id=1, source_target_pairs={{0,2},{2,0},{4,6},{6,4},{8,10},{10,8},{12,14},{14,12},{16,18},{18,... | collective-permute-start | bytes 7077896 | tf_op jit(solution)/shard_map/ppermute | solution.py:674
  222.3 28.1 %collective-permute-start.21 = (bf16[4,4,48,768]{3,2,1,0:T(8,128)(2,1)S(1)}, bf16[4,4,48,768]{3,2,1,0:T(8,128)(2,1)}, u32[]{:S(2)}, u32[]{:S(2)}) collective-permute-start(bf16[4,4,48,768]{3,2,1,0:T(8,128)(2,1)S(1)} %pad_maximum_fusion.1), channel_id=1, source_target_pairs={{0,4},{2,6},{4,0},{6,2},{8,12},{10,14},{12,8},{14,10},{16,20},{18,... | collective-permute-start | bytes 3538952 | tf_op jit(solution)/shard_map/ppermute | solution.py:674
  223.8 27.8 %collective-permute-start.20 = (bf16[2,4,4,48,384]{4,3,2,1,0:T(8,128)(2,1)S(1)}, bf16[2,4,4,48,384]{4,3,2,1,0:T(8,128)(2,1)}, u32[]{:S(2)}, u32[]{:S(2)}) collective-permute-start(bf16[2,4,4,48,384]{4,3,2,1,0:T(8,128)(2,1)S(1)} %fusion.2), channel_id=1, source_target_pairs={{0,1},{1,0},{2,3},{3,2},{4,5},{5,4},{6,7},{7,6},{8,9},{9,8},{10,11... | collective-permute-start | bytes 3538952 | tf_op jit(solution)/shard_map/ppermute | solution.py:674
  225.3 22.3 %collective-permute-start.17 = (bf16[4,48,768]{2,1,0:T(8,128)(2,1)}, bf16[4,48,768]{2,1,0:T(8,128)(2,1)S(1)}, u32[]{:S(2)}, u32[]{:S(2)}) collective-permute-start(bf16[4,48,768]{2,1,0:T(8,128)(2,1)} %get-tuple-element.176), channel_id=1, source_target_pairs={{0,8},{2,10},{4,12},{6,14},{8,16},{10,18},{12,20},{14,22},{16,24},... | collective-permute-start | bytes 884744 | tf_op jit(solution)/shard_map/ppermute | solution.py:674
  226.6 22.0 %collective-permute-start.18 = (bf16[4,48,768]{2,1,0:T(8,128)(2,1)}, bf16[4,48,768]{2,1,0:T(8,128)(2,1)}, u32[]{:S(2)}, u32[]{:S(2)}) collective-permute-start(bf16[4,48,768]{2,1,0:T(8,128)(2,1)} %get-tuple-element.177), channel_id=1, source_target_pairs={{0,16},{2,18},{4,20},{6,22},{8,24},{10,26},{12,28},{14,30},{16,0},... | collective-permute-start | bytes 884744 | tf_op jit(solution)/shard_map/ppermute | solution.py:674
  229.4 19.3 %collective-permute-start.19 = (bf16[4,48,768]{2,1,0:T(8,128)(2,1)S(1)}, bf16[4,48,768]{2,1,0:T(8,128)(2,1)}, u32[]{:S(2)}, u32[]{:S(2)}) collective-permute-start(bf16[4,48,768]{2,1,0:T(8,128)(2,1)S(1)} %copy-done.36), channel_id=1, source_target_pairs={{0,24},{2,26},{4,28},{6,30},{8,0},{10,2},{12,4},{14,6},{16,8},{18,... | collective-permute-start | bytes 884744 | tf_op jit(solution)/shard_map/ppermute | solution.py:674
  247.6 8.1 %collective-permute-start.22 = (bf16[2,2,4,4,48,384]{5,4,3,2,1,0:T(8,128)(2,1)}, bf16[2,2,4,4,48,384]{5,4,3,2,1,0:T(8,128)(2,1)}, u32[]{:S(2)}, u32[]{:S(2)}) collective-permute-start(bf16[2,2,4,4,48,384]{5,4,3,2,1,0:T(8,128)(2,1)} %get-tuple-element.190), channel_id=1, source_target_pairs={{0,2},{2,0},{4,6},{6,4},{8,10},{10,8},{12,14},{14,12},{16,18},{18,... | collective-permute-start | bytes 7077896 | tf_op jit(solution)/shard_map/ppermute | solution.py:674
  258.2 27.2 %collective-permute-start.26 = (bf16[2,4,4,48,384]{4,3,2,1,0:T(8,128)(2,1)}, bf16[2,4,4,48,384]{4,3,2,1,0:T(8,128)(2,1)}, u32[]{:S(2)}, u32[]{:S(2)}) collective-permute-start(bf16[2,4,4,48,384]{4,3,2,1,0:T(8,128)(2,1)} %fusion.3), channel_id=1, source_target_pairs={{0,1},{1,0},{2,3},{3,2},{4,5},{5,4},{6,7},{7,6},{8,9},{9,8},{10,11... | collective-permute-start | bytes 3538952 | tf_op jit(solution)/shard_map/ppermute | solution.py:674
  259.7 12.2 %collective-permute-start.23 = (bf16[4,48,768]{2,1,0:T(8,128)(2,1)}, bf16[4,48,768]{2,1,0:T(8,128)(2,1)}, u32[]{:S(2)}, u32[]{:S(2)}) collective-permute-start(bf16[4,48,768]{2,1,0:T(8,128)(2,1)} %get-tuple-element.193), channel_id=1, source_target_pairs={{0,8},{2,10},{4,12},{6,14},{8,16},{10,18},{12,20},{14,22},{16,24},... | collective-permute-start | bytes 884744 | tf_op jit(solution)/shard_map/ppermute | solution.py:674
  262.6 19.6 %collective-permute-start.24 = (bf16[4,48,768]{2,1,0:T(8,128)(2,1)}, bf16[4,48,768]{2,1,0:T(8,128)(2,1)}, u32[]{:S(2)}, u32[]{:S(2)}) collective-permute-start(bf16[4,48,768]{2,1,0:T(8,128)(2,1)} %get-tuple-element.194), channel_id=1, source_target_pairs={{0,16},{2,18},{4,20},{6,22},{8,24},{10,26},{12,28},{14,30},{16,0},... | collective-permute-start | bytes 884744 | tf_op jit(solution)/shard_map/ppermute | solution.py:674
  263.8 18.4 %collective-permute-start.25 = (bf16[4,48,768]{2,1,0:T(8,128)(2,1)}, bf16[4,48,768]{2,1,0:T(8,128)(2,1)}, u32[]{:S(2)}, u32[]{:S(2)}) collective-permute-start(bf16[4,48,768]{2,1,0:T(8,128)(2,1)} %get-tuple-element.195), channel_id=1, source_target_pairs={{0,24},{2,26},{4,28},{6,30},{8,0},{10,2},{12,4},{14,6},{16,8},{18,... | collective-permute-start | bytes 884744 | tf_op jit(solution)/shard_map/ppermute | solution.py:674
  265.2 17.1 %collective-permute-start.27 = (bf16[4,4,48,384]{3,2,1,0:T(8,128)(2,1)}, bf16[4,4,48,384]{3,2,1,0:T(8,128)(2,1)}, u32[]{:S(2)}, u32[]{:S(2)}) collective-permute-start(bf16[4,4,48,384]{3,2,1,0:T(8,128)(2,1)} %get-tuple-element.205), channel_id=1, source_target_pairs={{0,4},{2,6},{4,0},{6,2},{8,12},{10,14},{12,8},{14,10},{16,20},{18,... | collective-permute-start | bytes 1769480 | tf_op jit(solution)/shard_map/ppermute | solution.py:674
  288.9 8.6 %collective-permute-start.28 = (bf16[3,48,768]{2,1,0:T(8,128)(2,1)}, bf16[3,48,768]{2,1,0:T(8,128)(2,1)S(1)}, u32[]{:S(2)}, u32[]{:S(2)}) collective-permute-start(bf16[3,48,768]{2,1,0:T(8,128)(2,1)} %get-tuple-element.208), channel_id=1, source_target_pairs={{0,1},{1,0},{2,3},{3,2},{4,5},{5,4},{6,7},{7,6},{8,9},{9,8},{10,11... | collective-permute-start | bytes 663560 | tf_op jit(solution)/shard_map/ppermute | solution.py:674
  290.4 13.9 %collective-permute-start.30 = (bf16[4,48,384]{2,1,0:T(8,128)(2,1)}, bf16[4,48,384]{2,1,0:T(8,128)(2,1)}, u32[]{:S(2)}, u32[]{:S(2)}) collective-permute-start(bf16[4,48,384]{2,1,0:T(8,128)(2,1)} %get-tuple-element.210), channel_id=1, source_target_pairs={{0,8},{2,10},{4,12},{6,14},{8,16},{10,18},{12,20},{14,22},{16,24},... | collective-permute-start | bytes 442376 | tf_op jit(solution)/shard_map/ppermute | solution.py:674
  294.4 11.5 %collective-permute-start.31 = (bf16[4,48,384]{2,1,0:T(8,128)(2,1)}, bf16[4,48,384]{2,1,0:T(8,128)(2,1)}, u32[]{:S(2)}, u32[]{:S(2)}) collective-permute-start(bf16[4,48,384]{2,1,0:T(8,128)(2,1)} %get-tuple-element.211), channel_id=1, source_target_pairs={{0,16},{2,18},{4,20},{6,22},{8,24},{10,26},{12,28},{14,30},{16,0},... | collective-permute-start | bytes 442376 | tf_op jit(solution)/shard_map/ppermute | solution.py:674
  296.8 9.1 %collective-permute-start.32 = (bf16[4,48,384]{2,1,0:T(8,128)(2,1)}, bf16[4,48,384]{2,1,0:T(8,128)(2,1)}, u32[]{:S(2)}, u32[]{:S(2)}) collective-permute-start(bf16[4,48,384]{2,1,0:T(8,128)(2,1)} %get-tuple-element.212), channel_id=1, source_target_pairs={{0,24},{2,26},{4,28},{6,30},{8,0},{10,2},{12,4},{14,6},{16,8},{18,... | collective-permute-start | bytes 442376 | tf_op jit(solution)/shard_map/ppermute | solution.py:674
  296.8 13.9 %collective-permute-start.33 = (bf16[4,4,48,384]{3,2,1,0:T(8,128)(2,1)}, bf16[4,4,48,384]{3,2,1,0:T(8,128)(2,1)}, u32[]{:S(2)}, u32[]{:S(2)}) collective-permute-start(bf16[4,4,48,384]{3,2,1,0:T(8,128)(2,1)} %get-tuple-element.214), channel_id=1, source_target_pairs={{0,4},{2,6},{4,0},{6,2},{8,12},{10,14},{12,8},{14,10},{16,20},{18,... | collective-permute-start | bytes 1769480 | tf_op jit(solution)/shard_map/ppermute | solution.py:674
  317.2 7.4 %collective-permute-start.37 = (f32[26,128]{1,0:T(8,128)S(1)}, f32[26,128]{1,0:T(8,128)S(1)}, u32[]{:S(2)}, u32[]{:S(2)}) collective-permute-start(f32[26,128]{1,0:T(8,128)S(1)} %add.106), channel_id=1, source_target_pairs={{0,24},{2,26},{4,28},{6,30},{8,0},{10,2},{12,4},{14,6},{16,8},{18,... | collective-permute-start | bytes 39944 | tf_op jit(solution)/shard_map/ppermute | solution.py:674
  320.4 8.0 %collective-permute-start.35 = (f32[26,128]{1,0:T(8,128)S(1)}, f32[26,128]{1,0:T(8,128)S(1)}, u32[]{:S(2)}, u32[]{:S(2)}) collective-permute-start(f32[26,128]{1,0:T(8,128)S(1)} %add.106), channel_id=1, source_target_pairs={{0,8},{2,10},{4,12},{6,14},{8,16},{10,18},{12,20},{14,22},{16,24},... | collective-permute-start | bytes 39944 | tf_op jit(solution)/shard_map/ppermute | solution.py:674
  321.4 22.7 %collective-permute-start.41 = (bf16[8,48,768]{2,1,0:T(8,128)(2,1)}, bf16[8,48,768]{2,1,0:T(8,128)(2,1)S(1)}, u32[]{:S(2)}, u32[]{:S(2)}) collective-permute-start(bf16[8,48,768]{2,1,0:T(8,128)(2,1)} %get-tuple-element.216.refs_1_), channel_id=1, source_target_pairs={{0,1},{1,0},{2,3},{3,2},{4,5},{5,4},{6,7},{7,6},{8,9},{9,8},{10,11... | collective-permute-start | bytes 1769480 | tf_op jit(solution)/shard_map/ppermute | solution.py:674
  324.7 9.0 %collective-permute-start.39 = (bf16[4,48,384]{2,1,0:T(8,128)(2,1)}, bf16[4,48,384]{2,1,0:T(8,128)(2,1)S(1)}, u32[]{:S(2)}, u32[]{:S(2)}) collective-permute-start(bf16[4,48,384]{2,1,0:T(8,128)(2,1)} %get-tuple-element.220), channel_id=1, source_target_pairs={{0,16},{2,18},{4,20},{6,22},{8,24},{10,26},{12,28},{14,30},{16,0},... | collective-permute-start | bytes 442376 | tf_op jit(solution)/shard_map/ppermute | solution.py:674
  326.1 7.5 %collective-permute-start.40 = (bf16[4,48,384]{2,1,0:T(8,128)(2,1)}, bf16[4,48,384]{2,1,0:T(8,128)(2,1)S(1)}, u32[]{:S(2)}, u32[]{:S(2)}) collective-permute-start(bf16[4,48,384]{2,1,0:T(8,128)(2,1)} %get-tuple-element.221), channel_id=1, source_target_pairs={{0,24},{2,26},{4,28},{6,30},{8,0},{10,2},{12,4},{14,6},{16,8},{18,... | collective-permute-start | bytes 442376 | tf_op jit(solution)/shard_map/ppermute | solution.py:674
  336.3 7.8 %collective-permute-start.42 = (bf16[4,48,384]{2,1,0:T(8,128)(2,1)}, bf16[4,48,384]{2,1,0:T(8,128)(2,1)S(1)}, u32[]{:S(2)}, u32[]{:S(2)}) collective-permute-start(bf16[4,48,384]{2,1,0:T(8,128)(2,1)} %shard_map.318.refs_3_), channel_id=1, source_target_pairs={{0,1},{1,0},{2,3},{3,2},{4,5},{5,4},{6,7},{7,6},{8,9},{9,8},{10,11... | collective-permute-start | bytes 442376 | tf_op jit(solution)/shard_map/ppermute | solution.py:674
  (55 other events, 309.5 us)
Sparse Core Ops, SparseCore 0:
  10.2 108.1 all-gather.1

commit v4 on v3

--- a/solution.py
+++ b/solution.py
@@ -766,6 +766,7 @@
     if scalars:
         specs[0] = pl.BlockSpec(memory_space=pltpu.SMEM)
     outs = [jax.ShapeDtypeStruct(shape, dtype) for shape, dtype in shapes]
+    room = 20 if kernel in (kept_sums, sum_kernel, out_kernel) else 60
     buffers = [pltpu.VMEM(view_shape(operands[i].shape, views.get(i, ())), operands[i].dtype) for i in moved_in]
     buffers += [pltpu.VMEM(shape, dtype) for shape, dtype in shapes]
     buffers += [pltpu.SemaphoreType.DMA((split.get(i, 1),)) for i in moved_in]
@@ -798,7 +799,7 @@
         in_specs=specs,
         out_specs=[pl.BlockSpec(memory_space=pl.ANY) for _ in outs],
         scratch_shapes=list(scratch) + buffers,
-        compiler_params=pltpu.CompilerParams(vmem_limit_bytes=60 * 1024 * 1024),
+        compiler_params=pltpu.CompilerParams(vmem_limit_bytes=room * 1024 * 1024),
         cost_estimate=pl.CostEstimate(flops=flops, bytes_accessed=moved, transcendentals=0),
     )(*operands)
 
@@ -1061,6 +1062,9 @@
             + dot_nt(own_norm.astype(jnp.bfloat16), maker_norm)
         )
 
+    def hidden_outs(*made):
+        return [dot_tn(hidden, own.astype(jnp.bfloat16)) for own in made]
+
     grad_gains = jnp.concatenate([grad_gain_one, grad_gain_two, grad_gain_three])
     if ring:
         got_self = core_swap(grads_self[0])
@@ -1115,9 +1119,10 @@
             [hidden_of(own_down, own_up, own_norm), share_made[2, :3].reshape(-1, 128)]
         )
         sums = ring_step(sums, 1)
+        made_outs = hidden_outs(own_down, own_up, own_norm)
         totals, *parts = call(
             third_sums,
-            (parts[0], *far, own_self, other_self, totals),
+            (parts[0], *far, own_self, other_self, after(totals, made_outs)),
             [((8, unit, width), low)] + [column_half] * 4,
             [],
             5 * busy,
@@ -1129,7 +1134,7 @@
         far = after(far, sums)
         total_self = call(sum_kernel, (parts[0], *far), [column_half], [], 5 * busy)[0]
         other_self = x_swap(total_self)
-        sums, own_down, own_up, own_norm = after((sums, own_down, own_up, own_norm), total_self)
+        sums = after(sums, total_self)
         shapes = [((unit, ff_units * width), full), ((ff_units * unit, width), full)]
         shapes += [((unit, count * width), full) for count in (1, 2, 1, 3, 1)]
         out_feed_in, out_feed_out, out_query, out_keyval, out_cross_out, out_qkv, out_self_out = call(
@@ -1161,6 +1166,7 @@
         own_norm = own_norm.reshape(tasks, norm_span)
         sums = jnp.concatenate([hidden_of(own_down, own_up, own_norm), lax.psum(grad_gains, "dp").reshape(-1, 128)])
         sums = lax.psum(sums, "fsdp")
+        made_outs = hidden_outs(own_down, own_up, own_norm)
     grad_hidden = sums[:tasks]
     out_gains = lax.dynamic_slice_in_dim(
         sums[tasks:].reshape(3, width), place * gain_width, gain_width, 1
@@ -1171,9 +1177,7 @@
     out_table = exact_cols(grad_pre_hidden, own_hyper.astype(jnp.float32))
     own_pre = lax.dynamic_slice_in_dim(grad_pre_hidden, place * hyper_width, hyper_width, 1)
     out_hyper = exact_rows(whole_table.astype(jnp.float32), own_pre)
-    out_down, out_up, out_norm = (
-        dot_tn(hidden, own.astype(jnp.bfloat16)) for own in (own_down, own_up, own_norm)
-    )
+    out_down, out_up, out_norm = made_outs
     return (
         result.astype(jnp.bfloat16),
         grad_tokens,

time: 361 us -> 360 us (level)
  waiting for transfers between devices: 116 us -> 110 us
  local copies, waits for them, and re-layouts: 15.6 us -> 21.3 us
  Pallas kernels: 128 us -> 124 us
    unnamed x100 -> x112, local copies, waits for them, and re-layouts: 4.53 us -> 11 us
    ppermute x43, waiting for transfers between devices: 96.2 us -> 90.4 us  [swap(): return lax.ppermute(values, axis, [(i, mate(i)) for i in range(count)])]
    pallas_call x14, Pallas kernels: 128 us -> 124 us  [call(): pl.pallas_call(body, out_shape=outs, in_specs=specs, out_specs=[pl.BlockS...]
  transfers between devices with their start and end apart: 44 -> 44, of which waited for: 26 -> 25; matrix products, arithmetic and copies ran while one was open for 10% -> 10% of each run, Pallas kernels for 19% -> 18%
where the time goes in v4:
time: 360 us; the launch traced here: 355 us
  Pallas kernels  124 us (34%)
  waiting for transfers between devices  110 us (31%)
  starting transfers between devices  55.2 us (15%)
  local copies, waits for them, and re-layouts  21.3 us (6%)
  other arithmetic  20.7 us (6%)
  between operations  15.2 us (4%)
  matrix products  8.7 us (2%)
    pallas_call x14, Pallas kernels, call(): pl.pallas_call(body, out_shape=outs, in_specs=specs, out_specs=[pl.BlockS...  124 us
    ppermute x43, waiting for transfers between devices, swap(): return lax.ppermute(values, axis, [(i, mate(i)) for i in range(count)])  90.4 us
    ppermute x43, starting transfers between devices, swap(): return lax.ppermute(values, axis, [(i, mate(i)) for i in range(count)])  55.1 us
    all_gather x1, waiting for transfers between devices, per_device(): lax.all_gather(packed, 'fsdp', axis=0).reshape(devices, -1, unit, width)  19.6 us
    unnamed x112, local copies, waits for them, and re-layouts  11 us
    convert_element_type x5, other arithmetic, add_low(): (left.astype(jnp.float32) + right.astype(jnp.float32)).astype(jnp.bfloat16)  9.17 us
  transfers between devices with their start and end apart: 44, of which 25 were waited for; matrix products, arithmetic and copies ran while one was open for 10% of the time, Pallas kernels for 18%

profile of v4, /device:TPU:0, one launch (start us, length us, event | category | flops | bytes accessed | tf_op | source)
XLA Modules:
  0.0 354.9 jit_solution(5933494214218572517)
XLA Ops:
  7.2 2.5 shard_map.306
  10.5 5.0 %collective-permute-start = (bf16[16,128]{1,0:T(8,128)(2,1)S(1)}, bf16[16,128]{1,0:T(8,128)(2,1)S(1)}, u32[]{:S(2)}, u32[]{:S(2)}) collective-permute-start(bf16[16,128]{1,0:T(8,128)(2,1)S(1)} %fusion.24), channel_id=1, source_target_pairs={{0,24},{2,26},{4,28},{6,30},{8,0},{10,2},{12,4},{14,6},{16,8},{18,... | collective-permute-start | bytes 12296 | tf_op jit(solution)/shard_map/ppermute | solution.py:674
  16.9 3.2 collective-permute-done.1
  22.7 2.5 collective-permute-done.3
  29.1 3.1 collective-permute-start.5
  32.9 3.6 %collective-permute-done.5 = bf16[96,384]{1,0:T(8,128)(2,1)S(1)} collective-permute-done((bf16[96,384]{1,0:T(8,128)(2,1)S(1)}, bf16[96,384]{1,0:T(8,128)(2,1)S(1)}, u32[]{:S(2)}, u32[]{:S(2)}) %collective-permute-start.5) | collective-permute-done | bytes 73760 | tf_op jit(solution)/shard_map/ppermute | solution.py:674
  36.5 6.0 %collective-permute-done.6 = bf16[96,384]{1,0:T(8,128)(2,1)S(1)} collective-permute-done((bf16[96,384]{1,0:T(8,128)(2,1)S(1)}, bf16[96,384]{1,0:T(8,128)(2,1)S(1)}, u32[]{:S(2)}, u32[]{:S(2)}) %collective-permute-start.6) | collective-permute-done | bytes 73760 | tf_op jit(solution)/shard_map/ppermute | solution.py:674
  44.3 14.1 %collective-permute-done.8 = bf16[4,96,384]{2,1,0:T(8,128)(2,1)S(1)} collective-permute-done((bf16[4,96,384]{2,1,0:T(8,128)(2,1)S(1)}, bf16[4,96,384]{2,1,0:T(8,128)(2,1)S(1)}, u32[]{:S(2)}, u32[]{:S(2)}) %collective-permute-start.8) | collective-permute-done | bytes 294944 | tf_op jit(solution)/shard_map/ppermute | solution.py:674
  67.1 22.2 %collective-permute-done.10 = bf16[16,96,384]{2,1,0:T(8,128)(2,1)} collective-permute-done((bf16[16,96,384]{2,1,0:T(8,128)(2,1)S(1)}, bf16[16,96,384]{2,1,0:T(8,128)(2,1)}, u32[]{:S(2)}, u32[]{:S(2)}) %collective-permute-start.10) | collective-permute-done | bytes 1179680 | tf_op jit(solution)/shard_map/ppermute | solution.py:674
  94.5 2.5 reshape.183
  98.8 19.6 %all-gather.2.cloned.1.call-done = bf16[16,768,768]{2,1,0:T(8,128)(2,1)} async-done(((bf16[1,768,768]{2,1,0:T(8,128)(2,1)}), bf16[16,768,768]{2,1,0:T(8,128)(2,1)}) %all-gather.2.cloned.1.call-update) | async-done | bytes 18874384 | tf_op jit(solution)/shard_map/all_gather | solution.py:863
  118.4 24.5 %shard_map.307 = (bf16[384,768]{1,0:T(8,128)(2,1)}, bf16[384,2304]{1,0:T(8,128)(2,1)}, bf16[6,384,768]{2,1,0:T(8,128)(2,1)}, f32[6,1,768]{2,1,0:T(1,128)}, bf16[...) custom-call(bf16[384,768]{1,0:T(8,128)(2,1)} %refs_9_.5, ...), custom_call_target="tpu_custom_call" | custom-call | flops 62899998720 | bytes 48082944 | tf_op jit(solution)/shard_map/pallas_call | solution.py:796
  142.9 25.0 %shard_map.308 = (bf16[384,768]{1,0:T(8,128)(2,1)}, f32[384,768]{1,0:T(8,128)}, bf16[768,192]{1,0:T(8,128)(2,1)}, f32[192,768]{1,0:T(8,128)}, f32[8,768]{1,0:T(8...) custom-call(s32[4]{0:T(128)} %pad_add_fusion.refs_0_, ...), custom_call_target="tpu_custom_call" | custom-call | flops 61199998976 | bytes 35392528 | tf_op jit(solution)/shard_map/pallas_call | solution.py:796
  168.5 7.0 %shard_map.309 = (bf16[384,768]{1,0:T(8,128)(2,1)}, bf16[384,768]{1,0:T(8,128)(2,1)}, bf16[768,192]{1,0:T(8,128)(2,1)}, f32[192,768]{1,0:T(8,128)}, f32[8,768]{1,0:T(8,128)}) custom-call(s32[4]{0:T(128)} %pad_add_fusion.refs_0_, f32[384,768]{1,0:T(8,128)} %get-tuple-element.126.refs_1_.refs_13_, bf16[16,16,48,768]{3,2,1,0:T(8,128)(2,1)} %bitcast.146, ...), custom_call_target="tpu_custom_call" | custom-call | flops 51000000512 | bytes 26222608 | tf_op jit(solution)/shard_map/pallas_call | solution.py:796
  183.0 21.5 %shard_map.310 = (f32[384,768]{1,0:T(8,128)}, f32[768,768]{1,0:T(8,128)}, f32[1,768]{1,0:T(1,128)}, bf16[2,2,4,4,48,384]{5,4,3,2,1,0:T(8,128)(2,1)}, bf16[2,2,4,4,48,384]{5,4,3,2,1,0:T(8,128)(2,1)}) custom-call(s32[4]{0:T(128)} %pad_add_fusion.refs_0_, bf16[384,768]{1,0:T(8,128)(2,1)} %get-tuple-element.136.refs_1_, bf16[16,16,48,768]{3,2,1,0:T(8,128)(2,1)} %bitcast.147, ...), custom_call_target="tpu_custom_call" | custom-call | flops 40800002048 | bytes 43103248 | tf_op jit(solution)/shard_map/pallas_call | solution.py:796
  204.6 2.7 collective-permute-done.14.refs_21_
  209.2 9.1 %shard_map.311 = (bf16[384,768]{1,0:T(8,128)(2,1)}, bf16[384,768]{1,0:T(8,128)(2,1)}, bf16[768,192]{1,0:T(8,128)(2,1)}, f32[192,768]{1,0:T(8,128)}, f32[8,768]{1...) custom-call(s32[4]{0:T(128)} %pad_add_fusion.refs_0_, ...), custom_call_target="tpu_custom_call" | custom-call | flops 51000000512 | bytes 44556304 | tf_op jit(solution)/shard_map/pallas_call | solution.py:796
  218.5 2.7 fusion.2
  226.8 2.7 collective-permute-start.18
  229.9 16.4 %shard_map.312 = (f32[384,768]{1,0:T(8,128)}, f32[1,768]{1,0:T(1,128)}, bf16[2,2,4,4,48,384]{5,4,3,2,1,0:T(8,128)(2,1)}, bf16[2,2,4,4,48,384]{5,4,3,2,1,0:T(8,128)(2,1)}) custom-call(s32[4]{0:T(128)} %pad_add_fusion.refs_0_, bf16[384,768]{1,0:T(8,128)(2,1)} %get-tuple-element.161.refs_1_, bf16[16,16,48,768]{3,2,1,0:T(8,128)(2,1)} %bitcast.149, ...), custom_call_target="tpu_custom_call" | custom-call | flops 1700000000 | bytes 34255888 | tf_op jit(solution)/shard_map/pallas_call | solution.py:796
  253.5 4.0 %shard_map.313 = (bf16[4,4,48,384]{3,2,1,0:T(8,128)(2,1)}, bf16[4,48,768]{2,1,0:T(8,128)(2,1)}, bf16[4,48,768]{2,1,0:T(8,128)(2,1)}, bf16[4,48,768]{2,1,0:T(8,128)(2,1)}, bf16[4,48,768]{2,1,0:T(8,128)(2,1)}) custom-call(bf16[2,2,4,4,48,384]{5,4,3,2,1,0:T(8,128)(2,1)} %get-tuple-element.197.refs_0_, ...), custom_call_target="tpu_custom_call" | custom-call | flops 170000007168 | bytes 11796480 | tf_op jit(solution)/shard_map/pallas_call | solution.py:796
  257.6 2.7 fusion.3
  261.8 3.4 collective-permute-start.23
  274.6 10.5 %collective-permute-done.24.refs_2_ = bf16[4,48,768]{2,1,0:T(8,128)(2,1)} collective-permute-done((bf16[4,48,768]{2,1,0:T(8,128)(2,1)}, bf16[4,48,768]{2,1,0:T(8,128)(2,1)}, u32[]{:S(2)}, u32[]{:S(2)}) %collective-permute-start.24) | collective-permute-done | bytes 294944 | tf_op jit(solution)/shard_map/ppermute | solution.py:674
  285.1 3.1 collective-permute-done.26.refs_7_.refs_2_
  288.2 3.5 shard_map.315
  293.2 3.8 %collective-permute-start.30 = (bf16[4,48,384]{2,1,0:T(8,128)(2,1)}, bf16[4,48,384]{2,1,0:T(8,128)(2,1)}, u32[]{:S(2)}, u32[]{:S(2)}) collective-permute-start(bf16[4,48,384]{2,1,0:T(8,128)(2,1)} %get-tuple-element.208), channel_id=1, source_target_pairs={{0,8},{2,10},{4,12},{6,14},{8,16},{10,18},{12,20},{14,22},{16,24},... | collective-permute-start | bytes 442376 | tf_op jit(solution)/shard_map/ppermute | solution.py:674
  314.0 2.7 shard_map.317
  324.5 2.9 collective-permute-start.38
  329.8 3.7 %collective-permute-done.38.refs_1_ = bf16[4,48,384]{2,1,0:T(8,128)(2,1)S(1)} collective-permute-done((bf16[4,48,384]{2,1,0:T(8,128)(2,1)}, bf16[4,48,384]{2,1,0:T(8,128)(2,1)S(1)}, u32[]{:S(2)}, u32[]{:S(2)}) %collective-permute-start.38) | collective-permute-done | bytes 147488 | tf_op jit(solution)/shard_map/ppermute | solution.py:674
  333.4 4.0 %collective-permute-done.39.refs_2_ = bf16[4,48,384]{2,1,0:T(8,128)(2,1)S(1)} collective-permute-done((bf16[4,48,384]{2,1,0:T(8,128)(2,1)}, bf16[4,48,384]{2,1,0:T(8,128)(2,1)S(1)}, u32[]{:S(2)}, u32[]{:S(2)}) %collective-permute-start.39) | collective-permute-done | bytes 147488 | tf_op jit(solution)/shard_map/ppermute | solution.py:674
  345.1 2.7 shard_map.319
  (275 shorter events, 96.5 us)
Async XLA Ops:
  7.2 111.2 %all-gather.2.cloned.1.call-start = ((), (), s32[]{:S(2)}) async-start(), calls=%async_computation | async-start | bytes 20054016 | tf_op jit(solution)/shard_map/all_gather | solution.py:863
  29.1 7.3 %collective-permute-start.5 = (bf16[96,384]{1,0:T(8,128)(2,1)S(1)}, bf16[96,384]{1,0:T(8,128)(2,1)S(1)}, u32[]{:S(2)}, u32[]{:S(2)}) collective-permute-start(bf16[96,384]{1,0:T(8,128)(2,1)S(1)} %slice_select_fusion), channel_id=1, source_target_pairs={{0,24},{2,26},{4,28},{6,30},{8,0},{10,2},{12,4},{14,6},{16,8},{18,... | collective-permute-start | bytes 221192 | tf_op jit(solution)/shard_map/ppermute | solution.py:674
  32.3 10.3 %collective-permute-start.7 = (bf16[96,384]{1,0:T(8,128)(2,1)S(1)}, bf16[96,384]{1,0:T(8,128)(2,1)S(1)}, u32[]{:S(2)}, u32[]{:S(2)}) collective-permute-start(bf16[96,384]{1,0:T(8,128)(2,1)S(1)} %slice_select_fusion), channel_id=1, source_target_pairs={{0,8},{2,10},{4,12},{6,14},{8,16},{10,18},{12,20},{14,22},{16,24},... | collective-permute-start | bytes 221192 | tf_op jit(solution)/shard_map/ppermute | solution.py:674
  32.3 10.2 %collective-permute-start.6 = (bf16[96,384]{1,0:T(8,128)(2,1)S(1)}, bf16[96,384]{1,0:T(8,128)(2,1)S(1)}, u32[]{:S(2)}, u32[]{:S(2)}) collective-permute-start(bf16[96,384]{1,0:T(8,128)(2,1)S(1)} %slice_select_fusion), channel_id=1, source_target_pairs={{0,16},{2,18},{4,20},{6,22},{8,24},{10,26},{12,28},{14,30},{16,0},... | collective-permute-start | bytes 221192 | tf_op jit(solution)/shard_map/ppermute | solution.py:674
  42.8 15.7 %collective-permute-start.8 = (bf16[4,96,384]{2,1,0:T(8,128)(2,1)S(1)}, bf16[4,96,384]{2,1,0:T(8,128)(2,1)S(1)}, u32[]{:S(2)}, u32[]{:S(2)}) collective-permute-start(bf16[4,96,384]{2,1,0:T(8,128)(2,1)S(1)} %constant_dynamic-slice_fusion.1), channel_id=1, source_target_pairs={{0,4},{2,6},{4,0},{6,2},{8,12},{10,14},{12,8},{14,10},{16,20},{18,... | collective-permute-start | bytes 884744 | tf_op jit(solution)/shard_map/ppermute | solution.py:674
  61.1 28.2 %collective-permute-start.10 = (bf16[16,96,384]{2,1,0:T(8,128)(2,1)S(1)}, bf16[16,96,384]{2,1,0:T(8,128)(2,1)}, u32[]{:S(2)}, u32[]{:S(2)}) collective-permute-start(bf16[16,96,384]{2,1,0:T(8,128)(2,1)S(1)} %bitcast.150), channel_id=1, source_target_pairs={{0,1},{1,0},{2,3},{3,2},{4,5},{5,4},{6,7},{7,6},{8,9},{9,8},{10,11... | collective-permute-start | bytes 3538952 | tf_op jit(solution)/shard_map/ppermute | solution.py:674
  167.9 7.6 %collective-permute-start.11 = (bf16[2,2,4,4,48,384]{5,4,3,2,1,0:T(8,128)(2,1)}, bf16[2,2,4,4,48,384]{5,4,3,2,1,0:T(8,128)(2,1)S(1)}, u32[]{:S(2)}, u32[]{:S(2)}) collective-permute-start(bf16[2,2,4,4,48,384]{5,4,3,2,1,0:T(8,128)(2,1)} %get-tuple-element.131), channel_id=1, source_target_pairs={{0,2},{2,0},{4,6},{6,4},{8,10},{10,8},{12,14},{14,12},{16,18},{18,... | collective-permute-start | bytes 7077896 | tf_op jit(solution)/shard_map/ppermute | solution.py:674
  168.2 8.0 %collective-permute-start.12 = (bf16[2,4,4,48,768]{4,3,2,1,0:T(8,128)(2,1)}, bf16[2,4,4,48,768]{4,3,2,1,0:T(8,128)(2,1)}, u32[]{:S(2)}, u32[]{:S(2)}) collective-permute-start(bf16[2,4,4,48,768]{4,3,2,1,0:T(8,128)(2,1)} %get-tuple-element.132), channel_id=1, source_target_pairs={{0,2},{2,0},{4,6},{6,4},{8,10},{10,8},{12,14},{14,12},{16,18},{18,... | collective-permute-start | bytes 7077896 | tf_op jit(solution)/shard_map/ppermute | solution.py:674
  179.0 28.3 %collective-permute-start.14 = (bf16[4,4,48,768]{3,2,1,0:T(8,128)(2,1)S(1)}, bf16[4,4,48,768]{3,2,1,0:T(8,128)(2,1)}, u32[]{:S(2)}, u32[]{:S(2)}) collective-permute-start(bf16[4,4,48,768]{3,2,1,0:T(8,128)(2,1)S(1)} %fusion.1), channel_id=1, source_target_pairs={{0,4},{2,6},{4,0},{6,2},{8,12},{10,14},{12,8},{14,10},{16,20},{18,... | collective-permute-start | bytes 3538952 | tf_op jit(solution)/shard_map/ppermute | solution.py:674
  181.2 28.0 %collective-permute-start.13 = (bf16[2,4,4,48,384]{4,3,2,1,0:T(8,128)(2,1)S(1)}, bf16[2,4,4,48,384]{4,3,2,1,0:T(8,128)(2,1)}, u32[]{:S(2)}, u32[]{:S(2)}) collective-permute-start(bf16[2,4,4,48,384]{4,3,2,1,0:T(8,128)(2,1)S(1)} %fusion), channel_id=1, source_target_pairs={{0,1},{1,0},{2,3},{3,2},{4,5},{5,4},{6,7},{7,6},{8,9},{9,8},{10,11... | collective-permute-start | bytes 3538952 | tf_op jit(solution)/shard_map/ppermute | solution.py:674
  204.5 13.9 %collective-permute-start.16 = (bf16[2,2,4,4,48,384]{5,4,3,2,1,0:T(8,128)(2,1)}, bf16[2,2,4,4,48,384]{5,4,3,2,1,0:T(8,128)(2,1)}, u32[]{:S(2)}, u32[]{:S(2)}) collective-permute-start(bf16[2,2,4,4,48,384]{5,4,3,2,1,0:T(8,128)(2,1)} %get-tuple-element.158), channel_id=1, source_target_pairs={{0,2},{2,0},{4,6},{6,4},{8,10},{10,8},{12,14},{14,12},{16,18},{18,... | collective-permute-start | bytes 7077896 | tf_op jit(solution)/shard_map/ppermute | solution.py:674
  222.5 28.7 %collective-permute-start.21 = (bf16[4,4,48,768]{3,2,1,0:T(8,128)(2,1)S(1)}, bf16[4,4,48,768]{3,2,1,0:T(8,128)(2,1)}, u32[]{:S(2)}, u32[]{:S(2)}) collective-permute-start(bf16[4,4,48,768]{3,2,1,0:T(8,128)(2,1)S(1)} %pad_maximum_fusion.1), channel_id=1, source_target_pairs={{0,4},{2,6},{4,0},{6,2},{8,12},{10,14},{12,8},{14,10},{16,20},{18,... | collective-permute-start | bytes 3538952 | tf_op jit(solution)/shard_map/ppermute | solution.py:674
  224.0 28.5 %collective-permute-start.20 = (bf16[2,4,4,48,384]{4,3,2,1,0:T(8,128)(2,1)}, bf16[2,4,4,48,384]{4,3,2,1,0:T(8,128)(2,1)S(1)}, u32[]{:S(2)}, u32[]{:S(2)}) collective-permute-start(bf16[2,4,4,48,384]{4,3,2,1,0:T(8,128)(2,1)} %fusion.2), channel_id=1, source_target_pairs={{0,1},{1,0},{2,3},{3,2},{4,5},{5,4},{6,7},{7,6},{8,9},{9,8},{10,11... | collective-permute-start | bytes 3538952 | tf_op jit(solution)/shard_map/ppermute | solution.py:674
  225.5 22.2 %collective-permute-start.17 = (bf16[4,48,768]{2,1,0:T(8,128)(2,1)}, bf16[4,48,768]{2,1,0:T(8,128)(2,1)S(1)}, u32[]{:S(2)}, u32[]{:S(2)}) collective-permute-start(bf16[4,48,768]{2,1,0:T(8,128)(2,1)} %get-tuple-element.174), channel_id=1, source_target_pairs={{0,8},{2,10},{4,12},{6,14},{8,16},{10,18},{12,20},{14,22},{16,24},... | collective-permute-start | bytes 884744 | tf_op jit(solution)/shard_map/ppermute | solution.py:674
  226.8 22.5 %collective-permute-start.18 = (bf16[4,48,768]{2,1,0:T(8,128)(2,1)}, bf16[4,48,768]{2,1,0:T(8,128)(2,1)S(1)}, u32[]{:S(2)}, u32[]{:S(2)}) collective-permute-start(bf16[4,48,768]{2,1,0:T(8,128)(2,1)} %get-tuple-element.175), channel_id=1, source_target_pairs={{0,16},{2,18},{4,20},{6,22},{8,24},{10,26},{12,28},{14,30},{16,0},... | collective-permute-start | bytes 884744 | tf_op jit(solution)/shard_map/ppermute | solution.py:674
  229.6 20.5 %collective-permute-start.19 = (bf16[4,48,768]{2,1,0:T(8,128)(2,1)}, bf16[4,48,768]{2,1,0:T(8,128)(2,1)S(1)}, u32[]{:S(2)}, u32[]{:S(2)}) collective-permute-start(bf16[4,48,768]{2,1,0:T(8,128)(2,1)} %get-tuple-element.176), channel_id=1, source_target_pairs={{0,24},{2,26},{4,28},{6,30},{8,0},{10,2},{12,4},{14,6},{16,8},{18,... | collective-permute-start | bytes 884744 | tf_op jit(solution)/shard_map/ppermute | solution.py:674
  247.7 9.9 %collective-permute-start.22 = (bf16[2,2,4,4,48,384]{5,4,3,2,1,0:T(8,128)(2,1)}, bf16[2,2,4,4,48,384]{5,4,3,2,1,0:T(8,128)(2,1)}, u32[]{:S(2)}, u32[]{:S(2)}) collective-permute-start(bf16[2,2,4,4,48,384]{5,4,3,2,1,0:T(8,128)(2,1)} %get-tuple-element.188), channel_id=1, source_target_pairs={{0,2},{2,0},{4,6},{6,4},{8,10},{10,8},{12,14},{14,12},{16,18},{18,... | collective-permute-start | bytes 7077896 | tf_op jit(solution)/shard_map/ppermute | solution.py:674
  260.3 27.8 %collective-permute-start.26 = (bf16[2,4,4,48,384]{4,3,2,1,0:T(8,128)(2,1)}, bf16[2,4,4,48,384]{4,3,2,1,0:T(8,128)(2,1)}, u32[]{:S(2)}, u32[]{:S(2)}) collective-permute-start(bf16[2,4,4,48,384]{4,3,2,1,0:T(8,128)(2,1)} %fusion.3), channel_id=1, source_target_pairs={{0,1},{1,0},{2,3},{3,2},{4,5},{5,4},{6,7},{7,6},{8,9},{9,8},{10,11... | collective-permute-start | bytes 3538952 | tf_op jit(solution)/shard_map/ppermute | solution.py:674
  261.8 12.8 %collective-permute-start.23 = (bf16[4,48,768]{2,1,0:T(8,128)(2,1)}, bf16[4,48,768]{2,1,0:T(8,128)(2,1)}, u32[]{:S(2)}, u32[]{:S(2)}) collective-permute-start(bf16[4,48,768]{2,1,0:T(8,128)(2,1)} %get-tuple-element.191), channel_id=1, source_target_pairs={{0,8},{2,10},{4,12},{6,14},{8,16},{10,18},{12,20},{14,22},{16,24},... | collective-permute-start | bytes 884744 | tf_op jit(solution)/shard_map/ppermute | solution.py:674
  265.2 19.9 %collective-permute-start.24 = (bf16[4,48,768]{2,1,0:T(8,128)(2,1)}, bf16[4,48,768]{2,1,0:T(8,128)(2,1)}, u32[]{:S(2)}, u32[]{:S(2)}) collective-permute-start(bf16[4,48,768]{2,1,0:T(8,128)(2,1)} %get-tuple-element.192), channel_id=1, source_target_pairs={{0,16},{2,18},{4,20},{6,22},{8,24},{10,26},{12,28},{14,30},{16,0},... | collective-permute-start | bytes 884744 | tf_op jit(solution)/shard_map/ppermute | solution.py:674
  266.3 18.8 %collective-permute-start.25 = (bf16[4,48,768]{2,1,0:T(8,128)(2,1)}, bf16[4,48,768]{2,1,0:T(8,128)(2,1)}, u32[]{:S(2)}, u32[]{:S(2)}) collective-permute-start(bf16[4,48,768]{2,1,0:T(8,128)(2,1)} %get-tuple-element.193), channel_id=1, source_target_pairs={{0,24},{2,26},{4,28},{6,30},{8,0},{10,2},{12,4},{14,6},{16,8},{18,... | collective-permute-start | bytes 884744 | tf_op jit(solution)/shard_map/ppermute | solution.py:674
  267.8 17.3 %collective-permute-start.27 = (bf16[4,4,48,384]{3,2,1,0:T(8,128)(2,1)}, bf16[4,4,48,384]{3,2,1,0:T(8,128)(2,1)}, u32[]{:S(2)}, u32[]{:S(2)}) collective-permute-start(bf16[4,4,48,384]{3,2,1,0:T(8,128)(2,1)} %get-tuple-element.203), channel_id=1, source_target_pairs={{0,4},{2,6},{4,0},{6,2},{8,12},{10,14},{12,8},{14,10},{16,20},{18,... | collective-permute-start | bytes 1769480 | tf_op jit(solution)/shard_map/ppermute | solution.py:674
  291.6 9.1 %collective-permute-start.28 = (bf16[3,48,768]{2,1,0:T(8,128)(2,1)}, bf16[3,48,768]{2,1,0:T(8,128)(2,1)S(1)}, u32[]{:S(2)}, u32[]{:S(2)}) collective-permute-start(bf16[3,48,768]{2,1,0:T(8,128)(2,1)} %get-tuple-element.206), channel_id=1, source_target_pairs={{0,1},{1,0},{2,3},{3,2},{4,5},{5,4},{6,7},{7,6},{8,9},{9,8},{10,11... | collective-permute-start | bytes 663560 | tf_op jit(solution)/shard_map/ppermute | solution.py:674
  293.2 19.3 %collective-permute-start.30 = (bf16[4,48,384]{2,1,0:T(8,128)(2,1)}, bf16[4,48,384]{2,1,0:T(8,128)(2,1)}, u32[]{:S(2)}, u32[]{:S(2)}) collective-permute-start(bf16[4,48,384]{2,1,0:T(8,128)(2,1)} %get-tuple-element.208), channel_id=1, source_target_pairs={{0,8},{2,10},{4,12},{6,14},{8,16},{10,18},{12,20},{14,22},{16,24},... | collective-permute-start | bytes 442376 | tf_op jit(solution)/shard_map/ppermute | solution.py:674
  297.0 15.5 %collective-permute-start.31 = (bf16[4,48,384]{2,1,0:T(8,128)(2,1)}, bf16[4,48,384]{2,1,0:T(8,128)(2,1)}, u32[]{:S(2)}, u32[]{:S(2)}) collective-permute-start(bf16[4,48,384]{2,1,0:T(8,128)(2,1)} %get-tuple-element.209), channel_id=1, source_target_pairs={{0,16},{2,18},{4,20},{6,22},{8,24},{10,26},{12,28},{14,30},{16,0},... | collective-permute-start | bytes 442376 | tf_op jit(solution)/shard_map/ppermute | solution.py:674
  299.4 13.1 %collective-permute-start.32 = (bf16[4,48,384]{2,1,0:T(8,128)(2,1)}, bf16[4,48,384]{2,1,0:T(8,128)(2,1)}, u32[]{:S(2)}, u32[]{:S(2)}) collective-permute-start(bf16[4,48,384]{2,1,0:T(8,128)(2,1)} %get-tuple-element.210), channel_id=1, source_target_pairs={{0,24},{2,26},{4,28},{6,30},{8,0},{10,2},{12,4},{14,6},{16,8},{18,... | collective-permute-start | bytes 442376 | tf_op jit(solution)/shard_map/ppermute | solution.py:674
  299.4 14.6 %collective-permute-start.33 = (bf16[4,4,48,384]{3,2,1,0:T(8,128)(2,1)}, bf16[4,4,48,384]{3,2,1,0:T(8,128)(2,1)}, u32[]{:S(2)}, u32[]{:S(2)}) collective-permute-start(bf16[4,4,48,384]{3,2,1,0:T(8,128)(2,1)} %get-tuple-element.212), channel_id=1, source_target_pairs={{0,4},{2,6},{4,0},{6,2},{8,12},{10,14},{12,8},{14,10},{16,20},{18,... | collective-permute-start | bytes 1769480 | tf_op jit(solution)/shard_map/ppermute | solution.py:674
  320.6 6.8 %collective-permute-start.37 = (f32[26,128]{1,0:T(8,128)S(1)}, f32[26,128]{1,0:T(8,128)S(1)}, u32[]{:S(2)}, u32[]{:S(2)}) collective-permute-start(f32[26,128]{1,0:T(8,128)S(1)} %add.106), channel_id=1, source_target_pairs={{0,24},{2,26},{4,28},{6,30},{8,0},{10,2},{12,4},{14,6},{16,8},{18,... | collective-permute-start | bytes 39944 | tf_op jit(solution)/shard_map/ppermute | solution.py:674
  323.3 21.8 %collective-permute-start.41 = (bf16[8,48,768]{2,1,0:T(8,128)(2,1)}, bf16[8,48,768]{2,1,0:T(8,128)(2,1)S(1)}, u32[]{:S(2)}, u32[]{:S(2)}) collective-permute-start(bf16[8,48,768]{2,1,0:T(8,128)(2,1)} %get-tuple-element.215.refs_1_), channel_id=1, source_target_pairs={{0,1},{1,0},{2,3},{3,2},{4,5},{5,4},{6,7},{7,6},{8,9},{9,8},{10,11... | collective-permute-start | bytes 1769480 | tf_op jit(solution)/shard_map/ppermute | solution.py:674
  324.5 8.9 %collective-permute-start.38 = (bf16[4,48,384]{2,1,0:T(8,128)(2,1)}, bf16[4,48,384]{2,1,0:T(8,128)(2,1)S(1)}, u32[]{:S(2)}, u32[]{:S(2)}) collective-permute-start(bf16[4,48,384]{2,1,0:T(8,128)(2,1)} %get-tuple-element.218), channel_id=1, source_target_pairs={{0,8},{2,10},{4,12},{6,14},{8,16},{10,18},{12,20},{14,22},{16,24},... | collective-permute-start | bytes 442376 | tf_op jit(solution)/shard_map/ppermute | solution.py:674
  327.4 10.1 %collective-permute-start.39 = (bf16[4,48,384]{2,1,0:T(8,128)(2,1)}, bf16[4,48,384]{2,1,0:T(8,128)(2,1)S(1)}, u32[]{:S(2)}, u32[]{:S(2)}) collective-permute-start(bf16[4,48,384]{2,1,0:T(8,128)(2,1)} %get-tuple-element.219), channel_id=1, source_target_pairs={{0,16},{2,18},{4,20},{6,22},{8,24},{10,26},{12,28},{14,30},{16,0},... | collective-permute-start | bytes 442376 | tf_op jit(solution)/shard_map/ppermute | solution.py:674
  328.7 8.7 %collective-permute-start.40 = (bf16[4,48,384]{2,1,0:T(8,128)(2,1)}, bf16[4,48,384]{2,1,0:T(8,128)(2,1)S(1)}, u32[]{:S(2)}, u32[]{:S(2)}) collective-permute-start(bf16[4,48,384]{2,1,0:T(8,128)(2,1)} %get-tuple-element.220), channel_id=1, source_target_pairs={{0,24},{2,26},{4,28},{6,30},{8,0},{10,2},{12,4},{14,6},{16,8},{18,... | collective-permute-start | bytes 442376 | tf_op jit(solution)/shard_map/ppermute | solution.py:674
  (61 other events, 303.3 us)
Sparse Core Ops, SparseCore 0:
  10.2 108.1 all-gather.1

commit v5 on v4

--- a/solution.py
+++ b/solution.py
@@ -766,7 +766,7 @@
     if scalars:
         specs[0] = pl.BlockSpec(memory_space=pltpu.SMEM)
     outs = [jax.ShapeDtypeStruct(shape, dtype) for shape, dtype in shapes]
-    room = 20 if kernel in (kept_sums, sum_kernel, out_kernel) else 60
+    room = 20 if kernel in (sum_kernel, out_kernel) else 60
     buffers = [pltpu.VMEM(view_shape(operands[i].shape, views.get(i, ())), operands[i].dtype) for i in moved_in]
     buffers += [pltpu.VMEM(shape, dtype) for shape, dtype in shapes]
     buffers += [pltpu.SemaphoreType.DMA((split.get(i, 1),)) for i in moved_in]

time: 360 us -> 358 us (level)
  local copies, waits for them, and re-layouts: 21.3 us -> 13.6 us
  waiting for transfers between devices: 110 us -> 115 us
    unnamed x112 -> x94, local copies, waits for them, and re-layouts: 11 us -> 3.25 us
    ppermute x43, waiting for transfers between devices: 90.4 us -> 94.9 us  [swap(): return lax.ppermute(values, axis, [(i, mate(i)) for i in range(count)])]
  transfers between devices with their start and end apart: 44 -> 44, of which waited for: 25 -> 26; matrix products, arithmetic and copies ran while one was open for 10% -> 10% of each run, Pallas kernels for 18% -> 19%
where the time goes in v5:
time: 358 us; the launch traced here: 352 us
  Pallas kernels  126 us (35%)
  waiting for transfers between devices  115 us (32%)
  starting transfers between devices  54.1 us (15%)
  other arithmetic  20 us (6%)
  between operations  15.2 us (4%)
  local copies, waits for them, and re-layouts  13.6 us (4%)
  matrix products  8.7 us (2%)
    pallas_call x14, Pallas kernels, call(): pl.pallas_call(body, out_shape=outs, in_specs=specs, out_specs=[pl.BlockS...  126 us
    ppermute x43, waiting for transfers between devices, swap(): return lax.ppermute(values, axis, [(i, mate(i)) for i in range(count)])  94.9 us
    ppermute x43, starting transfers between devices, swap(): return lax.ppermute(values, axis, [(i, mate(i)) for i in range(count)])  54.1 us
    all_gather x1, waiting for transfers between devices, per_device(): lax.all_gather(packed, 'fsdp', axis=0).reshape(devices, -1, unit, width)  19.6 us
    convert_element_type x5, other arithmetic, add_low(): (left.astype(jnp.float32) + right.astype(jnp.float32)).astype(jnp.bfloat16)  8.37 us
  transfers between devices with their start and end apart: 44, of which 26 were waited for; matrix products, arithmetic and copies ran while one was open for 10% of the time, Pallas kernels for 19%

profile of v5, /device:TPU:0, one launch (start us, length us, event | category | flops | bytes accessed | tf_op | source)
XLA Modules:
  0.0 352.3 jit_solution(7639606977197470138)
XLA Ops:
  10.5 5.0 %collective-permute-start = (bf16[16,128]{1,0:T(8,128)(2,1)S(1)}, bf16[16,128]{1,0:T(8,128)(2,1)S(1)}, u32[]{:S(2)}, u32[]{:S(2)}) collective-permute-start(bf16[16,128]{1,0:T(8,128)(2,1)S(1)} %fusion.24), channel_id=1, source_target_pairs={{0,24},{2,26},{4,28},{6,30},{8,0},{10,2},{12,4},{14,6},{16,8},{18,... | collective-permute-start | bytes 12296 | tf_op jit(solution)/shard_map/ppermute | solution.py:674
  16.9 3.2 collective-permute-done.1
  22.7 2.5 collective-permute-done.3
  29.1 3.1 collective-permute-start.5
  32.9 3.6 %collective-permute-done.5 = bf16[96,384]{1,0:T(8,128)(2,1)S(1)} collective-permute-done((bf16[96,384]{1,0:T(8,128)(2,1)S(1)}, bf16[96,384]{1,0:T(8,128)(2,1)S(1)}, u32[]{:S(2)}, u32[]{:S(2)}) %collective-permute-start.5) | collective-permute-done | bytes 73760 | tf_op jit(solution)/shard_map/ppermute | solution.py:674
  36.5 6.0 %collective-permute-done.6 = bf16[96,384]{1,0:T(8,128)(2,1)S(1)} collective-permute-done((bf16[96,384]{1,0:T(8,128)(2,1)S(1)}, bf16[96,384]{1,0:T(8,128)(2,1)S(1)}, u32[]{:S(2)}, u32[]{:S(2)}) %collective-permute-start.6) | collective-permute-done | bytes 73760 | tf_op jit(solution)/shard_map/ppermute | solution.py:674
  44.3 14.1 %collective-permute-done.8 = bf16[4,96,384]{2,1,0:T(8,128)(2,1)S(1)} collective-permute-done((bf16[4,96,384]{2,1,0:T(8,128)(2,1)S(1)}, bf16[4,96,384]{2,1,0:T(8,128)(2,1)S(1)}, u32[]{:S(2)}, u32[]{:S(2)}) %collective-permute-start.8) | collective-permute-done | bytes 294944 | tf_op jit(solution)/shard_map/ppermute | solution.py:674
  67.1 22.2 %collective-permute-done.10 = bf16[16,96,384]{2,1,0:T(8,128)(2,1)} collective-permute-done((bf16[16,96,384]{2,1,0:T(8,128)(2,1)S(1)}, bf16[16,96,384]{2,1,0:T(8,128)(2,1)}, u32[]{:S(2)}, u32[]{:S(2)}) %collective-permute-start.10) | collective-permute-done | bytes 1179680 | tf_op jit(solution)/shard_map/ppermute | solution.py:674
  98.7 19.6 %all-gather.2.cloned.1.call-done = bf16[16,768,768]{2,1,0:T(8,128)(2,1)} async-done(((bf16[1,768,768]{2,1,0:T(8,128)(2,1)}), bf16[16,768,768]{2,1,0:T(8,128)(2,1)}) %all-gather.2.cloned.1.call-update) | async-done | bytes 18874384 | tf_op jit(solution)/shard_map/all_gather | solution.py:863
  118.4 24.5 %shard_map.307 = (bf16[384,768]{1,0:T(8,128)(2,1)}, bf16[384,2304]{1,0:T(8,128)(2,1)}, bf16[6,384,768]{2,1,0:T(8,128)(2,1)}, f32[6,1,768]{2,1,0:T(1,128)}, bf16[...) custom-call(bf16[384,768]{1,0:T(8,128)(2,1)} %refs_9_.5, ...), custom_call_target="tpu_custom_call" | custom-call | flops 62899998720 | bytes 48082944 | tf_op jit(solution)/shard_map/pallas_call | solution.py:796
  142.9 25.0 %shard_map.308 = (bf16[384,768]{1,0:T(8,128)(2,1)}, f32[384,768]{1,0:T(8,128)}, bf16[768,192]{1,0:T(8,128)(2,1)}, f32[192,768]{1,0:T(8,128)}, f32[8,768]{1,0:T(8...) custom-call(s32[4]{0:T(128)} %pad_add_fusion.refs_0_, ...), custom_call_target="tpu_custom_call" | custom-call | flops 61199998976 | bytes 35392528 | tf_op jit(solution)/shard_map/pallas_call | solution.py:796
  168.4 7.0 %shard_map.309 = (bf16[384,768]{1,0:T(8,128)(2,1)}, bf16[384,768]{1,0:T(8,128)(2,1)}, bf16[768,192]{1,0:T(8,128)(2,1)}, f32[192,768]{1,0:T(8,128)}, f32[8,768]{1,0:T(8,128)}) custom-call(s32[4]{0:T(128)} %pad_add_fusion.refs_0_, f32[384,768]{1,0:T(8,128)} %get-tuple-element.126.refs_1_.refs_13_, bf16[16,16,48,768]{3,2,1,0:T(8,128)(2,1)} %bitcast.146, ...), custom_call_target="tpu_custom_call" | custom-call | flops 51000000512 | bytes 26222608 | tf_op jit(solution)/shard_map/pallas_call | solution.py:796
  182.9 21.5 %shard_map.310 = (f32[384,768]{1,0:T(8,128)}, f32[768,768]{1,0:T(8,128)}, f32[1,768]{1,0:T(1,128)}, bf16[2,2,4,4,48,384]{5,4,3,2,1,0:T(8,128)(2,1)}, bf16[2,2,4,4,48,384]{5,4,3,2,1,0:T(8,128)(2,1)}) custom-call(s32[4]{0:T(128)} %pad_add_fusion.refs_0_, bf16[384,768]{1,0:T(8,128)(2,1)} %get-tuple-element.136.refs_1_, bf16[16,16,48,768]{3,2,1,0:T(8,128)(2,1)} %bitcast.147, ...), custom_call_target="tpu_custom_call" | custom-call | flops 40800002048 | bytes 43103248 | tf_op jit(solution)/shard_map/pallas_call | solution.py:796
  204.5 2.7 collective-permute-done.14.refs_21_
  209.1 9.0 %shard_map.311 = (bf16[384,768]{1,0:T(8,128)(2,1)}, bf16[384,768]{1,0:T(8,128)(2,1)}, bf16[768,192]{1,0:T(8,128)(2,1)}, f32[192,768]{1,0:T(8,128)}, f32[8,768]{1...) custom-call(s32[4]{0:T(128)} %pad_add_fusion.refs_0_, ...), custom_call_target="tpu_custom_call" | custom-call | flops 51000000512 | bytes 44556304 | tf_op jit(solution)/shard_map/pallas_call | solution.py:796
  226.6 2.7 collective-permute-start.18
  229.7 16.6 %shard_map.312 = (f32[384,768]{1,0:T(8,128)}, f32[1,768]{1,0:T(1,128)}, bf16[2,2,4,4,48,384]{5,4,3,2,1,0:T(8,128)(2,1)}, bf16[2,2,4,4,48,384]{5,4,3,2,1,0:T(8,128)(2,1)}) custom-call(s32[4]{0:T(128)} %pad_add_fusion.refs_0_, bf16[384,768]{1,0:T(8,128)(2,1)} %get-tuple-element.161.refs_1_, bf16[16,16,48,768]{3,2,1,0:T(8,128)(2,1)} %bitcast.149, ...), custom_call_target="tpu_custom_call" | custom-call | flops 1700000000 | bytes 34255888 | tf_op jit(solution)/shard_map/pallas_call | solution.py:796
  251.6 4.0 %shard_map.313 = (bf16[4,4,48,384]{3,2,1,0:T(8,128)(2,1)}, bf16[4,48,768]{2,1,0:T(8,128)(2,1)}, bf16[4,48,768]{2,1,0:T(8,128)(2,1)}, bf16[4,48,768]{2,1,0:T(8,128)(2,1)}, bf16[4,48,768]{2,1,0:T(8,128)(2,1)}) custom-call(bf16[2,2,4,4,48,384]{5,4,3,2,1,0:T(8,128)(2,1)} %get-tuple-element.197.refs_0_, ...), custom_call_target="tpu_custom_call" | custom-call | flops 170000007168 | bytes 11796480 | tf_op jit(solution)/shard_map/pallas_call | solution.py:796
  255.7 2.6 fusion.3
  259.7 2.9 collective-permute-start.23
  265.7 3.5 shard_map.314
  269.2 2.7 collective-permute-done.23.refs_1_
  271.9 10.3 %collective-permute-done.24.refs_2_ = bf16[4,48,768]{2,1,0:T(8,128)(2,1)} collective-permute-done((bf16[4,48,768]{2,1,0:T(8,128)(2,1)}, bf16[4,48,768]{2,1,0:T(8,128)(2,1)}, u32[]{:S(2)}, u32[]{:S(2)}) %collective-permute-start.24) | collective-permute-done | bytes 294944 | tf_op jit(solution)/shard_map/ppermute | solution.py:674
  282.2 3.2 collective-permute-done.26.refs_7_.refs_2_
  285.4 3.5 shard_map.315
  290.4 3.9 %collective-permute-start.30 = (bf16[4,48,384]{2,1,0:T(8,128)(2,1)}, bf16[4,48,384]{2,1,0:T(8,128)(2,1)}, u32[]{:S(2)}, u32[]{:S(2)}) collective-permute-start(bf16[4,48,384]{2,1,0:T(8,128)(2,1)} %get-tuple-element.208), channel_id=1, source_target_pairs={{0,8},{2,10},{4,12},{6,14},{8,16},{10,18},{12,20},{14,22},{16,24},... | collective-permute-start | bytes 442376 | tf_op jit(solution)/shard_map/ppermute | solution.py:674
  310.7 2.7 shard_map.317
  314.3 2.9 collective-permute-done.34
  321.9 2.9 collective-permute-start.38
  327.1 3.7 %collective-permute-done.38.refs_1_ = bf16[4,48,384]{2,1,0:T(8,128)(2,1)S(1)} collective-permute-done((bf16[4,48,384]{2,1,0:T(8,128)(2,1)}, bf16[4,48,384]{2,1,0:T(8,128)(2,1)S(1)}, u32[]{:S(2)}, u32[]{:S(2)}) %collective-permute-start.38) | collective-permute-done | bytes 147488 | tf_op jit(solution)/shard_map/ppermute | solution.py:674
  330.8 4.0 %collective-permute-done.39.refs_2_ = bf16[4,48,384]{2,1,0:T(8,128)(2,1)S(1)} collective-permute-done((bf16[4,48,384]{2,1,0:T(8,128)(2,1)}, bf16[4,48,384]{2,1,0:T(8,128)(2,1)S(1)}, u32[]{:S(2)}, u32[]{:S(2)}) %collective-permute-start.39) | collective-permute-done | bytes 147488 | tf_op jit(solution)/shard_map/ppermute | solution.py:674
  342.5 2.7 shard_map.319
  (257 shorter events, 93.1 us)
Async XLA Ops:
  7.2 111.2 %all-gather.2.cloned.1.call-start = ((), (), s32[]{:S(2)}) async-start(), calls=%async_computation | async-start | bytes 20054016 | tf_op jit(solution)/shard_map/all_gather | solution.py:863
  29.1 7.3 %collective-permute-start.5 = (bf16[96,384]{1,0:T(8,128)(2,1)S(1)}, bf16[96,384]{1,0:T(8,128)(2,1)S(1)}, u32[]{:S(2)}, u32[]{:S(2)}) collective-permute-start(bf16[96,384]{1,0:T(8,128)(2,1)S(1)} %slice_select_fusion), channel_id=1, source_target_pairs={{0,24},{2,26},{4,28},{6,30},{8,0},{10,2},{12,4},{14,6},{16,8},{18,... | collective-permute-start | bytes 221192 | tf_op jit(solution)/shard_map/ppermute | solution.py:674
  32.3 10.3 %collective-permute-start.7 = (bf16[96,384]{1,0:T(8,128)(2,1)S(1)}, bf16[96,384]{1,0:T(8,128)(2,1)S(1)}, u32[]{:S(2)}, u32[]{:S(2)}) collective-permute-start(bf16[96,384]{1,0:T(8,128)(2,1)S(1)} %slice_select_fusion), channel_id=1, source_target_pairs={{0,8},{2,10},{4,12},{6,14},{8,16},{10,18},{12,20},{14,22},{16,24},... | collective-permute-start | bytes 221192 | tf_op jit(solution)/shard_map/ppermute | solution.py:674
  32.3 10.2 %collective-permute-start.6 = (bf16[96,384]{1,0:T(8,128)(2,1)S(1)}, bf16[96,384]{1,0:T(8,128)(2,1)S(1)}, u32[]{:S(2)}, u32[]{:S(2)}) collective-permute-start(bf16[96,384]{1,0:T(8,128)(2,1)S(1)} %slice_select_fusion), channel_id=1, source_target_pairs={{0,16},{2,18},{4,20},{6,22},{8,24},{10,26},{12,28},{14,30},{16,0},... | collective-permute-start | bytes 221192 | tf_op jit(solution)/shard_map/ppermute | solution.py:674
  42.8 15.7 %collective-permute-start.8 = (bf16[4,96,384]{2,1,0:T(8,128)(2,1)S(1)}, bf16[4,96,384]{2,1,0:T(8,128)(2,1)S(1)}, u32[]{:S(2)}, u32[]{:S(2)}) collective-permute-start(bf16[4,96,384]{2,1,0:T(8,128)(2,1)S(1)} %constant_dynamic-slice_fusion.1), channel_id=1, source_target_pairs={{0,4},{2,6},{4,0},{6,2},{8,12},{10,14},{12,8},{14,10},{16,20},{18,... | collective-permute-start | bytes 884744 | tf_op jit(solution)/shard_map/ppermute | solution.py:674
  61.1 28.2 %collective-permute-start.10 = (bf16[16,96,384]{2,1,0:T(8,128)(2,1)S(1)}, bf16[16,96,384]{2,1,0:T(8,128)(2,1)}, u32[]{:S(2)}, u32[]{:S(2)}) collective-permute-start(bf16[16,96,384]{2,1,0:T(8,128)(2,1)S(1)} %bitcast.150), channel_id=1, source_target_pairs={{0,1},{1,0},{2,3},{3,2},{4,5},{5,4},{6,7},{7,6},{8,9},{9,8},{10,11... | collective-permute-start | bytes 3538952 | tf_op jit(solution)/shard_map/ppermute | solution.py:674
  167.9 7.6 %collective-permute-start.11 = (bf16[2,2,4,4,48,384]{5,4,3,2,1,0:T(8,128)(2,1)}, bf16[2,2,4,4,48,384]{5,4,3,2,1,0:T(8,128)(2,1)S(1)}, u32[]{:S(2)}, u32[]{:S(2)}) collective-permute-start(bf16[2,2,4,4,48,384]{5,4,3,2,1,0:T(8,128)(2,1)} %get-tuple-element.131), channel_id=1, source_target_pairs={{0,2},{2,0},{4,6},{6,4},{8,10},{10,8},{12,14},{14,12},{16,18},{18,... | collective-permute-start | bytes 7077896 | tf_op jit(solution)/shard_map/ppermute | solution.py:674
  168.2 8.0 %collective-permute-start.12 = (bf16[2,4,4,48,768]{4,3,2,1,0:T(8,128)(2,1)}, bf16[2,4,4,48,768]{4,3,2,1,0:T(8,128)(2,1)}, u32[]{:S(2)}, u32[]{:S(2)}) collective-permute-start(bf16[2,4,4,48,768]{4,3,2,1,0:T(8,128)(2,1)} %get-tuple-element.132), channel_id=1, source_target_pairs={{0,2},{2,0},{4,6},{6,4},{8,10},{10,8},{12,14},{14,12},{16,18},{18,... | collective-permute-start | bytes 7077896 | tf_op jit(solution)/shard_map/ppermute | solution.py:674
  179.0 28.3 %collective-permute-start.14 = (bf16[4,4,48,768]{3,2,1,0:T(8,128)(2,1)S(1)}, bf16[4,4,48,768]{3,2,1,0:T(8,128)(2,1)}, u32[]{:S(2)}, u32[]{:S(2)}) collective-permute-start(bf16[4,4,48,768]{3,2,1,0:T(8,128)(2,1)S(1)} %fusion.1), channel_id=1, source_target_pairs={{0,4},{2,6},{4,0},{6,2},{8,12},{10,14},{12,8},{14,10},{16,20},{18,... | collective-permute-start | bytes 3538952 | tf_op jit(solution)/shard_map/ppermute | solution.py:674
  181.1 28.0 %collective-permute-start.13 = (bf16[2,4,4,48,384]{4,3,2,1,0:T(8,128)(2,1)S(1)}, bf16[2,4,4,48,384]{4,3,2,1,0:T(8,128)(2,1)}, u32[]{:S(2)}, u32[]{:S(2)}) collective-permute-start(bf16[2,4,4,48,384]{4,3,2,1,0:T(8,128)(2,1)S(1)} %fusion), channel_id=1, source_target_pairs={{0,1},{1,0},{2,3},{3,2},{4,5},{5,4},{6,7},{7,6},{8,9},{9,8},{10,11... | collective-permute-start | bytes 3538952 | tf_op jit(solution)/shard_map/ppermute | solution.py:674
  204.4 13.8 %collective-permute-start.16 = (bf16[2,2,4,4,48,384]{5,4,3,2,1,0:T(8,128)(2,1)}, bf16[2,2,4,4,48,384]{5,4,3,2,1,0:T(8,128)(2,1)}, u32[]{:S(2)}, u32[]{:S(2)}) collective-permute-start(bf16[2,2,4,4,48,384]{5,4,3,2,1,0:T(8,128)(2,1)} %get-tuple-element.158), channel_id=1, source_target_pairs={{0,2},{2,0},{4,6},{6,4},{8,10},{10,8},{12,14},{14,12},{16,18},{18,... | collective-permute-start | bytes 7077896 | tf_op jit(solution)/shard_map/ppermute | solution.py:674
  222.3 28.1 %collective-permute-start.21 = (bf16[4,4,48,768]{3,2,1,0:T(8,128)(2,1)S(1)}, bf16[4,4,48,768]{3,2,1,0:T(8,128)(2,1)}, u32[]{:S(2)}, u32[]{:S(2)}) collective-permute-start(bf16[4,4,48,768]{3,2,1,0:T(8,128)(2,1)S(1)} %pad_maximum_fusion.1), channel_id=1, source_target_pairs={{0,4},{2,6},{4,0},{6,2},{8,12},{10,14},{12,8},{14,10},{16,20},{18,... | collective-permute-start | bytes 3538952 | tf_op jit(solution)/shard_map/ppermute | solution.py:674
  223.8 27.8 %collective-permute-start.20 = (bf16[2,4,4,48,384]{4,3,2,1,0:T(8,128)(2,1)S(1)}, bf16[2,4,4,48,384]{4,3,2,1,0:T(8,128)(2,1)}, u32[]{:S(2)}, u32[]{:S(2)}) collective-permute-start(bf16[2,4,4,48,384]{4,3,2,1,0:T(8,128)(2,1)S(1)} %fusion.2), channel_id=1, source_target_pairs={{0,1},{1,0},{2,3},{3,2},{4,5},{5,4},{6,7},{7,6},{8,9},{9,8},{10,11... | collective-permute-start | bytes 3538952 | tf_op jit(solution)/shard_map/ppermute | solution.py:674
  225.3 22.3 %collective-permute-start.17 = (bf16[4,48,768]{2,1,0:T(8,128)(2,1)}, bf16[4,48,768]{2,1,0:T(8,128)(2,1)S(1)}, u32[]{:S(2)}, u32[]{:S(2)}) collective-permute-start(bf16[4,48,768]{2,1,0:T(8,128)(2,1)} %get-tuple-element.174), channel_id=1, source_target_pairs={{0,8},{2,10},{4,12},{6,14},{8,16},{10,18},{12,20},{14,22},{16,24},... | collective-permute-start | bytes 884744 | tf_op jit(solution)/shard_map/ppermute | solution.py:674
  226.6 22.0 %collective-permute-start.18 = (bf16[4,48,768]{2,1,0:T(8,128)(2,1)}, bf16[4,48,768]{2,1,0:T(8,128)(2,1)}, u32[]{:S(2)}, u32[]{:S(2)}) collective-permute-start(bf16[4,48,768]{2,1,0:T(8,128)(2,1)} %get-tuple-element.175), channel_id=1, source_target_pairs={{0,16},{2,18},{4,20},{6,22},{8,24},{10,26},{12,28},{14,30},{16,0},... | collective-permute-start | bytes 884744 | tf_op jit(solution)/shard_map/ppermute | solution.py:674
  229.4 19.3 %collective-permute-start.19 = (bf16[4,48,768]{2,1,0:T(8,128)(2,1)S(1)}, bf16[4,48,768]{2,1,0:T(8,128)(2,1)}, u32[]{:S(2)}, u32[]{:S(2)}) collective-permute-start(bf16[4,48,768]{2,1,0:T(8,128)(2,1)S(1)} %copy-done.37), channel_id=1, source_target_pairs={{0,24},{2,26},{4,28},{6,30},{8,0},{10,2},{12,4},{14,6},{16,8},{18,... | collective-permute-start | bytes 884744 | tf_op jit(solution)/shard_map/ppermute | solution.py:674
  247.6 8.1 %collective-permute-start.22 = (bf16[2,2,4,4,48,384]{5,4,3,2,1,0:T(8,128)(2,1)}, bf16[2,2,4,4,48,384]{5,4,3,2,1,0:T(8,128)(2,1)}, u32[]{:S(2)}, u32[]{:S(2)}) collective-permute-start(bf16[2,2,4,4,48,384]{5,4,3,2,1,0:T(8,128)(2,1)} %get-tuple-element.188), channel_id=1, source_target_pairs={{0,2},{2,0},{4,6},{6,4},{8,10},{10,8},{12,14},{14,12},{16,18},{18,... | collective-permute-start | bytes 7077896 | tf_op jit(solution)/shard_map/ppermute | solution.py:674
  258.3 27.2 %collective-permute-start.26 = (bf16[2,4,4,48,384]{4,3,2,1,0:T(8,128)(2,1)}, bf16[2,4,4,48,384]{4,3,2,1,0:T(8,128)(2,1)}, u32[]{:S(2)}, u32[]{:S(2)}) collective-permute-start(bf16[2,4,4,48,384]{4,3,2,1,0:T(8,128)(2,1)} %fusion.3), channel_id=1, source_target_pairs={{0,1},{1,0},{2,3},{3,2},{4,5},{5,4},{6,7},{7,6},{8,9},{9,8},{10,11... | collective-permute-start | bytes 3538952 | tf_op jit(solution)/shard_map/ppermute | solution.py:674
  259.7 12.2 %collective-permute-start.23 = (bf16[4,48,768]{2,1,0:T(8,128)(2,1)}, bf16[4,48,768]{2,1,0:T(8,128)(2,1)}, u32[]{:S(2)}, u32[]{:S(2)}) collective-permute-start(bf16[4,48,768]{2,1,0:T(8,128)(2,1)} %get-tuple-element.191), channel_id=1, source_target_pairs={{0,8},{2,10},{4,12},{6,14},{8,16},{10,18},{12,20},{14,22},{16,24},... | collective-permute-start | bytes 884744 | tf_op jit(solution)/shard_map/ppermute | solution.py:674
  262.6 19.6 %collective-permute-start.24 = (bf16[4,48,768]{2,1,0:T(8,128)(2,1)}, bf16[4,48,768]{2,1,0:T(8,128)(2,1)}, u32[]{:S(2)}, u32[]{:S(2)}) collective-permute-start(bf16[4,48,768]{2,1,0:T(8,128)(2,1)} %get-tuple-element.192), channel_id=1, source_target_pairs={{0,16},{2,18},{4,20},{6,22},{8,24},{10,26},{12,28},{14,30},{16,0},... | collective-permute-start | bytes 884744 | tf_op jit(solution)/shard_map/ppermute | solution.py:674
  263.8 18.4 %collective-permute-start.25 = (bf16[4,48,768]{2,1,0:T(8,128)(2,1)}, bf16[4,48,768]{2,1,0:T(8,128)(2,1)}, u32[]{:S(2)}, u32[]{:S(2)}) collective-permute-start(bf16[4,48,768]{2,1,0:T(8,128)(2,1)} %get-tuple-element.193), channel_id=1, source_target_pairs={{0,24},{2,26},{4,28},{6,30},{8,0},{10,2},{12,4},{14,6},{16,8},{18,... | collective-permute-start | bytes 884744 | tf_op jit(solution)/shard_map/ppermute | solution.py:674
  265.2 17.1 %collective-permute-start.27 = (bf16[4,4,48,384]{3,2,1,0:T(8,128)(2,1)}, bf16[4,4,48,384]{3,2,1,0:T(8,128)(2,1)}, u32[]{:S(2)}, u32[]{:S(2)}) collective-permute-start(bf16[4,4,48,384]{3,2,1,0:T(8,128)(2,1)} %get-tuple-element.203), channel_id=1, source_target_pairs={{0,4},{2,6},{4,0},{6,2},{8,12},{10,14},{12,8},{14,10},{16,20},{18,... | collective-permute-start | bytes 1769480 | tf_op jit(solution)/shard_map/ppermute | solution.py:674
  288.9 8.6 %collective-permute-start.28 = (bf16[3,48,768]{2,1,0:T(8,128)(2,1)}, bf16[3,48,768]{2,1,0:T(8,128)(2,1)S(1)}, u32[]{:S(2)}, u32[]{:S(2)}) collective-permute-start(bf16[3,48,768]{2,1,0:T(8,128)(2,1)} %get-tuple-element.206), channel_id=1, source_target_pairs={{0,1},{1,0},{2,3},{3,2},{4,5},{5,4},{6,7},{7,6},{8,9},{9,8},{10,11... | collective-permute-start | bytes 663560 | tf_op jit(solution)/shard_map/ppermute | solution.py:674
  290.4 18.7 %collective-permute-start.30 = (bf16[4,48,384]{2,1,0:T(8,128)(2,1)}, bf16[4,48,384]{2,1,0:T(8,128)(2,1)}, u32[]{:S(2)}, u32[]{:S(2)}) collective-permute-start(bf16[4,48,384]{2,1,0:T(8,128)(2,1)} %get-tuple-element.208), channel_id=1, source_target_pairs={{0,8},{2,10},{4,12},{6,14},{8,16},{10,18},{12,20},{14,22},{16,24},... | collective-permute-start | bytes 442376 | tf_op jit(solution)/shard_map/ppermute | solution.py:674
  294.4 14.8 %collective-permute-start.31 = (bf16[4,48,384]{2,1,0:T(8,128)(2,1)}, bf16[4,48,384]{2,1,0:T(8,128)(2,1)}, u32[]{:S(2)}, u32[]{:S(2)}) collective-permute-start(bf16[4,48,384]{2,1,0:T(8,128)(2,1)} %get-tuple-element.209), channel_id=1, source_target_pairs={{0,16},{2,18},{4,20},{6,22},{8,24},{10,26},{12,28},{14,30},{16,0},... | collective-permute-start | bytes 442376 | tf_op jit(solution)/shard_map/ppermute | solution.py:674
  296.8 12.4 %collective-permute-start.32 = (bf16[4,48,384]{2,1,0:T(8,128)(2,1)}, bf16[4,48,384]{2,1,0:T(8,128)(2,1)}, u32[]{:S(2)}, u32[]{:S(2)}) collective-permute-start(bf16[4,48,384]{2,1,0:T(8,128)(2,1)} %get-tuple-element.210), channel_id=1, source_target_pairs={{0,24},{2,26},{4,28},{6,30},{8,0},{10,2},{12,4},{14,6},{16,8},{18,... | collective-permute-start | bytes 442376 | tf_op jit(solution)/shard_map/ppermute | solution.py:674
  296.8 13.9 %collective-permute-start.33 = (bf16[4,4,48,384]{3,2,1,0:T(8,128)(2,1)}, bf16[4,4,48,384]{3,2,1,0:T(8,128)(2,1)}, u32[]{:S(2)}, u32[]{:S(2)}) collective-permute-start(bf16[4,4,48,384]{3,2,1,0:T(8,128)(2,1)} %get-tuple-element.212), channel_id=1, source_target_pairs={{0,4},{2,6},{4,0},{6,2},{8,12},{10,14},{12,8},{14,10},{16,20},{18,... | collective-permute-start | bytes 1769480 | tf_op jit(solution)/shard_map/ppermute | solution.py:674
  317.2 7.5 %collective-permute-start.37 = (f32[26,128]{1,0:T(8,128)S(1)}, f32[26,128]{1,0:T(8,128)S(1)}, u32[]{:S(2)}, u32[]{:S(2)}) collective-permute-start(f32[26,128]{1,0:T(8,128)S(1)} %add.106), channel_id=1, source_target_pairs={{0,24},{2,26},{4,28},{6,30},{8,0},{10,2},{12,4},{14,6},{16,8},{18,... | collective-permute-start | bytes 39944 | tf_op jit(solution)/shard_map/ppermute | solution.py:674
  320.7 21.7 %collective-permute-start.41 = (bf16[8,48,768]{2,1,0:T(8,128)(2,1)}, bf16[8,48,768]{2,1,0:T(8,128)(2,1)S(1)}, u32[]{:S(2)}, u32[]{:S(2)}) collective-permute-start(bf16[8,48,768]{2,1,0:T(8,128)(2,1)} %get-tuple-element.215.refs_1_), channel_id=1, source_target_pairs={{0,1},{1,0},{2,3},{3,2},{4,5},{5,4},{6,7},{7,6},{8,9},{9,8},{10,11... | collective-permute-start | bytes 1769480 | tf_op jit(solution)/shard_map/ppermute | solution.py:674
  321.9 8.9 %collective-permute-start.38 = (bf16[4,48,384]{2,1,0:T(8,128)(2,1)}, bf16[4,48,384]{2,1,0:T(8,128)(2,1)S(1)}, u32[]{:S(2)}, u32[]{:S(2)}) collective-permute-start(bf16[4,48,384]{2,1,0:T(8,128)(2,1)} %get-tuple-element.218), channel_id=1, source_target_pairs={{0,8},{2,10},{4,12},{6,14},{8,16},{10,18},{12,20},{14,22},{16,24},... | collective-permute-start | bytes 442376 | tf_op jit(solution)/shard_map/ppermute | solution.py:674
  324.7 10.1 %collective-permute-start.39 = (bf16[4,48,384]{2,1,0:T(8,128)(2,1)}, bf16[4,48,384]{2,1,0:T(8,128)(2,1)S(1)}, u32[]{:S(2)}, u32[]{:S(2)}) collective-permute-start(bf16[4,48,384]{2,1,0:T(8,128)(2,1)} %get-tuple-element.219), channel_id=1, source_target_pairs={{0,16},{2,18},{4,20},{6,22},{8,24},{10,26},{12,28},{14,30},{16,0},... | collective-permute-start | bytes 442376 | tf_op jit(solution)/shard_map/ppermute | solution.py:674
  325.6 9.2 %collective-permute-start.40 = (bf16[4,48,384]{2,1,0:T(8,128)(2,1)}, bf16[4,48,384]{2,1,0:T(8,128)(2,1)S(1)}, u32[]{:S(2)}, u32[]{:S(2)}) collective-permute-start(bf16[4,48,384]{2,1,0:T(8,128)(2,1)} %get-tuple-element.220), channel_id=1, source_target_pairs={{0,24},{2,26},{4,28},{6,30},{8,0},{10,2},{12,4},{14,6},{16,8},{18,... | collective-permute-start | bytes 442376 | tf_op jit(solution)/shard_map/ppermute | solution.py:674
  (52 other events, 312.3 us)
Sparse Core Ops, SparseCore 0:
  10.2 108.1 all-gather.1
